TPU v7x, 32 devices: a whole 2x2x4 slice. The times are simulated.
32 devices in a mesh: section: 2 (over x), patch: 4 (over y, core), shard: 4 (over z).
Axes of the slice: x: 2, y: 2, z: 4, core: 2. Of those that a mesh axis runs over, the one named last changes fastest.
Arguments:
- hidden: bfloat16 [8, 1024, 2432], P('shard', 'patch'), may hold values from -6 to 6
- text_kv: bfloat16 [2, 8, 154, 2432], P('section', 'shard'), may hold values from -6 to 6, as said below
- stale_kv: bfloat16 [2, 8, 1024, 2432], P('section', 'shard', 'patch'), may hold values from -6 to 6, as said below
- modulation: float32 [2, 8, 3, 2432], P('section', 'shard'), may hold values from -3 to 3
- score_gain: float32 [2, 64], P('section'), may hold values from 1.5 to 4
- qkv_weight: bfloat16 [2, 2432, 3648], P('section', 'shard'), may hold values from -0.125 to 0.125
- out_weight: bfloat16 [2, 1216, 2432], P('section', None, 'shard'), may hold values from -0.15625 to 0.15625
- final_mod: float32 [8, 2, 2432], P('shard'), may hold values from -3 to 3
- final_weight: bfloat16 [2432, 64], replicated, may hold values from -0.125 to 0.125
- latent: float32 [8, 1024, 64], P('shard', ('patch', 'section')), may hold values from -6 to 6
- step_index: int32 [8], P('shard'), may hold values from 0 to 27
Outputs:
- new_kv: bfloat16 [2, 8, 1024, 2432], P('section', 'shard', 'patch')
- latent_next: float32 [8, 1024, 64], P('shard', ('patch', 'section'))
- denoised: float32 [8, 1024, 64], P('shard', ('patch', 'section'))
Inputs may be any that keep to these rules, and one draw needn't show every extreme that they name: `text_kv`: in every row the first 1216 columns are 19 heads of 64 key features, each head with mean square one up to bfloat16 rounding. `stale_kv`: in every row the first 1216 columns are 19 heads of 64 key features, each head with mean square one up to bfloat16 rounding.
All inputs are finite; a program needn't handle non-finite values.
Results may differ from a plain program's by a relative error of at most 0.008.
Values may be sent and summed in bfloat16 or wider, within the bound.
A program may use at most 192 MiB of HBM per device.

v0:
```python
import math

import jax
import jax.numpy as jnp
from jax import lax
from jax.sharding import PartitionSpec as P

HEAD = 64
NSTEPS = 28


eps_norm = 1e-06
flow_shift = 3.0


def passed_along(value, axis, steps):
    count = lax.axis_size(axis)
    first, last = (max(0, -steps), min(count, count - steps))
    return lax.ppermute(value, axis, [(source, source + steps) for source in range(first, last)])


def spread(array, axis, root):
    mine = lax.axis_index(axis) == root
    return lax.psum(jnp.where(mine, array, jnp.zeros_like(array)), axis)


def sigma_of(step):
    s = 1.0 - step.astype(jnp.float32) / NSTEPS
    return flow_shift * s / (1.0 + (flow_shift - 1.0) * s)


def modulated(xf, shift, scale):
    mean = jnp.mean(xf, -1, keepdims=True)
    cent = xf - mean
    var = jnp.mean(cent * cent, -1, keepdims=True)
    return cent * lax.rsqrt(var + eps_norm) * (1.0 + scale) + shift


def attend_one(query, keys_all, width, heads):
    count = keys_all.shape[0]
    keys = keys_all[:, :width].reshape(count, heads, HEAD)
    values = keys_all[:, width:].reshape(count, heads, HEAD)
    scores = jnp.einsum("qhe,khe->hqk", query, keys, preferred_element_type=jnp.float32)
    expo = jnp.exp(scores)
    total = jnp.sum(expo, -1)
    weights = expo.astype(jnp.bfloat16)
    mixed = jnp.einsum("hqk,khe->qhe", weights, values, preferred_element_type=jnp.float32)
    mixed = mixed / jnp.transpose(total)[:, :, None]
    return mixed.reshape(query.shape[0], width).astype(jnp.bfloat16)


def run_layer(x, stale_all, text_one, mod_one, gain, w_qkv, w_out, patch_index):
    requests, rows = (x.shape[0], x.shape[1])
    width = w_out.shape[0]
    heads = width // HEAD
    xf = x.astype(jnp.float32)
    normed = modulated(xf, mod_one[:, 0:1, :], mod_one[:, 1:2, :]).astype(jnp.bfloat16)
    proj_in = jnp.einsum("rid,dc->ric", normed, w_qkv, preferred_element_type=jnp.float32)
    q = proj_in[..., :width].reshape(requests, rows, heads, HEAD)
    k = proj_in[..., width : 2 * width].reshape(requests, rows, heads, HEAD)
    v = proj_in[..., 2 * width :]
    q_hat = q * lax.rsqrt(jnp.mean(q * q, -1, keepdims=True) + eps_norm)
    k_hat = k * lax.rsqrt(jnp.mean(k * k, -1, keepdims=True) + eps_norm)
    fresh = jnp.concatenate(
        [k_hat.reshape(requests, rows, width).astype(jnp.bfloat16), v.astype(jnp.bfloat16)], -1
    )
    query = (q_hat * gain / math.sqrt(HEAD)).astype(jnp.bfloat16)
    mixed = lax.dynamic_update_slice_in_dim(stale_all, fresh, patch_index * rows, 1)
    keys_all = jnp.concatenate([text_one, mixed], 1)

    def per_request(pair):
        return attend_one(pair[0], pair[1], width, heads)

    attn = lax.map(per_request, (query, keys_all))
    proj = jnp.einsum("riw,wd->rid", attn, w_out, preferred_element_type=jnp.float32)
    x_next = (xf + mod_one[:, 2:3, :] * proj).astype(jnp.bfloat16)
    return (x_next, fresh)


def on_device(
    hidden,
    text_kv,
    stale_kv,
    modulation,
    score_gain,
    qkv_weight,
    out_weight,
    final_mod,
    final_weight,
    latent,
    step_index,
):
    w_qkv, w_out = (
        lax.all_gather(qkv_weight[0], "shard", axis=0, tiled=True),
        lax.all_gather(out_weight[0], "shard", axis=1, tiled=True),
    )
    stale_all = lax.all_gather(stale_kv[0], "patch", axis=1, tiled=True)
    section = lax.axis_index("section")
    patch_index = lax.axis_index("patch")

    def compute(x):
        return run_layer(
            x, stale_all, text_kv[0], modulation[0], score_gain[0], w_qkv, w_out, patch_index
        )

    def passing(x):
        return (x, jnp.zeros(stale_kv.shape[1:], jnp.bfloat16))

    first, fresh_first = lax.cond(section == 0, compute, passing, hidden)
    arrived = passed_along(first, "section", 1)
    last, fresh_last = lax.cond(section == 1, compute, passing, arrived)
    fresh = jnp.where(section == 0, fresh_first, fresh_last)
    final = modulated(last.astype(jnp.float32), final_mod[:, 0:1, :], final_mod[:, 1:2, :]).astype(
        jnp.bfloat16
    )
    velocity = jnp.einsum("rid,dc->ric", final, final_weight, preferred_element_type=jnp.float32)
    half = latent.shape[1]
    shared = spread(velocity.astype(jnp.bfloat16), "section", 1).astype(velocity.dtype)
    velocity_mine = lax.dynamic_slice_in_dim(shared, section * half, half, 1)
    sig = sigma_of(step_index)[:, None, None]
    sig_next = sigma_of(step_index + 1)[:, None, None]
    latent_next = latent + (sig_next - sig) * velocity_mine
    denoised = latent - sig * velocity_mine
    return (fresh[None], latent_next, denoised)


def solution(mesh):
    in_specs = (
        P("shard", "patch", None),
        P("section", "shard", None, None),
        P("section", "shard", "patch", None),
        P("section", "shard", None, None),
        P("section", None),
        P("section", "shard", None),
        P("section", None, "shard"),
        P("shard", None, None),
        P(),
        P("shard", ("patch", "section"), None),
        P("shard"),
    )
    out_specs = (
        P("section", "shard", "patch", None),
        P("shard", ("patch", "section"), None),
        P("shard", ("patch", "section"), None),
    )
    return jax.shard_map(
        on_device, mesh=mesh, in_specs=in_specs, out_specs=out_specs, check_vma=False
    )
```

profile of v0, /device:TPU:0, one launch (start us, length us, event | category | flops | bytes accessed | tf_op | source)
XLA Modules:
  0.0 953.2 jit_solution(15327422627470284871)
XLA Ops:
  7.2 7.7 copy.37
  15.0 2.5 copy.36
  17.6 0.7 all-gather.7.cloned.1.call-update
  18.4 215.5 %all-gather.11.cloned.1.call-done = bf16[1,1216,2432]{1,0,2:T(2,128)(2,1)} async-done(((bf16[1,1216,608]{1,0,2:T(2,128)(2,1)}), bf16[1,1216,2432]{1,0,2:T(2,128)(2,1)}) %all-gather.11.cloned.1.call-update) | async-done | bytes 5914640 | tf_op jit(solution)/shard_map/all_gather | solution.py:95
  233.9 25.3 %copy.38 = bf16[1,1216,2432]{2,1,0:T(8,128)(2,1)} copy(bf16[1,1216,2432]{1,0,2:T(2,128)(2,1)} %all-gather.11.cloned.1.call-done) | data formatting | bytes 11829248 | tf_op jit(solution)/shard_map/all_gather | solution.py:95
  259.2 43.6 %all-gather.9.cloned.1.call-done = bf16[1,2,1024,2432]{2,3,1,0:T(8,128)(2,1)} async-done(((bf16[1,2,256,2432]{2,3,1,0:T(8,128)(2,1)}), bf16[1,2,1024,2432]{2,3,1,0:T(8,128)(2,1)}) %all-gather.9.cloned.1.call-update) | async-done | bytes 9961488 | tf_op jit(solution)/shard_map/all_gather | solution.py:97
  302.8 310.8 %all-gather.7.cloned.1.call-done = bf16[1,2432,3648]{2,1,0:T(8,128)(2,1)} async-done(((bf16[1,608,3648]{2,1,0:T(8,128)(2,1)}), bf16[1,2432,3648]{2,1,0:T(8,128)(2,1)}) %all-gather.7.cloned.1.call-update) | async-done | bytes 17743888 | tf_op jit(solution)/shard_map/all_gather | solution.py:94
  613.7 129.8 %conditional.2 = (bf16[2,256,2432]{2,1,0:T(8,128)(2,1)S(1)}, bf16[2,256,2432]{2,1,0:T(8,128)(2,1)}) conditional(s32[]{:T(128)} %convert_element_type.88, bf16[2,256,2432]{2,1,0:T(8,128)(2,1)S(1)} %copy-done.2, (bf16[2,256,2432]{2,1,0:T(8,128)(2,1)S(1)}, f32[1,2,3,2432]{3,1,2,0:T(2,128)S(1)}, bf16[2432,3648]{1,0:T(8,128)(2,1)}, f32[1,64]{1,0:T(1,128)S(1)}, ...), branch_computations={%region_0.0_spmd, %region_1.9_spmd} | conditional | flops 13646128128 | bytes 220811024 | solution.py:109
  613.7 0.4 convert_reduce_fusion
  614.1 0.8 fusion.15
  614.9 0.6 slice_bitcast_fusion.1
  615.5 16.5 %fusion.6 = f32[2,256,3648]{1,2,0:T(8,128)} fusion(bf16[2432,3648]{1,0:T(8,128)(2,1)} %get-tuple-element.155, bf16[2,256,2432]{2,1,0:T(8,128)(2,1)S(1)} %get-tuple-element.71, f32[2,2432]{1,0:T(2,128)S(1)} %get-tuple-element.198, f32[2,2432]{1,0:T(2,128)S(1)} %get-tuple-element.199, f32[2,256]{1,0:T(2,128)S(1)} %add_rsqrt_fusion.2, ...), kind=kOutput, calls=%fused_computation.11 | convolution fusion | flops 9092333568 | bytes 27748352 | tf_op jit(solution)/shard_map/cond/branch_1_fun/rid,dc->ric/dot_general | solution.py:58
  632.0 3.3 slice_multiply_fusion
  635.3 2.0 reduce_sum.99
  637.3 4.6 fusion.76
  642.0 2.9 slice.91
  644.8 8.8 copy.66
  653.6 4.3 pad_maximum_fusion.1
  658.0 5.8 copy.40
  663.7 13.1 %pad_maximum_fusion = bf16[2,1178,2432]{1,2,0:T(8,128)(2,1)} fusion(bf16[2,1024,2432]{1,2,0:T(8,128)(2,1)} %get-tuple-element.196, bf16[2,154,2432]{1,2,0:T(8,128)(2,1)} %bitcast.147), kind=kLoop, calls=%fused_computation.13 | loop fusion | flops 22919168 | bytes 22919168 | tf_op jit(solution)/shard_map/cond/branch_1_fun/concatenate | solution.py:69
  677.2 1.6 multiply_convert_fusion
  678.7 52.1 %while.18 = (s32[]{:T(128)}, bf16[2,256,1216]{1,2,0:T(8,128)(2,1)}, bf16[2,1178,2432]{1,2,0:T(8,128)(2,1)}, bf16[2,256,19,64]{1,3,2,0:T(8,128)(2,1)}, s32[]{:T(128)}) while((s32[]{:T(128)}, bf16[2,256,1216]{1,2,0:T(8,128)(2,1)}, bf16[2,1178,2432]{1,2,0:T(8,128)(2,1)}, bf16[2,256,19,64]{1,3,2,0:T(8,128)(2,1)}, s32[]{:T(128)}) %tuple.90), condition=%wide.region_8.8_spmd, body=%wide.region_6.7_spmd.sunk | while | flops 1478904064 | bytes 82245984 | solution.py:74
  678.9 3.2 dynamic-slice_bitcast_fusion.5
  682.1 0.4 fusion.96
  682.5 0.9 copy-done.5
  683.4 9.7 %exponential_reduce_fusion.5 = (f32[19,256]{1,0:T(8,128)S(1)}, f32[19,256,1178]{1,2,0:T(8,128)}) fusion(bf16[1178,19,64]{0,2,1:T(8,128)(2,1)S(1)} %bitcast.134, bf16[2,256,19,64]{1,3,2,0:T(8,128)(2,1)S(1)} %copy-done.5, s32[]{:T(128)} %get-tuple-element.303), kind=kOutput, calls=%fused_computation.clone.1 | convolution fusion | flops 739138304 | bytes 26674180 | tf_op jit(solution)/shard_map/cond/branch_1_fun/while/body/eval_jaxpr/qhe,khe->hqk/dot_general | solution.py:43
  693.1 10.9 %divide_convert_fusion.5 = bf16[256,19,64]{0,2,1:T(8,128)(2,1)S(1)} fusion(bf16[1178,19,64]{0,2,1:T(8,128)(2,1)S(1)} %bitcast.136, f32[19,256,1178]{1,2,0:T(8,128)} %get-tuple-element.281, f32[256,19]{0,1:T(8,128)S(1)} %bitcast.152), kind=kOutput, calls=%fused_computation.5.clone.1 | convolution fusion | flops 739765760 | bytes 26426112 | tf_op jit(solution)/shard_map/cond/branch_1_fun/while/body/eval_jaxpr/hqk,khe->qhe/dot_general | solution.py:47
  704.0 0.9 constant_dynamic-update-slice_fusion.7
  704.9 3.2 dynamic-slice_bitcast_fusion.5
  708.5 0.9 copy-done.5
  709.3 9.7 %exponential_reduce_fusion.5 = (f32[19,256]{1,0:T(8,128)S(1)}, f32[19,256,1178]{1,2,0:T(8,128)}) fusion(bf16[1178,19,64]{0,2,1:T(8,128)(2,1)S(1)} %bitcast.134, bf16[2,256,19,64]{1,3,2,0:T(8,128)(2,1)S(1)} %copy-done.5, s32[]{:T(128)} %get-tuple-element.303), kind=kOutput, calls=%fused_computation.clone.1 | convolution fusion | flops 739138304 | bytes 26674180 | tf_op jit(solution)/shard_map/cond/branch_1_fun/while/body/eval_jaxpr/qhe,khe->hqk/dot_general | solution.py:43
  719.0 10.9 %divide_convert_fusion.5 = bf16[256,19,64]{0,2,1:T(8,128)(2,1)S(1)} fusion(bf16[1178,19,64]{0,2,1:T(8,128)(2,1)S(1)} %bitcast.136, f32[19,256,1178]{1,2,0:T(8,128)} %get-tuple-element.281, f32[256,19]{0,1:T(8,128)S(1)} %bitcast.152), kind=kOutput, calls=%fused_computation.5.clone.1 | convolution fusion | flops 739765760 | bytes 26426112 | tf_op jit(solution)/shard_map/cond/branch_1_fun/while/body/eval_jaxpr/hqk,khe->qhe/dot_general | solution.py:47
  729.9 0.9 constant_dynamic-update-slice_fusion.7
  730.8 7.9 fusion.19
  738.7 4.3 copy.50
  743.4 1.5 copy-done.1
  744.9 1.4 collective-permute-start
  746.4 0.6 divide_subtract_fusion
  747.0 0.6 copy_bitcast_fusion
  747.6 52.4 %collective-permute-done = bf16[2,256,2432]{2,1,0:T(8,128)(2,1)S(1)} collective-permute-done((bf16[2,256,2432]{2,1,0:T(8,128)(2,1)}, bf16[2,256,2432]{2,1,0:T(8,128)(2,1)S(1)}, u32[]{:S(2)}, u32[]{:S(2)}) %collective-permute-start) | collective-permute-done | bytes 2490400 | tf_op jit(solution)/shard_map/ppermute | solution.py:19
  800.1 4.3 conditional.3
  800.1 1.6 broadcast.161.clone
  804.4 0.4 convert_reduce_fusion.2
  804.8 0.8 fusion.60
  805.6 1.8 fusion.69
  807.5 3.4 select_bitcast_fusion
  810.9 134.0 %all-reduce.2.cloned.1.call-done = bf16[2,256,64]{1,2,0:T(8,128)(2,1)} async-done(((bf16[2,256,64]{1,2,0:T(8,128)(2,1)}), bf16[2,256,64]{1,2,0:T(8,128)(2,1)}) %all-reduce.2.cloned.1.call-update) | async-done | bytes 65552 | tf_op jit(solution)/shard_map/psum | solution.py:24
  944.9 1.5 fusion.73
  (48 shorter events, 1.1 us)
Async XLA Ops:
  7.2 798.4 %copy-start = (bf16[2432,64]{0,1:T(8,128)(2,1)S(1)}, bf16[2432,64]{0,1:T(8,128)(2,1)}, u32[]{:S(2)}) copy-start(bf16[2432,64]{0,1:T(8,128)(2,1)} %param.27) | copy-start | bytes 933892
  7.2 226.7 %all-gather.11.cloned.1.call-start = ((), (), s32[]{:S(2)}) async-start(), calls=%async_computation.3 | async-start | bytes 15564800 | tf_op jit(solution)/shard_map/all_gather | solution.py:95
  7.2 7.8 copy-start.7
  15.0 287.8 %all-gather.9.cloned.1.call-start = ((), (), s32[]{:S(2)}) async-start(), calls=%async_computation.2 | async-start | bytes 12451840 | tf_op jit(solution)/shard_map/all_gather | solution.py:97
  17.6 596.0 %all-gather.7.cloned.1.call-start = ((), (), s32[]{:S(2)}) async-start(), calls=%async_computation.1 | async-start | bytes 22568960 | tf_op jit(solution)/shard_map/all_gather | solution.py:94
  18.3 926.6 %all-reduce.2.cloned.1.call-start = ((), (), s32[]{:S(2)}) async-start(), calls=%async_computation | async-start | bytes 131072 | tf_op jit(solution)/shard_map/psum | solution.py:24
  18.4 595.3 %copy-start.8 = (f32[1,2,3,2432]{3,1,2,0:T(2,128)S(1)}, f32[1,2,3,2432]{3,1,2,0:T(2,128)}, u32[]{:S(2)}) copy-start(f32[1,2,3,2432]{3,1,2,0:T(2,128)} %param.22) | copy-start | bytes 175108
  18.4 595.2 %copy-start.15 = (f32[1,64]{1,0:T(1,128)S(1)}, f32[1,64]{1,0:T(1,128)}, u32[]{:S(2)}) copy-start(f32[1,64]{1,0:T(1,128)} %param.23) | copy-start | bytes 772
  233.9 379.8 %copy-start.2 = (bf16[2,256,2432]{2,1,0:T(8,128)(2,1)S(1)}, bf16[2,256,2432]{2,1,0:T(8,128)(2,1)}, u32[]{:S(2)}) copy-start(bf16[2,256,2432]{2,1,0:T(8,128)(2,1)} %param.19) | copy-start | bytes 7471108
  613.6 132.7 %copy-start.18 = (s32[2]{0:T(128)S(1)}, s32[2]{0:T(128)}, u32[]{:S(2)}) copy-start(s32[2]{0:T(128)} %param.29) | copy-start | bytes 28
  613.6 133.3 %copy-start.10 = (f32[2,2,2432]{2,1,0:T(2,128)S(1)}, f32[2,2,2432]{2,1,0:T(2,128)}, u32[]{:S(2)}) copy-start(f32[2,2,2432]{2,1,0:T(2,128)} %param.26) | copy-start | bytes 116740
  663.7 13.1 %copy-start.3 = (f32[2,256,1216]{1,2,0:T(8,128)S(1)}, f32[2,256,1216]{1,2,0:T(8,128)}, u32[]{:S(2)}) copy-start(f32[2,256,1216]{1,2,0:T(8,128)} %get-tuple-element.193) | copy-start | bytes 7471108 | tf_op jit(solution)/shard_map/cond
  678.7 52.1 %copy-start.11 = (f32[2,2432]{1,0:T(2,128)S(1)}, f32[2,2432]{1,0:T(2,128)}, u32[]{:S(2)}) copy-start(f32[2,2432]{1,0:T(2,128)} %get-tuple-element.197) | copy-start | bytes 58372 | tf_op jit(solution)/shard_map/cond
  682.1 1.3 copy-start.5
  708.0 1.3 copy-start.5
  743.4 1.5 copy-start.1
  744.9 55.2 %collective-permute-start = (bf16[2,256,2432]{2,1,0:T(8,128)(2,1)}, bf16[2,256,2432]{2,1,0:T(8,128)(2,1)S(1)}, u32[]{:S(2)}, u32[]{:S(2)}) collective-permute-start(bf16[2,256,2432]{2,1,0:T(8,128)(2,1)} %copy-done.1), channel_id=1, source_target_pairs={{0,16},{1,17},{2,18},{3,19},{4,20},{5,21},{6,22},{7,23},{8,24},{9,... | collective-permute-start | bytes 7471112 | tf_op jit(solution)/shard_map/ppermute | solution.py:19
  804.4 1.2 copy-start.13
  804.4 1.2 copy-start.14
  807.5 137.4 %copy-start.9 = (f32[2,128,64]{1,2,0:T(8,128)S(1)}, f32[2,128,64]{1,2,0:T(8,128)}, u32[]{:S(2)}) copy-start(f32[2,128,64]{1,2,0:T(8,128)} %param.28) | copy-start | bytes 196612
  807.5 137.4 %copy-start.16 = (f32[2]{0:T(128)S(1)}, f32[2]{0:T(128)}, u32[]{:S(2)}) copy-start(f32[2]{0:T(128)} %get-tuple-element.187) | copy-start | bytes 28
  807.5 137.4 %copy-start.17 = (f32[2]{0:T(128)S(1)}, f32[2]{0:T(128)}, u32[]{:S(2)}) copy-start(f32[2]{0:T(128)} %get-tuple-element.188) | copy-start | bytes 28
Sparse Core Ops, SparseCore 0:
  15.1 218.7 all-gather.10
  236.0 66.7 all-gather.8
  304.4 309.2 all-gather.6
  807.6 137.2 all-reduce.1
where the time goes:
time: 964 us; the launch traced here: 953 us
  waiting for transfers between devices  757 us (79%)
  local copies, waits for them, and re-layouts  71.8 us (7%)
  matrix products  67.4 us (7%)
  other arithmetic  37.8 us (4%)
  between operations  14.2 us (1%)
    all_gather x1, waiting for transfers between devices, on_device(): lax.all_gather(qkv_weight[0], 'shard', axis=0, tiled=True)  311 us
    all_gather x1, waiting for transfers between devices, on_device(): lax.all_gather(out_weight[0], 'shard', axis=1, tiled=True)  215 us
    psum x1, waiting for transfers between devices, spread(): return lax.psum(jnp.where(mine, array, jnp.zeros_like(array)), axis)  134 us
    ppermute x1, waiting for transfers between devices, passed_along(): lax.ppermute(value, axis, [(source, source + steps) for source in range(f...  52.4 us
    all_gather x1, waiting for transfers between devices, on_device(): stale_all = lax.all_gather(stale_kv[0], 'patch', axis=1, tiled=True)  43.6 us
    all_gather x1, local copies, waits for them, and re-layouts, on_device(): lax.all_gather(out_weight[0], 'shard', axis=1, tiled=True)  25.3 us
    dot_general x2, matrix products, attend_one(): jnp.einsum('hqk,khe->qhe', weights, values, preferred_element_type=jnp.fl...  21.8 us
    dot_general x2, matrix products, attend_one(): jnp.einsum('qhe,khe->hqk', query, keys, preferred_element_type=jnp.float32)  19.4 us
  transfers between devices with their start and end apart: 5, of which 5 were waited for; matrix products, arithmetic and copies ran while one was open for 3% of the time, Pallas kernels for 0%

commit v1 on v0

v1 whole, which is shorter than its diff:
```python
import functools
import math

import jax
import jax.numpy as jnp
from jax import lax
from jax.experimental import pallas as pl
from jax.experimental.pallas import tpu as pltpu
from jax.sharding import PartitionSpec as P

HEAD = 64
NSTEPS = 28
LANES = 128
BLOCK = 512

eps_norm = 1e-06
flow_shift = 3.0

PARAMS = pltpu.CompilerParams(vmem_limit_bytes=56 * 1024 * 1024)


def sigma_of(step):
    s = 1.0 - step.astype(jnp.float32) / NSTEPS
    return flow_shift * s / (1.0 + (flow_shift - 1.0) * s)


def modulated(xf, shift, scale):
    mean = jnp.mean(xf, -1, keepdims=True)
    cent = xf - mean
    var = jnp.mean(cent * cent, -1, keepdims=True)
    return cent * lax.rsqrt(var + eps_norm) * (1.0 + scale) + shift


def head_means(squares):
    row = lax.broadcasted_iota(jnp.int32, (LANES, LANES), 0) // HEAD
    col = lax.broadcasted_iota(jnp.int32, (LANES, LANES), 1) // HEAD
    same = jnp.where(row == col, 1.0 / HEAD, 0.0).astype(jnp.bfloat16)
    high = squares.astype(jnp.bfloat16)
    low = (squares - high.astype(jnp.float32)).astype(jnp.bfloat16)
    return jnp.dot(high, same, preferred_element_type=jnp.float32) + jnp.dot(
        low, same, preferred_element_type=jnp.float32
    )


def qkv_kernel(n_query, n_key, x_ref, mod_ref, gain_ref, w_ref, out_ref, normed_ref):
    step = pl.program_id(0)

    @pl.when(step == 0)
    def _():
        xf = x_ref[...].astype(jnp.float32)
        normed_ref[...] = modulated(xf, mod_ref[0:1, :], mod_ref[1:2, :]).astype(jnp.bfloat16)

    proj = jnp.dot(normed_ref[...], w_ref[...], preferred_element_type=jnp.float32)
    for low in range(0, BLOCK, LANES):
        part = proj[:, low : low + LANES]
        col = step * BLOCK + low + lax.broadcasted_iota(jnp.int32, (1, LANES), 1)
        factor = lax.rsqrt(head_means(part * part) + eps_norm)
        scaled = part * factor * jnp.where(col < n_query, gain_ref[...], 1.0)
        out_ref[:, low : low + LANES] = jnp.where(col < n_query + n_key, scaled, part).astype(
            jnp.bfloat16
        )


def qkv(x, mod_one, gain, w, n_query, n_key):
    rows, depth = x.shape
    columns = w.shape[1]
    gain_row = jnp.tile(gain / math.sqrt(HEAD), LANES // HEAD)[None]
    return pl.pallas_call(
        functools.partial(qkv_kernel, n_query, n_key),
        grid=(pl.cdiv(columns, BLOCK),),
        in_specs=[
            pl.BlockSpec((rows, depth), lambda i: (0, 0)),
            pl.BlockSpec((3, depth), lambda i: (0, 0)),
            pl.BlockSpec((1, LANES), lambda i: (0, 0)),
            pl.BlockSpec((depth, BLOCK), lambda i: (0, i)),
        ],
        out_specs=pl.BlockSpec((rows, BLOCK), lambda i: (0, i)),
        out_shape=jax.ShapeDtypeStruct((rows, columns), jnp.bfloat16),
        scratch_shapes=[pltpu.VMEM((rows, depth), jnp.bfloat16)],
        compiler_params=PARAMS,
        cost_estimate=pl.CostEstimate(
            flops=2 * rows * depth * columns,
            bytes_accessed=2 * (depth * columns + rows * depth + rows * columns),
            transcendentals=0,
        ),
    )(x, mod_one, gain_row, w)


def attend_kernel(n_sets, *refs):
    q_ref, out_ref = refs[0], refs[-1]
    sets = [refs[1 + 3 * s : 4 + 3 * s] for s in range(n_sets)]
    query = q_ref[...]
    lane = lax.broadcasted_iota(jnp.int32, (1, LANES), 1)
    halves = []
    for head in range(2):
        mine = (lane >= HEAD) == (head == 1)
        q_one = jnp.where(mine, query, jnp.zeros_like(query))
        total = None
        for keys, value_even, value_odd in sets:
            values = (value_even, value_odd)[head]
            scores = lax.dot_general(
                q_one, keys[...], (((1,), (1,)), ((), ())), preferred_element_type=jnp.float32
            )
            weights = jnp.exp(scores).astype(jnp.bfloat16)
            held = jnp.where(mine, jnp.ones((), jnp.bfloat16), values[...])
            part = jnp.dot(weights, held, preferred_element_type=jnp.float32)
            total = part if total is None else total + part
        halves.append(pltpu.roll(total, HEAD, 1) / total)
    out_ref[...] = jnp.where(lane < HEAD, halves[0], halves[1]).astype(jnp.bfloat16)


def attend(qkv_out, n_query, sets, width):
    rows = qkv_out.shape[0]
    pairs = n_query // LANES
    own = n_query // LANES
    last = 2 * width // LANES - 1
    first_value = width // LANES

    def specs(count, offset):
        return [
            pl.BlockSpec((count, LANES), lambda i: (0, offset + i)),
            pl.BlockSpec((count, LANES), lambda i: (0, offset + first_value + i)),
            pl.BlockSpec(
                (count, LANES), lambda i: (0, offset + jnp.minimum(first_value + 1 + i, last))
            ),
        ]

    in_specs = [pl.BlockSpec((rows, LANES), lambda i: (0, i))]
    operands = [qkv_out]
    for array, offset in [(qkv_out, own)] + [(array, 0) for array in sets]:
        in_specs += specs(array.shape[0], offset)
        operands += [array] * 3
    count = rows + sum(array.shape[0] for array in sets)
    return pl.pallas_call(
        functools.partial(attend_kernel, 1 + len(sets)),
        grid=(pairs,),
        in_specs=in_specs,
        out_specs=pl.BlockSpec((rows, LANES), lambda i: (0, i)),
        out_shape=jax.ShapeDtypeStruct((rows, n_query), jnp.bfloat16),
        compiler_params=PARAMS,
        cost_estimate=pl.CostEstimate(
            flops=16 * rows * count * width,
            bytes_accessed=4 * count * width,
            transcendentals=rows * count * width // HEAD,
        ),
    )(*operands)


def out_kernel(width, x_ref, attn_ref, mod_ref, w_ref, *rest):
    attn = attn_ref[:, :width]
    proj = jnp.concatenate(
        [
            jnp.dot(attn, w_ref[shard], preferred_element_type=jnp.float32)
            for shard in range(w_ref.shape[0])
        ],
        -1,
    )
    x_next = (x_ref[...].astype(jnp.float32) + mod_ref[2:3, :] * proj).astype(jnp.bfloat16)
    if len(rest) == 1:
        rest[0][...] = x_next
        return
    fmod_ref, fw_ref, vel_ref = rest
    final = modulated(x_next.astype(jnp.float32), fmod_ref[0:1, :], fmod_ref[1:2, :])
    vel_ref[...] = jnp.dot(
        final.astype(jnp.bfloat16), fw_ref[...], preferred_element_type=jnp.float32
    )


def project_out(x, attn, mod_one, w, final=None):
    rows, depth = x.shape
    width = w.shape[1]
    operands = [x, attn, mod_one, w]
    if final is None:
        shape = jax.ShapeDtypeStruct((rows, depth), jnp.bfloat16)
    else:
        operands += list(final)
        shape = jax.ShapeDtypeStruct((rows, final[1].shape[1]), jnp.float32)
    return pl.pallas_call(
        functools.partial(out_kernel, width),
        in_specs=[pl.BlockSpec(memory_space=pltpu.VMEM)] * len(operands),
        out_specs=pl.BlockSpec(memory_space=pltpu.VMEM),
        out_shape=shape,
        compiler_params=PARAMS,
        cost_estimate=pl.CostEstimate(
            flops=2 * rows * depth * width,
            bytes_accessed=2 * (depth * width + 3 * rows * depth),
            transcendentals=0,
        ),
    )(*operands)


def on_device(
    hidden,
    text_kv,
    stale_kv,
    modulation,
    score_gain,
    qkv_weight,
    out_weight,
    final_mod,
    final_weight,
    latent,
    step_index,
):
    section = lax.axis_index("section")
    patch = lax.axis_index("patch")
    patches = lax.axis_size("patch")
    shards = lax.axis_size("shard")
    requests, rows, depth = hidden.shape
    width = out_weight.shape[1]
    n_query = pl.cdiv(width, LANES) * LANES

    share = qkv_weight.shape[1] // patches
    mine = lax.dynamic_slice_in_dim(qkv_weight[0], patch * share, share, 0)
    mine = jnp.concatenate(
        [mine[:, :width], jnp.zeros((share, n_query - width), mine.dtype), mine[:, width:]], 1
    )
    w_qkv = lax.all_gather(mine, ("shard", "patch"), axis=0, tiled=True)
    stale = [stale_kv[0]]
    step = patches // 2
    while step >= 1:
        pairs = [(p, p ^ step) for p in range(patches)]
        stale = stale + [lax.ppermute(array, "patch", pairs) for array in stale]
        step //= 2
    stale = stale[1:]
    share = width // patches
    mine = lax.dynamic_slice_in_dim(out_weight[0], patch * share, share, 0)
    w_out = lax.all_gather(mine, ("shard", "patch"), axis=0, tiled=True)
    w_out = w_out.reshape(shards, width, out_weight.shape[2])

    def layer(r, x, final=None):
        mod_one = modulation[0, r]
        held = qkv(x, mod_one, score_gain[0], w_qkv, n_query, width)
        sets = [array[r] for array in stale] + [text_kv[0, r]]
        attn = attend(held, n_query, sets, width)
        return project_out(x, attn, mod_one, w_out, final), held[:, n_query:]

    hop = [(s, s + 1) for s in range(lax.axis_size("section") - 1)]
    arrived, fresh_first, fresh_last, velocity = [], [], [], []
    for r in range(requests):
        x_next, fresh = layer(r, hidden[r])
        arrived.append(lax.ppermute(x_next, "section", hop))
        fresh_first.append(fresh)
    for r in range(requests):
        vel, fresh = layer(r, arrived[r], (final_mod[r], final_weight))
        velocity.append(vel)
        fresh_last.append(fresh)
    fresh = jnp.where(section == 0, jnp.stack(fresh_first), jnp.stack(fresh_last))
    velocity = jnp.stack(velocity)
    half = latent.shape[1]
    back = lax.ppermute(velocity[:, :half].astype(jnp.bfloat16), "section", [(1, 0)])
    velocity_mine = jnp.where(section == 0, back.astype(jnp.float32), velocity[:, half:])
    sig = sigma_of(step_index)[:, None, None]
    sig_next = sigma_of(step_index + 1)[:, None, None]
    latent_next = latent + (sig_next - sig) * velocity_mine
    denoised = latent - sig * velocity_mine
    return (fresh[None], latent_next, denoised)


def solution(mesh):
    in_specs = (
        P("shard", "patch", None),
        P("section", "shard", None, None),
        P("section", "shard", "patch", None),
        P("section", "shard", None, None),
        P("section", None),
        P("section", "shard", None),
        P("section", None, "shard"),
        P("shard", None, None),
        P(),
        P("shard", ("patch", "section"), None),
        P("shard"),
    )
    out_specs = (
        P("section", "shard", "patch", None),
        P("shard", ("patch", "section"), None),
        P("shard", ("patch", "section"), None),
    )
    return jax.shard_map(
        on_device, mesh=mesh, in_specs=in_specs, out_specs=out_specs, check_vma=False
    )
```

time: 964 us -> 367 us (0.38); the launches traced: 953 us -> 366 us
  waiting for transfers between devices: 757 us -> 161 us
  Pallas kernels: 0 us -> 153 us
  matrix products: 67.4 us -> 0 us
  local copies, waits for them, and re-layouts: 71.8 us -> 25.6 us
  other arithmetic: 37.8 us -> 2.82 us
    all_gather x3 -> x2, waiting for transfers between devices: 570 us -> 62 us  [the longest x1 34.1 us: on_device(): w_out = lax.all_gather(mine, ('shard', 'patch'), axis=0, tiled=True)]
    pallas_call x0 -> x12, Pallas kernels: none -> 153 us  [the longest x4 65 us: attend(): pl.pallas_call(functools.partial(attend_kernel, 1 + len(sets)), grid=(pai...]
    psum x1 -> x0, waiting for transfers between devices: 134 us -> none  [spread(): return lax.psum(jnp.where(mine, array, jnp.zeros_like(array)), axis)]
    dot_general x7 -> x0, matrix products: 67.4 us -> none  [the longest x2 21.8 us: attend_one(): jnp.einsum('hqk,khe->qhe', weights, values, preferred_element_type=jnp.fl...]
    ppermute x1 -> x6, waiting for transfers between devices: 52.4 us -> 98.5 us  [the longest x3 95.5 us: on_device(): stale = stale + [lax.ppermute(array, 'patch', pairs) for array in stale]]
    all_gather x1 -> x0, local copies, waits for them, and re-layouts: 25.3 us -> none  [on_device(): lax.all_gather(out_weight[0], 'shard', axis=1, tiled=True)]
    concatenate x2 -> x0, other arithmetic: 17.4 us -> none  [the longest x1 13.1 us: run_layer(): keys_all = jnp.concatenate([text_one, mixed], 1)]
    cond x6 -> x0, local copies, waits for them, and re-layouts: 13.1 us -> none
  transfers between devices with their start and end apart: 5 -> 8, of which waited for: 5 -> 4; matrix products, arithmetic and copies ran while one was open for 3% -> 6% of each run, Pallas kernels for 0% -> 27%
where the time goes in v1:
time: 367 us; the launch traced here: 366 us
  waiting for transfers between devices  161 us (44%)
  Pallas kernels  153 us (42%)
  local copies, waits for them, and re-layouts  25.6 us (7%)
  between operations  14.3 us (4%)
  starting transfers between devices  10.4 us (3%)
    ppermute x3, waiting for transfers between devices, on_device(): stale = stale + [lax.ppermute(array, 'patch', pairs) for array in stale]  95.5 us
    pallas_call x4, Pallas kernels, attend(): pl.pallas_call(functools.partial(attend_kernel, 1 + len(sets)), grid=(pai...  65 us
    pallas_call x4, Pallas kernels, qkv(): pl.pallas_call(functools.partial(qkv_kernel, n_query, n_key), grid=(pl.cd...  59.2 us
    all_gather x1, waiting for transfers between devices, on_device(): w_out = lax.all_gather(mine, ('shard', 'patch'), axis=0, tiled=True)  34.1 us
    pallas_call x4, Pallas kernels, project_out(): pl.pallas_call(functools.partial(out_kernel, width), in_specs=[pl.BlockSp...  28.6 us
    all_gather x1, waiting for transfers between devices, on_device(): w_qkv = lax.all_gather(mine, ('shard', 'patch'), axis=0, tiled=True)  27.9 us
    squeeze x4, local copies, waits for them, and re-layouts, layer(): sets = [array[r] for array in stale] + [text_kv[0, r]]  9.57 us
  transfers between devices with their start and end apart: 8, of which 4 were waited for; matrix products, arithmetic and copies ran while one was open for 6% of the time, Pallas kernels for 27%

profile of v1, /device:TPU:0, one launch (start us, length us, event | category | flops | bytes accessed | tf_op | source)
XLA Modules:
  0.0 366.3 jit_solution(16142794467552757117)
XLA Ops:
  7.2 0.0 all-gather.4.cloned.1.call-start
  7.2 1.4 dynamic-slice_bitcast_fusion
  8.7 0.3 slice.100
  9.0 1.9 concatenate.17
  10.9 0.0 all-gather.4.cloned.1.call-update
  10.9 0.0 all-gather.6.cloned.1.call-start
  11.0 0.8 constant_dynamic-slice_fusion
  11.8 3.0 collective-permute-start
  14.9 2.2 fusion.3
  17.2 1.4 copy_bitcast_fusion
  18.5 0.6 copy.33
  19.2 0.6 broadcast_in_dim_tile.2.gain_ref
  19.8 1.1 copy.18.rest_1_
  20.9 0.6 copy.32
  21.5 0.1 copy.20
  21.6 0.6 slice_bitcast_fusion.13
  22.2 95.5 %collective-permute-done = bf16[2,256,2432]{2,1,0:T(8,128)(2,1)} collective-permute-done((bf16[2,256,2432]{2,1,0:T(8,128)(2,1)}, bf16[2,256,2432]{2,1,0:T(8,128)(2,1)}, u32[]{:S(2)}, u32[]{:S(2)}) %collective-permute-start) | collective-permute-done | bytes 2490400 | tf_op jit(solution)/shard_map/ppermute | solution.py:223
  117.8 1.6 slice_bitcast_fusion.11
  119.4 3.3 slice_bitcast_fusion.7
  122.7 3.3 slice_bitcast_fusion.6
  126.0 1.6 slice_bitcast_fusion.5
  127.6 27.9 %all-gather.4.cloned.1.call-done.w_ref = bf16[2432,3712]{1,0:T(8,128)(2,1)} async-done(((bf16[152,3712]{1,0:T(8,128)(2,1)}), bf16[2432,3712]{1,0:T(8,128)(2,1)}) %all-gather.4.cloned.1.call-update) | async-done | bytes 18055184 | tf_op jit(solution)/shard_map/all_gather | solution.py:218
  155.5 14.9 %shard_map.130.refs_0_.refs_1_.refs_2_.refs_3_ = bf16[256,3712]{1,0:T(8,128)(2,1)} custom-call(bf16[256,2432]{1,0:T(8,128)(2,1)} %get-tuple-element.14.x_ref, f32[3,2432]{1,0:T(4,128)} %bitcast.54, f32[1,128]{1,0:T(1,128)} %broadcast_in_dim_tile.2.gain_ref, bf16[2432,3712]{1,0:T(8,128)(2,1)} %all-gather.4.cloned.1.call-done.w_ref), custom_call_target="tpu_custom_call" | custom-call | flops 4622123008 | bytes 21200896 | tf_op jit(solution)/shard_map/pallas_call | solution.py:68
  170.4 16.2 %shard_map.132.attn_ref = bf16[256,1280]{1,0:T(8,128)(2,1)} custom-call(bf16[256,3712]{1,0:T(8,128)(2,1)} %shard_map.130.refs_0_.refs_1_.refs_2_.refs_3_, bf16[256,3712]{1,0:T(8,128)(2,1)} %shard_map.130.refs_0_.refs_1_.refs_2_.refs_3_, bf16[256,3712]{1,0:T(8,128)(2,1)} %shard_map.130.refs_0_.refs_1_.refs_2_.refs_3_, ...), custom_call_target="tpu_custom_call" | custom-call | flops 5867307008 | bytes 5729792 | tf_op jit(solution)/shard_map/pallas_call | solution.py:134
  186.6 34.1 %all-gather.6.cloned.1.call-done = bf16[1,4864,608]{2,1,0:T(8,128)(2,1)} async-done(((bf16[1,304,608]{2,1,0:T(8,128)(2,1)}), bf16[1,4864,608]{2,1,0:T(8,128)(2,1)}) %all-gather.6.cloned.1.call-update) | async-done | bytes 5914640 | tf_op jit(solution)/shard_map/all_gather | solution.py:228
  220.7 6.7 %shard_map.133 = bf16[256,2432]{1,0:T(8,128)(2,1)} custom-call(bf16[256,2432]{1,0:T(8,128)(2,1)} %get-tuple-element.14.x_ref, bf16[256,1280]{1,0:T(8,128)(2,1)} %shard_map.132.attn_ref, f32[3,2432]{1,0:T(4,128)} %bitcast.55, bf16[4,1216,608]{2,1,0:T(8,128)(2,1)} %bitcast.46), custom_call_target="tpu_custom_call" | custom-call | flops 1514143744 | bytes 9650176 | tf_op jit(solution)/shard_map/pallas_call | solution.py:178
  227.4 3.6 collective-permute-start.3
  231.0 14.8 %shard_map.131.refs_0_.refs_1_.refs_2_.refs_3_ = bf16[256,3712]{1,0:T(8,128)(2,1)} custom-call(bf16[256,2432]{1,0:T(8,128)(2,1)} %get-tuple-element.15.x_ref, f32[3,2432]{1,0:T(4,128)} %bitcast.58, f32[1,128]{1,0:T(1,128)} %broadcast_in_dim_tile.2.gain_ref, bf16[2432,3712]{1,0:T(8,128)(2,1)} %all-gather.4.cloned.1.call-done.w_ref), custom_call_target="tpu_custom_call" | custom-call | flops 4622123008 | bytes 21200896 | tf_op jit(solution)/shard_map/pallas_call | solution.py:68
  245.8 16.2 %shard_map.135.attn_ref = bf16[256,1280]{1,0:T(8,128)(2,1)} custom-call(bf16[256,3712]{1,0:T(8,128)(2,1)} %shard_map.131.refs_0_.refs_1_.refs_2_.refs_3_, bf16[256,3712]{1,0:T(8,128)(2,1)} %shard_map.131.refs_0_.refs_1_.refs_2_.refs_3_, bf16[256,3712]{1,0:T(8,128)(2,1)} %shard_map.131.refs_0_.refs_1_.refs_2_.refs_3_, ...), custom_call_target="tpu_custom_call" | custom-call | flops 5867307008 | bytes 5729792 | tf_op jit(solution)/shard_map/pallas_call | solution.py:134
  262.0 6.8 %shard_map.136 = bf16[256,2432]{1,0:T(8,128)(2,1)} custom-call(bf16[256,2432]{1,0:T(8,128)(2,1)} %get-tuple-element.15.x_ref, bf16[256,1280]{1,0:T(8,128)(2,1)} %shard_map.135.attn_ref, f32[3,2432]{1,0:T(4,128)} %bitcast.59, bf16[4,1216,608]{2,1,0:T(8,128)(2,1)} %bitcast.47), custom_call_target="tpu_custom_call" | custom-call | flops 1514143744 | bytes 9650176 | tf_op jit(solution)/shard_map/pallas_call | solution.py:178
  268.8 2.3 collective-permute-start.4
  271.2 1.2 slice_bitcast_fusion.8
  272.4 1.1 copy-done.8
  273.5 14.8 %shard_map.134.refs_0_.refs_1_.refs_2_.refs_3_ = bf16[256,3712]{1,0:T(8,128)(2,1)} custom-call(bf16[256,2432]{1,0:T(8,128)(2,1)} %copy-done.8, f32[3,2432]{1,0:T(4,128)} %bitcast.56, f32[1,128]{1,0:T(1,128)} %broadcast_in_dim_tile.2.gain_ref, bf16[2432,3712]{1,0:T(8,128)(2,1)} %all-gather.4.cloned.1.call-done.w_ref), custom_call_target="tpu_custom_call" | custom-call | flops 4622123008 | bytes 21200896 | tf_op jit(solution)/shard_map/pallas_call | solution.py:68
  288.3 16.3 %shard_map.138.attn_ref = bf16[256,1280]{1,0:T(8,128)(2,1)} custom-call(bf16[256,3712]{1,0:T(8,128)(2,1)} %shard_map.134.refs_0_.refs_1_.refs_2_.refs_3_, bf16[256,3712]{1,0:T(8,128)(2,1)} %shard_map.134.refs_0_.refs_1_.refs_2_.refs_3_, bf16[256,3712]{1,0:T(8,128)(2,1)} %shard_map.134.refs_0_.refs_1_.refs_2_.refs_3_, ...), custom_call_target="tpu_custom_call" | custom-call | flops 5867307008 | bytes 5729792 | tf_op jit(solution)/shard_map/pallas_call | solution.py:134
  304.6 0.1 slice_bitcast_fusion.4
  304.7 14.8 %shard_map.137.refs_0_.refs_1_.refs_2_.refs_3_ = bf16[256,3712]{1,0:T(8,128)(2,1)} custom-call(bf16[256,2432]{1,0:T(8,128)(2,1)} %collective-permute-done.4.x_ref, f32[3,2432]{1,0:T(4,128)} %bitcast.60, f32[1,128]{1,0:T(1,128)} %broadcast_in_dim_tile.2.gain_ref, bf16[2432,3712]{1,0:T(8,128)(2,1)} %all-gather.4.cloned.1.call-done.w_ref), custom_call_target="tpu_custom_call" | custom-call | flops 4622123008 | bytes 21200896 | tf_op jit(solution)/shard_map/pallas_call | solution.py:68
  319.5 16.3 %shard_map.140.attn_ref = bf16[256,1280]{1,0:T(8,128)(2,1)} custom-call(bf16[256,3712]{1,0:T(8,128)(2,1)} %shard_map.137.refs_0_.refs_1_.refs_2_.refs_3_, bf16[256,3712]{1,0:T(8,128)(2,1)} %shard_map.137.refs_0_.refs_1_.refs_2_.refs_3_, bf16[256,3712]{1,0:T(8,128)(2,1)} %shard_map.137.refs_0_.refs_1_.refs_2_.refs_3_, ...), custom_call_target="tpu_custom_call" | custom-call | flops 5867307008 | bytes 5729792 | tf_op jit(solution)/shard_map/pallas_call | solution.py:134
  335.8 0.1 slice_bitcast_fusion
  335.9 7.5 %shard_map.139 = f32[256,64]{1,0:T(8,128)} custom-call(bf16[256,2432]{1,0:T(8,128)(2,1)} %copy-done.8, bf16[256,1280]{1,0:T(8,128)(2,1)} %shard_map.138.attn_ref, f32[3,2432]{1,0:T(4,128)} %bitcast.57, bf16[4,1216,608]{2,1,0:T(8,128)(2,1)} %bitcast.48, f32[2,2432]{1,0:T(2,128)} %get-tuple-element.22.rest_0_, bf16[2432,64]{1,0:T(8,128)(2,1)} %copy.18.rest_1_), custom_call_target="tpu_custom_call" | custom-call | flops 1514143744 | bytes 9650176 | tf_op jit(solution)/shard_map/pallas_call | solution.py:178
  343.4 7.6 %shard_map.141 = f32[256,64]{1,0:T(8,128)} custom-call(bf16[256,2432]{1,0:T(8,128)(2,1)} %collective-permute-done.4.x_ref, bf16[256,1280]{1,0:T(8,128)(2,1)} %shard_map.140.attn_ref, f32[3,2432]{1,0:T(4,128)} %bitcast.61, bf16[4,1216,608]{2,1,0:T(8,128)(2,1)} %bitcast.49, f32[2,2432]{1,0:T(2,128)} %get-tuple-element.23.rest_0_, bf16[2432,64]{1,0:T(8,128)(2,1)} %copy.18.rest_1_), custom_call_target="tpu_custom_call" | custom-call | flops 1514143744 | bytes 9650176 | tf_op jit(solution)/shard_map/pallas_call | solution.py:178
  350.9 0.9 fusion.1
  351.8 1.3 collective-permute-start.5
  353.1 1.9 maximum_select_fusion
  355.0 3.0 collective-permute-done.5
  358.0 0.1 multiply_subtract_fusion
  358.1 0.7 copy.22
  358.8 0.7 copy.23
  (48 shorter events, 0.2 us)
Async XLA Ops:
  7.2 3.8 %copy-start = (bf16[1,1216,608]{2,1,0:T(8,128)(2,1)S(1)}, bf16[1,1216,608]{2,1,0:T(8,128)(2,1)}, u32[]{:S(2)}) copy-start(bf16[1,1216,608]{2,1,0:T(8,128)(2,1)} %param.17) | copy-start | bytes 4435972
  7.2 148.3 %all-gather.4.cloned.1.call-start = ((), (), s32[]{:S(2)}) async-start(), calls=%async_computation | async-start | bytes 19183616 | tf_op jit(solution)/shard_map/all_gather | solution.py:218
  10.9 4.0 %copy-start.14 = (f32[1,2,3,2432]{3,1,2,0:T(2,128)S(1)}, f32[1,2,3,2432]{3,1,2,0:T(2,128)}, u32[]{:S(2)}) copy-start(f32[1,2,3,2432]{3,1,2,0:T(2,128)} %param.14) | copy-start | bytes 175108
  10.9 4.0 %copy-start.6 = (bf16[1,2,154,2432]{3,1,2,0:T(2,128)(2,1)S(1)}, bf16[1,2,154,2432]{3,1,2,0:T(2,128)(2,1)}, u32[]{:S(2)}) copy-start(bf16[1,2,154,2432]{3,1,2,0:T(2,128)(2,1)} %param.12) | copy-start | bytes 4494340
  10.9 209.8 %all-gather.6.cloned.1.call-start = ((), (), s32[]{:S(2)}) async-start(), calls=%async_computation.1 | async-start | bytes 6615040 | tf_op jit(solution)/shard_map/all_gather | solution.py:228
  11.8 105.9 %collective-permute-start = (bf16[2,256,2432]{2,1,0:T(8,128)(2,1)}, bf16[2,256,2432]{2,1,0:T(8,128)(2,1)}, u32[]{:S(2)}, u32[]{:S(2)}) collective-permute-start(bf16[2,256,2432]{2,1,0:T(8,128)(2,1)} %bitcast.62), channel_id=1, source_target_pairs={{0,8},{4,12},{8,0},{12,4},{1,9},{5,13},{9,1},{13,5},{2,10},{6,14},... | collective-permute-start | bytes 7471112 | tf_op jit(solution)/shard_map/ppermute | solution.py:223
  14.9 107.8 %collective-permute-start.1 = (bf16[2,256,2432]{2,1,0:T(8,128)(2,1)}, bf16[2,256,2432]{2,1,0:T(8,128)(2,1)}, u32[]{:S(2)}, u32[]{:S(2)}) collective-permute-start(bf16[2,256,2432]{2,1,0:T(8,128)(2,1)} %bitcast.63), channel_id=1, source_target_pairs={{0,4},{4,0},{8,12},{12,8},{1,5},{5,1},{9,13},{13,9},{2,6},{6,2},{1... | collective-permute-start | bytes 7471112 | tf_op jit(solution)/shard_map/ppermute | solution.py:223
  17.1 1.4 copy-start.16
  17.1 2.7 copy-start.12
  17.1 4.4 %copy-start.13 = (f32[2,128,64]{1,2,0:T(8,128)S(1)}, f32[2,128,64]{1,2,0:T(8,128)}, u32[]{:S(2)}) copy-start(f32[2,128,64]{1,2,0:T(8,128)} %param.20) | copy-start | bytes 196612
  17.1 4.5 %copy-start.15 = (f32[2,2,2432]{2,1,0:T(2,128)S(1)}, f32[2,2,2432]{2,1,0:T(2,128)}, u32[]{:S(2)}) copy-start(f32[2,2,2432]{2,1,0:T(2,128)} %param.18) | copy-start | bytes 116740
  17.1 100.6 %copy-start.17 = (s32[2]{0:T(128)S(1)}, s32[2]{0:T(128)}, u32[]{:S(2)}) copy-start(s32[2]{0:T(128)} %param.21) | copy-start | bytes 28
  17.1 100.6 %copy-start.9 = (bf16[2,256,2432]{2,1,0:T(8,128)(2,1)S(1)}, bf16[2,256,2432]{2,1,0:T(8,128)(2,1)}, u32[]{:S(2)}) copy-start(bf16[2,256,2432]{2,1,0:T(8,128)(2,1)} %param.11) | copy-start | bytes 7471108
  117.7 8.3 %collective-permute-start.2 = (bf16[2,256,2432]{2,1,0:T(8,128)(2,1)}, bf16[2,256,2432]{2,1,0:T(8,128)(2,1)S(1)}, u32[]{:S(2)}, u32[]{:S(2)}) collective-permute-start(bf16[2,256,2432]{2,1,0:T(8,128)(2,1)} %collective-permute-done), channel_id=1, source_target_pairs={{0,4},{4,0},{8,12},{12,8},{1,5},{5,1},{9,13},{13,9},{2,6},{6,2},{1... | collective-permute-start | bytes 7471112 | tf_op jit(solution)/shard_map/ppermute | solution.py:223
  227.4 45.0 %collective-permute-start.3 = (bf16[256,2432]{1,0:T(8,128)(2,1)}, bf16[256,2432]{1,0:T(8,128)(2,1)S(1)}, u32[]{:S(2)}, u32[]{:S(2)}) collective-permute-start(bf16[256,2432]{1,0:T(8,128)(2,1)} %shard_map.133), channel_id=1, source_target_pairs={{0,16},{1,17},{2,18},{3,19},{4,20},{5,21},{6,22},{7,23},{8,24},{9,... | collective-permute-start | bytes 3735560 | tf_op jit(solution)/shard_map/ppermute | solution.py:242
  262.0 9.2 %copy-start.2 = (bf16[256,3712]{1,0:T(8,128)(2,1)S(1)}, bf16[256,3712]{1,0:T(8,128)(2,1)}, u32[]{:S(2)}) copy-start(bf16[256,3712]{1,0:T(8,128)(2,1)} %shard_map.130.refs_0_.refs_1_.refs_2_.refs_3_) | copy-start | bytes 5701636
  262.0 9.2 %copy-start.3 = (bf16[256,3712]{1,0:T(8,128)(2,1)S(1)}, bf16[256,3712]{1,0:T(8,128)(2,1)}, u32[]{:S(2)}) copy-start(bf16[256,3712]{1,0:T(8,128)(2,1)} %shard_map.131.refs_0_.refs_1_.refs_2_.refs_3_) | copy-start | bytes 5701636
  268.8 35.9 %collective-permute-start.4 = (bf16[256,2432]{1,0:T(8,128)(2,1)}, bf16[256,2432]{1,0:T(8,128)(2,1)}, u32[]{:S(2)}, u32[]{:S(2)}) collective-permute-start(bf16[256,2432]{1,0:T(8,128)(2,1)} %shard_map.136), channel_id=1, source_target_pairs={{0,16},{1,17},{2,18},{3,19},{4,20},{5,21},{6,22},{7,23},{8,24},{9,... | collective-permute-start | bytes 3735560 | tf_op jit(solution)/shard_map/ppermute | solution.py:242
  272.4 1.1 copy-start.8
  288.3 16.3 %copy-start.5 = (bf16[256,3712]{1,0:T(8,128)(2,1)S(1)}, bf16[256,3712]{1,0:T(8,128)(2,1)}, u32[]{:S(2)}) copy-start(bf16[256,3712]{1,0:T(8,128)(2,1)} %shard_map.134.refs_0_.refs_1_.refs_2_.refs_3_) | copy-start | bytes 5701636
  319.5 16.3 %copy-start.4 = (bf16[256,3712]{1,0:T(8,128)(2,1)S(1)}, bf16[256,3712]{1,0:T(8,128)(2,1)}, u32[]{:S(2)}) copy-start(bf16[256,3712]{1,0:T(8,128)(2,1)} %shard_map.137.refs_0_.refs_1_.refs_2_.refs_3_) | copy-start | bytes 5701636
  343.4 7.6 %copy-start.10 = (f32[256,64]{1,0:T(8,128)S(1)}, f32[256,64]{1,0:T(8,128)}, u32[]{:S(2)}) copy-start(f32[256,64]{1,0:T(8,128)} %shard_map.139) | copy-start | bytes 196612
  343.4 9.7 %copy-start.7 = (bf16[1,1,256,2432]{3,2,1,0:T(8,128)(2,1)S(1)}, bf16[1,1,256,2432]{3,2,1,0:T(8,128)(2,1)}, u32[]{:S(2)}) copy-start(bf16[1,1,256,2432]{3,2,1,0:T(8,128)(2,1)} %get-tuple-element.27) | copy-start | bytes 3735556
  351.8 6.2 %collective-permute-start.5 = (bf16[2,128,64]{2,1,0:T(8,128)(2,1)S(1)}, bf16[2,128,64]{2,1,0:T(8,128)(2,1)S(1)}, u32[]{:S(2)}, u32[]{:S(2)}) collective-permute-start(bf16[2,128,64]{2,1,0:T(8,128)(2,1)S(1)} %fusion.1), channel_id=1, source_target_pairs={{16,0},{17,1},{18,2},{19,3},{20,4},{21,5},{22,6},{23,7},{24,8},{25... | collective-permute-start | bytes 98312 | tf_op jit(solution)/shard_map/ppermute | solution.py:251
  353.1 4.9 %copy-start.11 = (f32[256,64]{1,0:T(8,128)S(1)}, f32[256,64]{1,0:T(8,128)}, u32[]{:S(2)}) copy-start(f32[256,64]{1,0:T(8,128)} %shard_map.141) | copy-start | bytes 196612
  353.1 6.4 %copy-start.1 = (bf16[1,1216,608]{2,1,0:T(8,128)(2,1)S(1)}, bf16[1,1216,608]{2,1,0:T(8,128)(2,1)}, u32[]{:S(2)}) copy-start(bf16[1,1216,608]{2,1,0:T(8,128)(2,1)} %param.17) | copy-start | bytes 4435972
Sparse Core Ops, SparseCore 0:
  11.0 144.4 all-gather.3
  157.7 62.9 all-gather.5

commit v2 on v1

--- a/solution.py
+++ b/solution.py
@@ -11,7 +11,7 @@
 HEAD = 64
 NSTEPS = 28
 LANES = 128
-BLOCK = 512
+BLOCK = 768
 
 eps_norm = 1e-06
 flow_shift = 3.0
@@ -61,16 +61,22 @@
         )
 
 
-def qkv(x, mod_one, gain, w, n_query, n_key):
-    rows, depth = x.shape
+def picked(array, lead, shape, index):
+    return pl.BlockSpec(
+        (None,) * len(lead) + shape, lambda *grid: tuple(lead) + tuple(index(*grid))
+    )
+
+
+def qkv(x, x_lead, modulation, r, gain, w, n_query, n_key):
+    rows, depth = x.shape[-2:]
     columns = w.shape[1]
     gain_row = jnp.tile(gain / math.sqrt(HEAD), LANES // HEAD)[None]
     return pl.pallas_call(
         functools.partial(qkv_kernel, n_query, n_key),
         grid=(pl.cdiv(columns, BLOCK),),
         in_specs=[
-            pl.BlockSpec((rows, depth), lambda i: (0, 0)),
-            pl.BlockSpec((3, depth), lambda i: (0, 0)),
+            picked(x, x_lead, (rows, depth), lambda i: (0, 0)),
+            picked(modulation, (0, r), (3, depth), lambda i: (0, 0)),
             pl.BlockSpec((1, LANES), lambda i: (0, 0)),
             pl.BlockSpec((depth, BLOCK), lambda i: (0, i)),
         ],
@@ -83,7 +89,7 @@
             bytes_accessed=2 * (depth * columns + rows * depth + rows * columns),
             transcendentals=0,
         ),
-    )(x, mod_one, gain_row, w)
+    )(x, modulation, gain_row, w)
 
 
 def attend_kernel(n_sets, *refs):
@@ -116,21 +122,25 @@
     last = 2 * width // LANES - 1
     first_value = width // LANES
 
-    def specs(count, offset):
+    def specs(array, lead, offset):
+        shape = (array.shape[-2], LANES)
         return [
-            pl.BlockSpec((count, LANES), lambda i: (0, offset + i)),
-            pl.BlockSpec((count, LANES), lambda i: (0, offset + first_value + i)),
-            pl.BlockSpec(
-                (count, LANES), lambda i: (0, offset + jnp.minimum(first_value + 1 + i, last))
+            picked(array, lead, shape, lambda i: (0, offset + i)),
+            picked(array, lead, shape, lambda i: (0, offset + first_value + i)),
+            picked(
+                array,
+                lead,
+                shape,
+                lambda i: (0, offset + jnp.minimum(first_value + 1 + i, last)),
             ),
         ]
 
     in_specs = [pl.BlockSpec((rows, LANES), lambda i: (0, i))]
     operands = [qkv_out]
-    for array, offset in [(qkv_out, own)] + [(array, 0) for array in sets]:
-        in_specs += specs(array.shape[0], offset)
+    for array, lead, offset in [(qkv_out, (), own)] + [pair + (0,) for pair in sets]:
+        in_specs += specs(array, lead, offset)
         operands += [array] * 3
-    count = rows + sum(array.shape[0] for array in sets)
+    count = rows + sum(array.shape[-2] for array, _ in sets)
     return pl.pallas_call(
         functools.partial(attend_kernel, 1 + len(sets)),
         grid=(pairs,),
@@ -166,19 +176,28 @@
     )
 
 
-def project_out(x, attn, mod_one, w, final=None):
-    rows, depth = x.shape
+def project_out(x, x_lead, attn, modulation, r, w, final=None):
+    rows, depth = x.shape[-2:]
     width = w.shape[1]
-    operands = [x, attn, mod_one, w]
+    operands = [x, attn, modulation, w]
+    specs = [
+        picked(x, x_lead, (rows, depth), lambda i: (0, 0)),
+        pl.BlockSpec(attn.shape, lambda i: (0, 0)),
+        picked(modulation, (0, r), (3, depth), lambda i: (0, 0)),
+        pl.BlockSpec(w.shape, lambda i: (0, 0, 0)),
+    ]
     if final is None:
         shape = jax.ShapeDtypeStruct((rows, depth), jnp.bfloat16)
     else:
         operands += list(final)
+        specs.append(picked(final[0], (r,), final[0].shape[1:], lambda i: (0, 0)))
+        specs.append(pl.BlockSpec(final[1].shape, lambda i: (0, 0)))
         shape = jax.ShapeDtypeStruct((rows, final[1].shape[1]), jnp.float32)
     return pl.pallas_call(
         functools.partial(out_kernel, width),
-        in_specs=[pl.BlockSpec(memory_space=pltpu.VMEM)] * len(operands),
-        out_specs=pl.BlockSpec(memory_space=pltpu.VMEM),
+        grid=(1,),
+        in_specs=specs,
+        out_specs=pl.BlockSpec(shape.shape, lambda i: (0, 0)),
         out_shape=shape,
         compiler_params=PARAMS,
         cost_estimate=pl.CostEstimate(
@@ -187,6 +206,266 @@
             transcendentals=0,
         ),
     )(*operands)
+
+
+MESH = pl.DeviceIdType.MESH
+LAG = 3
+
+
+def row_chunks(rows):
+    first = pl.cdiv(rows // 16, 2) * 16
+    return ((0, first), (first, rows - first))
+
+
+def gather_kernel(
+    n, w_ref, wo_ref, stale_ref, w_all, wo_all, stale_all, own, zs, zr, hs, hr, os_, or_, ss, sr
+):
+    me = lax.axis_index("shard")
+    patch = lax.axis_index("patch")
+    rows, columns = w_ref.shape
+    half_rows, half_columns = rows // 2, columns // 2
+    o_rows = wo_ref.shape[0] // 2
+    chunks = row_chunks(half_rows)
+    requests = stale_ref.shape[0]
+    has_left, has_right = me > 0, me < n - 1
+
+    barrier = pltpu.get_barrier_semaphore()
+    for other in (1, 2):
+        pl.semaphore_signal(
+            barrier, inc=1, device_id={"patch": patch ^ other}, device_id_type=MESH
+        )
+
+    @pl.when(has_left)
+    def _():
+        pl.semaphore_signal(barrier, inc=1, device_id={"shard": me - 1}, device_id_type=MESH)
+
+    @pl.when(has_right)
+    def _():
+        pl.semaphore_signal(barrier, inc=1, device_id={"shard": me + 1}, device_id_type=MESH)
+
+    pl.semaphore_wait(
+        barrier, 2 + jnp.where(has_left, 1, 0) + jnp.where(has_right, 1, 0)
+    )
+
+    def spot(ref, base, quarter, k):
+        start, size = chunks[k]
+        return ref.at[
+            pl.ds(pl.multiple_of(base + (quarter // 2) * half_rows + start, 16), size),
+            pl.ds(pl.multiple_of((quarter % 2) * half_columns, LANES), half_columns),
+        ]
+
+    def block(way, t):
+        return me - t if way == 0 else me + t
+
+    def incoming(way, t):
+        return (me - 1 - t >= 0) if way == 0 else (me + 1 + t < n)
+
+    def ahead(way):
+        return has_right if way == 0 else has_left
+
+    def z_copy(way, t, k, sending):
+        b = block(way, t if sending else t + 1)
+        dst = spot(w_all, b * rows, patch, k)
+        src = spot(w_ref, 0, patch, k) if sending and t == 0 else dst
+        return pltpu.make_async_remote_copy(
+            src_ref=src,
+            dst_ref=dst,
+            send_sem=zs.at[way, t, k],
+            recv_sem=zr.at[way, t, k],
+            device_id={"shard": me + 1 if way == 0 else me - 1},
+            device_id_type=MESH,
+        )
+
+    def hop(kind, way, t, k, sending):
+        to = 2 if kind == 0 else 1
+        held = patch ^ 2 if kind == 2 else patch
+        place = spot(w_all, block(way, t + 1) * rows, held if sending else held ^ to, k)
+        return pltpu.make_async_remote_copy(
+            src_ref=place,
+            dst_ref=place,
+            send_sem=hs.at[kind, way, t, k],
+            recv_sem=hr.at[kind, way, t, k],
+            device_id={"patch": patch ^ to},
+            device_id_type=MESH,
+        )
+
+    def o_copy(way, t, sending):
+        b = block(way, t if sending else t + 1)
+        half = pl.ds(pl.multiple_of((patch % 2) * o_rows, 16), o_rows)
+        dst = wo_all.at[b, half]
+        src = wo_ref.at[half] if sending and t == 0 else dst
+        return pltpu.make_async_remote_copy(
+            src_ref=src,
+            dst_ref=dst,
+            send_sem=os_.at[0, way, t],
+            recv_sem=or_.at[0, way, t],
+            device_id={"shard": me + 1 if way == 0 else me - 1},
+            device_id_type=MESH,
+        )
+
+    def o_hop(way, t, sending):
+        parity = patch % 2 if sending else 1 - patch % 2
+        place = wo_all.at[
+            block(way, t + 1), pl.ds(pl.multiple_of(parity * o_rows, 16), o_rows)
+        ]
+        return pltpu.make_async_remote_copy(
+            src_ref=place,
+            dst_ref=place,
+            send_sem=os_.at[1, way, t],
+            recv_sem=or_.at[1, way, t],
+            device_id={"patch": patch ^ 1},
+            device_id_type=MESH,
+        )
+
+    def s_copy(kind, r):
+        return pltpu.make_async_remote_copy(
+            src_ref=stale_all.at[0, r] if kind == 2 else stale_ref.at[r],
+            dst_ref=stale_all.at[kind, r],
+            send_sem=ss.at[kind, r],
+            recv_sem=sr.at[kind, r],
+            device_id={"patch": patch ^ (2 if kind == 0 else 1)},
+            device_id_type=MESH,
+        )
+
+    for way in range(2):
+
+        @pl.when(ahead(way))
+        def _(way=way):
+            for k in range(len(chunks)):
+                z_copy(way, 0, k, True).start()
+
+    s_copy(0, 0).start()
+    for r in range(requests):
+        s_copy(1, r).start()
+    own_w = pltpu.make_async_copy(
+        w_ref, w_all.at[pl.ds(pl.multiple_of(me * rows, 16), rows)], own.at[0]
+    )
+    own_o = pltpu.make_async_copy(wo_ref, wo_all.at[me], own.at[1])
+    own_w.start()
+    own_o.start()
+
+    items = [
+        (way, t, k) for t in range(n - 1) for k in range(len(chunks)) for way in range(2)
+    ]
+
+    def pass_on(way, t, k):
+        @pl.when(incoming(way, t))
+        def _():
+            hop(0, way, t, k, False).wait_recv()
+            hop(2, way, t, k, True).start()
+
+    for place, (way, t, k) in enumerate(items):
+
+        @pl.when(incoming(way, t))
+        def _(way=way, t=t, k=k):
+            z_copy(way, t, k, False).wait_recv()
+            if t + 1 < n - 1:
+
+                @pl.when(ahead(way))
+                def _():
+                    z_copy(way, t + 1, k, True).start()
+
+            hop(0, way, t, k, True).start()
+            hop(1, way, t, k, True).start()
+
+        if place >= 2 * LAG:
+            pass_on(*items[place - 2 * LAG])
+        if t == max(n - 3, 0) and k == len(chunks) - 1:
+
+            @pl.when(ahead(way))
+            def _(way=way):
+                o_copy(way, 0, True).start()
+
+    for r in range(1, requests):
+        s_copy(0, r).start()
+    s_copy(0, 0).wait_recv()
+    s_copy(2, 0).start()
+    for place in range(max(len(items) - 2 * LAG, 0), len(items)):
+        pass_on(*items[place])
+    for t in range(n - 1):
+        for way in range(2):
+
+            @pl.when(incoming(way, t))
+            def _(way=way, t=t):
+                o_copy(way, t, False).wait_recv()
+                if t + 1 < n - 1:
+
+                    @pl.when(ahead(way))
+                    def _():
+                        o_copy(way, t + 1, True).start()
+
+                o_hop(way, t, True).start()
+
+    for r in range(1, requests):
+        s_copy(0, r).wait_recv()
+        s_copy(2, r).start()
+    for way, t, k in items:
+
+        @pl.when(incoming(way, t))
+        def _(way=way, t=t, k=k):
+            for kind in range(3):
+                hop(kind, way, t, k, True).wait_send()
+            for kind in (1, 2):
+                hop(kind, way, t, k, False).wait_recv()
+
+        sends = incoming(way, t - 1) if t > 0 else True
+
+        @pl.when(jnp.logical_and(ahead(way), sends))
+        def _(way=way, t=t, k=k):
+            z_copy(way, t, k, True).wait_send()
+
+        if k == 0:
+
+            @pl.when(incoming(way, t))
+            def _(way=way, t=t):
+                o_hop(way, t, True).wait_send()
+                o_hop(way, t, False).wait_recv()
+
+            @pl.when(jnp.logical_and(ahead(way), sends))
+            def _(way=way, t=t):
+                o_copy(way, t, True).wait_send()
+
+    for r in range(requests):
+        for kind in range(3):
+            s_copy(kind, r).wait_send()
+        for kind in (1, 2):
+            s_copy(kind, r).wait_recv()
+    own_w.wait()
+    own_o.wait()
+
+
+def gather(w, w_out, stale, n):
+    rows, columns = w.shape
+    anywhere = pl.BlockSpec(memory_space=pl.ANY)
+    dma = pltpu.SemaphoreType.DMA
+    requests = stale.shape[0]
+    return pl.pallas_call(
+        functools.partial(gather_kernel, n),
+        in_specs=[anywhere] * 3,
+        out_specs=[anywhere] * 3,
+        out_shape=[
+            jax.ShapeDtypeStruct((n * rows, columns), w.dtype),
+            jax.ShapeDtypeStruct((n,) + w_out.shape, w_out.dtype),
+            jax.ShapeDtypeStruct((3,) + stale.shape, stale.dtype),
+        ],
+        scratch_shapes=[
+            dma((2,)),
+            dma((2, n - 1, 2)),
+            dma((2, n - 1, 2)),
+            dma((3, 2, n - 1, 2)),
+            dma((3, 2, n - 1, 2)),
+            dma((2, 2, n - 1)),
+            dma((2, 2, n - 1)),
+            dma((3, requests)),
+            dma((3, requests)),
+        ],
+        compiler_params=pltpu.CompilerParams(
+            collective_id=0, has_side_effects=True, vmem_limit_bytes=56 * 1024 * 1024
+        ),
+        cost_estimate=pl.CostEstimate(
+            flops=0, bytes_accessed=4 * n * rows * columns, transcendentals=0
+        ),
+    )(w, w_out, stale)
 
 
 def on_device(
@@ -210,39 +489,51 @@
     width = out_weight.shape[1]
     n_query = pl.cdiv(width, LANES) * LANES
 
-    share = qkv_weight.shape[1] // patches
-    mine = lax.dynamic_slice_in_dim(qkv_weight[0], patch * share, share, 0)
-    mine = jnp.concatenate(
-        [mine[:, :width], jnp.zeros((share, n_query - width), mine.dtype), mine[:, width:]], 1
-    )
-    w_qkv = lax.all_gather(mine, ("shard", "patch"), axis=0, tiled=True)
-    stale = [stale_kv[0]]
-    step = patches // 2
-    while step >= 1:
-        pairs = [(p, p ^ step) for p in range(patches)]
-        stale = stale + [lax.ppermute(array, "patch", pairs) for array in stale]
-        step //= 2
-    stale = stale[1:]
-    share = width // patches
-    mine = lax.dynamic_slice_in_dim(out_weight[0], patch * share, share, 0)
-    w_out = lax.all_gather(mine, ("shard", "patch"), axis=0, tiled=True)
-    w_out = w_out.reshape(shards, width, out_weight.shape[2])
-
-    def layer(r, x, final=None):
-        mod_one = modulation[0, r]
-        held = qkv(x, mod_one, score_gain[0], w_qkv, n_query, width)
-        sets = [array[r] for array in stale] + [text_kv[0, r]]
+    columns = pl.cdiv(n_query + 2 * width, 2 * LANES) * 2 * LANES
+    w = qkv_weight[0]
+    packed = jnp.concatenate(
+        [
+            w[:, :width],
+            jnp.zeros((w.shape[0], n_query - width), w.dtype),
+            w[:, width:],
+            jnp.zeros((w.shape[0], columns - n_query - 2 * width), w.dtype),
+        ],
+        1,
+    )
+    if patches == 4 and w.shape[0] % 32 == 0 and width % 32 == 0:
+        w_qkv, w_out, stale = gather(packed, out_weight[0], stale_kv[0], shards)
+        stale = [(stale, (i,)) for i in range(3)]
+    else:
+        share = w.shape[0] // patches
+        mine = lax.dynamic_slice_in_dim(packed, patch * share, share, 0)
+        w_qkv = lax.all_gather(mine, ("shard", "patch"), axis=0, tiled=True)
+        share = width // patches
+        mine = lax.dynamic_slice_in_dim(out_weight[0], patch * share, share, 0)
+        w_out = lax.all_gather(mine, ("shard", "patch"), axis=0, tiled=True)
+        w_out = w_out.reshape(shards, width, out_weight.shape[2])
+        stale = [stale_kv[0]]
+        step = patches // 2
+        while step >= 1:
+            pairs = [(p, p ^ step) for p in range(patches)]
+            stale = stale + [lax.ppermute(array, "patch", pairs) for array in stale]
+            step //= 2
+        stale = [(array, ()) for array in stale[1:]]
+
+    def layer(r, x, x_lead, final=None):
+        held = qkv(x, x_lead, modulation, r, score_gain[0], w_qkv, n_query, width)
+        sets = [(array, lead + (r,)) for array, lead in stale] + [(text_kv, (0, r))]
         attn = attend(held, n_query, sets, width)
-        return project_out(x, attn, mod_one, w_out, final), held[:, n_query:]
+        fresh = held[:, n_query : n_query + 2 * width]
+        return project_out(x, x_lead, attn, modulation, r, w_out, final), fresh
 
     hop = [(s, s + 1) for s in range(lax.axis_size("section") - 1)]
     arrived, fresh_first, fresh_last, velocity = [], [], [], []
     for r in range(requests):
-        x_next, fresh = layer(r, hidden[r])
+        x_next, fresh = layer(r, hidden, (r,))
         arrived.append(lax.ppermute(x_next, "section", hop))
         fresh_first.append(fresh)
     for r in range(requests):
-        vel, fresh = layer(r, arrived[r], (final_mod[r], final_weight))
+        vel, fresh = layer(r, arrived[r], (), (final_mod, final_weight))
         velocity.append(vel)
         fresh_last.append(fresh)
     fresh = jnp.where(section == 0, jnp.stack(fresh_first), jnp.stack(fresh_last))

time: 367 us -> 380 us (1.035)
  Pallas kernels: 153 us -> 341 us
  waiting for transfers between devices: 161 us -> 2.99 us
  between operations: 14.3 us -> 0.83 us
    pallas_call x4 -> x5, Pallas kernels: 28.6 us -> 222 us  [the longest x1 194 us: gather(): pl.pallas_call(functools.partial(gather_kernel, n), in_specs=[anywhere] *...]
    ppermute x3 -> x0, waiting for transfers between devices: 95.5 us -> none  [on_device(): stale = stale + [lax.ppermute(array, 'patch', pairs) for array in stale]]
    all_gather x2 -> x0, waiting for transfers between devices: 62 us -> none  [the longest x1 34.1 us: on_device(): w_out = lax.all_gather(mine, ('shard', 'patch'), axis=0, tiled=True)]
    squeeze x6 -> x0, local copies, waits for them, and re-layouts: 11.8 us -> none  [the longest x4 9.57 us: layer(): sets = [array[r] for array in stale] + [text_kv[0, r]]]
    concatenate x1, local copies, waits for them, and re-layouts: 1.88 us -> 7.14 us  [on_device(): jnp.concatenate([w[:, :width], jnp.zeros((w.shape[0], n_query - width), w...]
    pallas_call x4, Pallas kernels: 59.2 us -> 54 us  [qkv(): pl.pallas_call(functools.partial(qkv_kernel, n_query, n_key), grid=(pl.cd...]
    unnamed x42 -> x26, local copies, waits for them, and re-layouts: 5.09 us -> 8 us
  transfers between devices with their start and end apart: 8 -> 3, of which waited for: 4 -> 1; matrix products, arithmetic and copies ran while one was open for 6% -> 1% of each run, Pallas kernels for 27% -> 18%
where the time goes in v2:
time: 380 us; the launch traced here: 379 us
  Pallas kernels  341 us (90%)
  local copies, waits for them, and re-layouts  23.3 us (6%)
  starting transfers between devices  7.26 us (2%)
    pallas_call x1, Pallas kernels, gather(): pl.pallas_call(functools.partial(gather_kernel, n), in_specs=[anywhere] *...  194 us
    pallas_call x4, Pallas kernels, attend(): pl.pallas_call(functools.partial(attend_kernel, 1 + len(sets)), grid=(pai...  65 us
    pallas_call x4, Pallas kernels, qkv(): pl.pallas_call(functools.partial(qkv_kernel, n_query, n_key), grid=(pl.cd...  54 us
    pallas_call x4, Pallas kernels, project_out(): pl.pallas_call(functools.partial(out_kernel, width), grid=(1,), in_specs=...  28.5 us
    unnamed x26, local copies, waits for them, and re-layouts  8 us
  transfers between devices with their start and end apart: 3, of which 1 were waited for; matrix products, arithmetic and copies ran while one was open for 1% of the time, Pallas kernels for 18%

profile of v2, /device:TPU:0, one launch (start us, length us, event | category | flops | bytes accessed | tf_op | source)
XLA Modules:
  0.0 378.6 jit_solution(10659874167606403459)
XLA Ops:
  0.6 2.6 slice.33
  3.3 3.2 slice.34
  6.5 0.0 copy-done.8
  6.5 0.6 broadcast_in_dim_tile.2.gain_ref
  7.1 0.0 copy-done.7
  7.1 0.7 copy.14.mod_ref
  7.8 2.7 copy.16.refs_13_.refs_14_.refs_15_
  10.5 7.1 %concatenate.17.w_ref = bf16[608,3840]{1,0:T(8,128)(2,1)} concatenate(bf16[608,1216]{1,0:T(8,128)(2,1)} %slice.33, bf16[608,64]{1,0:T(8,128)(2,1)S(1)} %broadcast_in_dim.4, bf16[608,2432]{1,0:T(8,128)(2,1)S(1)} %slice.34, bf16[608,128]{1,0:T(8,128)(2,1)S(1)} %broadcast_in_dim.10), dimensions={1} | concatenate | bytes 9338880 | tf_op jit(solution)/shard_map/concatenate | solution.py:494
  17.6 193.9 %shard_map.130 = (bf16[2432,3840]{1,0:T(8,128)(2,1)}, bf16[4,1216,608]{2,1,0:T(8,128)(2,1)}, bf16[3,2,256,2432]{3,2,1,0:T(8,128)(2,1)}) custom-call(bf16[608,3840]{1,0:T(8,128)(2,1)} %concatenate.17.w_ref, bf16[1216,608]{1,0:T(8,128)(2,1)} %bitcast.18, bf16[2,256,2432]{2,1,0:T(8,128)(2,1)} %bitcast.17), custom_call_target="tpu_custom_call" | custom-call | bytes 37355520 | tf_op jit(solution)/shard_map/pallas_call | solution.py:442
  211.6 13.5 %shard_map.132.refs_0_.refs_1_.refs_2_.refs_3_ = bf16[256,3840]{1,0:T(8,128)(2,1)} custom-call(bf16[2,256,2432]{2,1,0:T(8,128)(2,1)} %x_ref.7, f32[1,2,3,2432]{3,2,1,0:T(4,128)} %copy.14.mod_ref, f32[1,128]{1,0:T(1,128)} %broadcast_in_dim_tile.2.gain_ref, bf16[2432,3840]{1,0:T(8,128)(2,1)} %get-tuple-element.6.w_ref), custom_call_target="tpu_custom_call" | custom-call | flops 4781506560 | bytes 21889024 | tf_op jit(solution)/shard_map/pallas_call | solution.py:74
  225.1 16.2 %shard_map.136.attn_ref = bf16[256,1280]{1,0:T(8,128)(2,1)} custom-call(bf16[256,3840]{1,0:T(8,128)(2,1)} %shard_map.132.refs_0_.refs_1_.refs_2_.refs_3_, bf16[256,3840]{1,0:T(8,128)(2,1)} %shard_map.132.refs_0_.refs_1_.refs_2_.refs_3_, bf16[256,3840]{1,0:T(8,128)(2,1)} %shard_map.132.refs_0_.refs_1_.refs_2_.refs_3_, ...), custom_call_target="tpu_custom_call" | custom-call | flops 5867307008 | bytes 5729792 | tf_op jit(solution)/shard_map/pallas_call | solution.py:144
  241.3 6.7 %shard_map.137 = bf16[256,2432]{1,0:T(8,128)(2,1)} custom-call(bf16[2,256,2432]{2,1,0:T(8,128)(2,1)} %x_ref.7, bf16[256,1280]{1,0:T(8,128)(2,1)} %shard_map.136.attn_ref, f32[1,2,3,2432]{3,2,1,0:T(4,128)} %copy.14.mod_ref, bf16[4,1216,608]{2,1,0:T(8,128)(2,1)} %get-tuple-element.8.w_ref), custom_call_target="tpu_custom_call" | custom-call | flops 1514143744 | bytes 9650176 | tf_op jit(solution)/shard_map/pallas_call | solution.py:196
  248.0 3.6 collective-permute-start.1
  251.6 13.5 %shard_map.131.refs_0_.refs_1_.refs_2_.refs_3_ = bf16[256,3840]{1,0:T(8,128)(2,1)} custom-call(bf16[2,256,2432]{2,1,0:T(8,128)(2,1)} %x_ref.7, f32[1,2,3,2432]{3,2,1,0:T(4,128)} %copy.14.mod_ref, f32[1,128]{1,0:T(1,128)} %broadcast_in_dim_tile.2.gain_ref, bf16[2432,3840]{1,0:T(8,128)(2,1)} %get-tuple-element.6.w_ref), custom_call_target="tpu_custom_call" | custom-call | flops 4781506560 | bytes 21889024 | tf_op jit(solution)/shard_map/pallas_call | solution.py:74
  265.1 16.2 %shard_map.133.attn_ref = bf16[256,1280]{1,0:T(8,128)(2,1)} custom-call(bf16[256,3840]{1,0:T(8,128)(2,1)} %shard_map.131.refs_0_.refs_1_.refs_2_.refs_3_, bf16[256,3840]{1,0:T(8,128)(2,1)} %shard_map.131.refs_0_.refs_1_.refs_2_.refs_3_, bf16[256,3840]{1,0:T(8,128)(2,1)} %shard_map.131.refs_0_.refs_1_.refs_2_.refs_3_, ...), custom_call_target="tpu_custom_call" | custom-call | flops 5867307008 | bytes 5729792 | tf_op jit(solution)/shard_map/pallas_call | solution.py:144
  281.3 0.0 copy-start.6
  281.3 0.0 copy-start.9
  281.4 0.0 copy-start.2
  281.4 6.8 %shard_map.134 = bf16[256,2432]{1,0:T(8,128)(2,1)} custom-call(bf16[2,256,2432]{2,1,0:T(8,128)(2,1)} %x_ref.7, bf16[256,1280]{1,0:T(8,128)(2,1)} %shard_map.133.attn_ref, f32[1,2,3,2432]{3,2,1,0:T(4,128)} %copy.14.mod_ref, bf16[4,1216,608]{2,1,0:T(8,128)(2,1)} %get-tuple-element.8.w_ref), custom_call_target="tpu_custom_call" | custom-call | flops 1514143744 | bytes 9650176 | tf_op jit(solution)/shard_map/pallas_call | solution.py:196
  288.2 2.3 collective-permute-start
  290.5 0.0 copy-done.6
  290.5 0.1 copy.36
  290.6 2.1 copy.30.rest_1_
  292.7 0.0 copy-done.9
  292.7 0.0 copy-done.2
  292.7 1.5 slice_bitcast_fusion.2
  294.2 0.0 collective-permute-done.1.x_ref
  294.2 0.0 copy-start.3
  294.2 1.0 copy-done.3
  295.2 13.5 %shard_map.138.refs_0_.refs_1_.refs_2_.refs_3_ = bf16[256,3840]{1,0:T(8,128)(2,1)} custom-call(bf16[256,2432]{1,0:T(8,128)(2,1)} %copy-done.3, f32[1,2,3,2432]{3,2,1,0:T(4,128)} %copy.14.mod_ref, f32[1,128]{1,0:T(1,128)} %broadcast_in_dim_tile.2.gain_ref, bf16[2432,3840]{1,0:T(8,128)(2,1)} %get-tuple-element.6.w_ref), custom_call_target="tpu_custom_call" | custom-call | flops 4781506560 | bytes 21889024 | tf_op jit(solution)/shard_map/pallas_call | solution.py:74
  308.8 16.3 %shard_map.141.attn_ref = bf16[256,1280]{1,0:T(8,128)(2,1)} custom-call(bf16[256,3840]{1,0:T(8,128)(2,1)} %shard_map.138.refs_0_.refs_1_.refs_2_.refs_3_, bf16[256,3840]{1,0:T(8,128)(2,1)} %shard_map.138.refs_0_.refs_1_.refs_2_.refs_3_, bf16[256,3840]{1,0:T(8,128)(2,1)} %shard_map.138.refs_0_.refs_1_.refs_2_.refs_3_, ...), custom_call_target="tpu_custom_call" | custom-call | flops 5867307008 | bytes 5729792 | tf_op jit(solution)/shard_map/pallas_call | solution.py:144
  325.1 0.1 slice_bitcast_fusion
  325.1 0.0 collective-permute-done.x_ref
  325.2 13.5 %shard_map.135.refs_0_.refs_1_.refs_2_.refs_3_ = bf16[256,3840]{1,0:T(8,128)(2,1)} custom-call(bf16[256,2432]{1,0:T(8,128)(2,1)} %collective-permute-done.x_ref, f32[1,2,3,2432]{3,2,1,0:T(4,128)} %copy.14.mod_ref, f32[1,128]{1,0:T(1,128)} %broadcast_in_dim_tile.2.gain_ref, bf16[2432,3840]{1,0:T(8,128)(2,1)} %get-tuple-element.6.w_ref), custom_call_target="tpu_custom_call" | custom-call | flops 4781506560 | bytes 21889024 | tf_op jit(solution)/shard_map/pallas_call | solution.py:74
  338.7 16.3 %shard_map.139.attn_ref = bf16[256,1280]{1,0:T(8,128)(2,1)} custom-call(bf16[256,3840]{1,0:T(8,128)(2,1)} %shard_map.135.refs_0_.refs_1_.refs_2_.refs_3_, bf16[256,3840]{1,0:T(8,128)(2,1)} %shard_map.135.refs_0_.refs_1_.refs_2_.refs_3_, bf16[256,3840]{1,0:T(8,128)(2,1)} %shard_map.135.refs_0_.refs_1_.refs_2_.refs_3_, ...), custom_call_target="tpu_custom_call" | custom-call | flops 5867307008 | bytes 5729792 | tf_op jit(solution)/shard_map/pallas_call | solution.py:144
  354.9 0.0 copy-done
  355.0 0.1 slice_bitcast_fusion.1
  355.0 7.5 %shard_map.142 = f32[256,64]{1,0:T(8,128)} custom-call(bf16[256,2432]{1,0:T(8,128)(2,1)} %copy-done.3, bf16[256,1280]{1,0:T(8,128)(2,1)} %shard_map.141.attn_ref, f32[1,2,3,2432]{3,2,1,0:T(4,128)} %copy.14.mod_ref, bf16[4,1216,608]{2,1,0:T(8,128)(2,1)} %get-tuple-element.8.w_ref, f32[2,2,2432]{2,1,0:T(2,128)} %rest_0_.3, bf16[2432,64]{1,0:T(8,128)(2,1)} %copy.30.rest_1_), custom_call_target="tpu_custom_call" | custom-call | flops 1514143744 | bytes 9650176 | tf_op jit(solution)/shard_map/pallas_call | solution.py:196
  362.5 7.5 %shard_map.140 = f32[256,64]{1,0:T(8,128)} custom-call(bf16[256,2432]{1,0:T(8,128)(2,1)} %collective-permute-done.x_ref, bf16[256,1280]{1,0:T(8,128)(2,1)} %shard_map.139.attn_ref, f32[1,2,3,2432]{3,2,1,0:T(4,128)} %copy.14.mod_ref, bf16[4,1216,608]{2,1,0:T(8,128)(2,1)} %get-tuple-element.8.w_ref, f32[2,2,2432]{2,1,0:T(2,128)} %rest_0_.3, ...), custom_call_target="tpu_custom_call" | custom-call | flops 1514143744 | bytes 9650176 | tf_op jit(solution)/shard_map/pallas_call | solution.py:196
  370.0 0.9 fusion.1
  370.9 1.3 collective-permute-start.2
  372.2 0.0 copy-start.5
  372.2 1.9 maximum_select_fusion
  374.1 3.0 collective-permute-done.2
  377.1 0.0 copy-done.5
  377.1 0.1 multiply_subtract_fusion
  377.2 0.7 copy.39
  377.9 0.7 copy.38
  (12 shorter events, 0.1 us)
Async XLA Ops:
  3.3 3.2 copy-start.8
  3.3 3.8 %copy-start.7 = (f32[1,2,3,2432]{3,1,2,0:T(2,128)S(1)}, f32[1,2,3,2432]{3,1,2,0:T(2,128)}, u32[]{:S(2)}) copy-start(f32[1,2,3,2432]{3,1,2,0:T(2,128)} %param.14) | copy-start | bytes 175108
  248.0 46.2 %collective-permute-start.1 = (bf16[256,2432]{1,0:T(8,128)(2,1)}, bf16[256,2432]{1,0:T(8,128)(2,1)S(1)}, u32[]{:S(2)}, u32[]{:S(2)}) collective-permute-start(bf16[256,2432]{1,0:T(8,128)(2,1)} %shard_map.137), channel_id=1, source_target_pairs={{0,16},{1,17},{2,18},{3,19},{4,20},{5,21},{6,22},{7,23},{8,24},{9,... | collective-permute-start | bytes 3735560 | tf_op jit(solution)/shard_map/ppermute | solution.py:533
  281.3 9.2 %copy-start.6 = (f32[2,128,64]{1,2,0:T(8,128)S(1)}, f32[2,128,64]{1,2,0:T(8,128)}, u32[]{:S(2)}) copy-start(f32[2,128,64]{1,2,0:T(8,128)} %param.20) | copy-start | bytes 196612
  281.3 11.4 %copy-start.9 = (s32[2]{0:T(128)S(1)}, s32[2]{0:T(128)}, u32[]{:S(2)}) copy-start(s32[2]{0:T(128)} %param.21) | copy-start | bytes 28
  281.4 11.4 %copy-start.2 = (bf16[256,3840]{1,0:T(8,128)(2,1)S(1)}, bf16[256,3840]{1,0:T(8,128)(2,1)}, u32[]{:S(2)}) copy-start(bf16[256,3840]{1,0:T(8,128)(2,1)} %shard_map.132.refs_0_.refs_1_.refs_2_.refs_3_) | copy-start | bytes 5898244
  288.2 37.0 %collective-permute-start = (bf16[256,2432]{1,0:T(8,128)(2,1)}, bf16[256,2432]{1,0:T(8,128)(2,1)}, u32[]{:S(2)}, u32[]{:S(2)}) collective-permute-start(bf16[256,2432]{1,0:T(8,128)(2,1)} %shard_map.134), channel_id=1, source_target_pairs={{0,16},{1,17},{2,18},{3,19},{4,20},{5,21},{6,22},{7,23},{8,24},{9,... | collective-permute-start | bytes 3735560 | tf_op jit(solution)/shard_map/ppermute | solution.py:533
  294.2 1.0 copy-start.3
  308.8 16.3 %copy-start.1 = (bf16[256,3840]{1,0:T(8,128)(2,1)S(1)}, bf16[256,3840]{1,0:T(8,128)(2,1)}, u32[]{:S(2)}) copy-start(bf16[256,3840]{1,0:T(8,128)(2,1)} %shard_map.138.refs_0_.refs_1_.refs_2_.refs_3_) | copy-start | bytes 5898244
  338.6 16.3 %copy-start = (bf16[256,3840]{1,0:T(8,128)(2,1)S(1)}, bf16[256,3840]{1,0:T(8,128)(2,1)}, u32[]{:S(2)}) copy-start(bf16[256,3840]{1,0:T(8,128)(2,1)} %shard_map.135.refs_0_.refs_1_.refs_2_.refs_3_) | copy-start | bytes 5898244
  362.5 7.5 %copy-start.4 = (f32[256,64]{1,0:T(8,128)S(1)}, f32[256,64]{1,0:T(8,128)}, u32[]{:S(2)}) copy-start(f32[256,64]{1,0:T(8,128)} %shard_map.142) | copy-start | bytes 196612
  370.9 6.2 %collective-permute-start.2 = (bf16[2,128,64]{2,1,0:T(8,128)(2,1)S(1)}, bf16[2,128,64]{2,1,0:T(8,128)(2,1)S(1)}, u32[]{:S(2)}, u32[]{:S(2)}) collective-permute-start(bf16[2,128,64]{2,1,0:T(8,128)(2,1)S(1)} %fusion.1), channel_id=1, source_target_pairs={{16,0},{17,1},{18,2},{19,3},{20,4},{21,5},{22,6},{23,7},{24,8},{25... | collective-permute-start | bytes 98312 | tf_op jit(solution)/shard_map/ppermute | solution.py:542
  372.2 4.9 %copy-start.5 = (f32[256,64]{1,0:T(8,128)S(1)}, f32[256,64]{1,0:T(8,128)}, u32[]{:S(2)}) copy-start(f32[256,64]{1,0:T(8,128)} %shard_map.140) | copy-start | bytes 196612

commit v3 on v2

--- a/solution.py
+++ b/solution.py
@@ -12,6 +12,7 @@
 NSTEPS = 28
 LANES = 128
 BLOCK = 768
+PART = 256
 
 eps_norm = 1e-06
 flow_shift = 3.0
@@ -32,8 +33,9 @@
 
 
 def head_means(squares):
-    row = lax.broadcasted_iota(jnp.int32, (LANES, LANES), 0) // HEAD
-    col = lax.broadcasted_iota(jnp.int32, (LANES, LANES), 1) // HEAD
+    count = squares.shape[1]
+    row = lax.broadcasted_iota(jnp.int32, (count, count), 0) // HEAD
+    col = lax.broadcasted_iota(jnp.int32, (count, count), 1) // HEAD
     same = jnp.where(row == col, 1.0 / HEAD, 0.0).astype(jnp.bfloat16)
     high = squares.astype(jnp.bfloat16)
     low = (squares - high.astype(jnp.float32)).astype(jnp.bfloat16)
@@ -50,15 +52,17 @@
         xf = x_ref[...].astype(jnp.float32)
         normed_ref[...] = modulated(xf, mod_ref[0:1, :], mod_ref[1:2, :]).astype(jnp.bfloat16)
 
-    proj = jnp.dot(normed_ref[...], w_ref[...], preferred_element_type=jnp.float32)
-    for low in range(0, BLOCK, LANES):
-        part = proj[:, low : low + LANES]
-        col = step * BLOCK + low + lax.broadcasted_iota(jnp.int32, (1, LANES), 1)
+    for low in range(0, BLOCK, PART):
+        part = jnp.dot(
+            normed_ref[...], w_ref[:, low : low + PART], preferred_element_type=jnp.float32
+        )
+        first = step * BLOCK + low
+        col = first + lax.broadcasted_iota(jnp.int32, (1, PART), 1)
         factor = lax.rsqrt(head_means(part * part) + eps_norm)
-        scaled = part * factor * jnp.where(col < n_query, gain_ref[...], 1.0)
-        out_ref[:, low : low + LANES] = jnp.where(col < n_query + n_key, scaled, part).astype(
-            jnp.bfloat16
-        )
+        factor = factor * jnp.where(col < n_query, gain_ref[...], 1.0)
+        out_ref[:, low : low + PART] = (
+            part * jnp.where(col < n_query + n_key, factor, 1.0)
+        ).astype(jnp.bfloat16)
 
 
 def picked(array, lead, shape, index):
@@ -70,14 +74,14 @@
 def qkv(x, x_lead, modulation, r, gain, w, n_query, n_key):
     rows, depth = x.shape[-2:]
     columns = w.shape[1]
-    gain_row = jnp.tile(gain / math.sqrt(HEAD), LANES // HEAD)[None]
+    gain_row = jnp.tile(gain / math.sqrt(HEAD), PART // HEAD)[None]
     return pl.pallas_call(
         functools.partial(qkv_kernel, n_query, n_key),
         grid=(pl.cdiv(columns, BLOCK),),
         in_specs=[
             picked(x, x_lead, (rows, depth), lambda i: (0, 0)),
             picked(modulation, (0, r), (3, depth), lambda i: (0, 0)),
-            pl.BlockSpec((1, LANES), lambda i: (0, 0)),
+            pl.BlockSpec((1, PART), lambda i: (0, 0)),
             pl.BlockSpec((depth, BLOCK), lambda i: (0, i)),
         ],
         out_specs=pl.BlockSpec((rows, BLOCK), lambda i: (0, i)),
@@ -96,22 +100,25 @@
     q_ref, out_ref = refs[0], refs[-1]
     sets = [refs[1 + 3 * s : 4 + 3 * s] for s in range(n_sets)]
     query = q_ref[...]
+    rows = query.shape[0]
     lane = lax.broadcasted_iota(jnp.int32, (1, LANES), 1)
-    halves = []
-    for head in range(2):
-        mine = (lane >= HEAD) == (head == 1)
-        q_one = jnp.where(mine, query, jnp.zeros_like(query))
-        total = None
-        for keys, value_even, value_odd in sets:
-            values = (value_even, value_odd)[head]
-            scores = lax.dot_general(
-                q_one, keys[...], (((1,), (1,)), ((), ())), preferred_element_type=jnp.float32
-            )
-            weights = jnp.exp(scores).astype(jnp.bfloat16)
-            held = jnp.where(mine, jnp.ones((), jnp.bfloat16), values[...])
-            part = jnp.dot(weights, held, preferred_element_type=jnp.float32)
-            total = part if total is None else total + part
-        halves.append(pltpu.roll(total, HEAD, 1) / total)
+    low = lane < HEAD
+    none = jnp.zeros((), jnp.bfloat16)
+    one = jnp.ones((), jnp.bfloat16)
+    both = jnp.concatenate([jnp.where(low, query, none), jnp.where(low, none, query)], 0)
+    total = None
+    for keys, value_even, value_odd in sets:
+        scores = lax.dot_general(
+            both, keys[...], (((1,), (1,)), ((), ())), preferred_element_type=jnp.float32
+        )
+        weights = jnp.exp(scores).astype(jnp.bfloat16)
+        held = jnp.concatenate(
+            [jnp.where(low, one, value_even[...]), jnp.where(low, value_odd[...], one)], 1
+        )
+        part = jnp.dot(weights, held, preferred_element_type=jnp.float32)
+        total = part if total is None else total + part
+    even, odd = total[:rows, :LANES], total[rows:, LANES:]
+    halves = [pltpu.roll(each, HEAD, 1) / each for each in (even, odd)]
     out_ref[...] = jnp.where(lane < HEAD, halves[0], halves[1]).astype(jnp.bfloat16)
 
 
@@ -157,23 +164,24 @@
 
 
 def out_kernel(width, x_ref, attn_ref, mod_ref, w_ref, *rest):
-    attn = attn_ref[:, :width]
-    proj = jnp.concatenate(
-        [
-            jnp.dot(attn, w_ref[shard], preferred_element_type=jnp.float32)
-            for shard in range(w_ref.shape[0])
-        ],
-        -1,
-    )
-    x_next = (x_ref[...].astype(jnp.float32) + mod_ref[2:3, :] * proj).astype(jnp.bfloat16)
-    if len(rest) == 1:
-        rest[0][...] = x_next
-        return
-    fmod_ref, fw_ref, vel_ref = rest
-    final = modulated(x_next.astype(jnp.float32), fmod_ref[0:1, :], fmod_ref[1:2, :])
-    vel_ref[...] = jnp.dot(
-        final.astype(jnp.bfloat16), fw_ref[...], preferred_element_type=jnp.float32
-    )
+    step = pl.program_id(0)
+    proj_ref = rest[-1]
+    proj_ref[step] = jnp.dot(
+        attn_ref[:, :width], w_ref[...], preferred_element_type=jnp.float32
+    )
+
+    @pl.when(step == pl.num_programs(0) - 1)
+    def _():
+        proj = jnp.concatenate([proj_ref[shard] for shard in range(proj_ref.shape[0])], -1)
+        x_next = (x_ref[...].astype(jnp.float32) + mod_ref[2:3, :] * proj).astype(jnp.bfloat16)
+        if len(rest) == 2:
+            rest[0][...] = x_next
+        else:
+            fmod_ref, fw_ref, vel_ref = rest[:-1]
+            final = modulated(x_next.astype(jnp.float32), fmod_ref[0:1, :], fmod_ref[1:2, :])
+            vel_ref[...] = jnp.dot(
+                final.astype(jnp.bfloat16), fw_ref[...], preferred_element_type=jnp.float32
+            )
 
 
 def project_out(x, x_lead, attn, modulation, r, w, final=None):
@@ -184,7 +192,7 @@
         picked(x, x_lead, (rows, depth), lambda i: (0, 0)),
         pl.BlockSpec(attn.shape, lambda i: (0, 0)),
         picked(modulation, (0, r), (3, depth), lambda i: (0, 0)),
-        pl.BlockSpec(w.shape, lambda i: (0, 0, 0)),
+        pl.BlockSpec((None,) + w.shape[1:], lambda i: (i, 0, 0)),
     ]
     if final is None:
         shape = jax.ShapeDtypeStruct((rows, depth), jnp.bfloat16)
@@ -195,10 +203,11 @@
         shape = jax.ShapeDtypeStruct((rows, final[1].shape[1]), jnp.float32)
     return pl.pallas_call(
         functools.partial(out_kernel, width),
-        grid=(1,),
+        grid=(w.shape[0],),
         in_specs=specs,
         out_specs=pl.BlockSpec(shape.shape, lambda i: (0, 0)),
         out_shape=shape,
+        scratch_shapes=[pltpu.VMEM((w.shape[0], rows, w.shape[2]), jnp.float32)],
         compiler_params=PARAMS,
         cost_estimate=pl.CostEstimate(
             flops=2 * rows * depth * width,

time: 380 us -> 389 us (1.024)
  Pallas kernels: 341 us -> 351 us
    pallas_call x4, Pallas kernels: 54 us -> 67.3 us  [qkv(): pl.pallas_call(functools.partial(qkv_kernel, n_query, n_key), grid=(pl.cd...]
    pallas_call x4, Pallas kernels: 65 us -> 59.1 us  [attend(): pl.pallas_call(functools.partial(attend_kernel, 1 + len(sets)), grid=(pai...]
where the time goes in v3:
time: 389 us; the launch traced here: 388 us
  Pallas kernels  351 us (90%)
  local copies, waits for them, and re-layouts  23.3 us (6%)
  starting transfers between devices  7.26 us (2%)
    pallas_call x1, Pallas kernels, gather(): pl.pallas_call(functools.partial(gather_kernel, n), in_specs=[anywhere] *...  194 us
    pallas_call x4, Pallas kernels, qkv(): pl.pallas_call(functools.partial(qkv_kernel, n_query, n_key), grid=(pl.cd...  67.3 us
    pallas_call x4, Pallas kernels, attend(): pl.pallas_call(functools.partial(attend_kernel, 1 + len(sets)), grid=(pai...  59.1 us
    pallas_call x4, Pallas kernels, project_out(): pl.pallas_call(functools.partial(out_kernel, width), grid=(w.shape[0],),...  30.8 us
    unnamed x26, local copies, waits for them, and re-layouts  8 us
  transfers between devices with their start and end apart: 3, of which 1 were waited for; matrix products, arithmetic and copies ran while one was open for 1% of the time, Pallas kernels for 18%

profile of v3, /device:TPU:0, one launch (start us, length us, event | category | flops | bytes accessed | tf_op | source)
XLA Modules:
  0.0 388.3 jit_solution(6010321802514947385)
XLA Ops:
  0.6 2.6 slice.33
  3.3 3.2 slice.34
  6.5 0.0 copy-done.8
  6.5 0.6 broadcast_in_dim_tile.2.gain_ref
  7.2 0.0 copy-done.7
  7.2 0.7 copy.14.mod_ref
  7.8 2.7 copy.16.refs_13_.refs_14_.refs_15_
  10.5 7.1 %concatenate.17.w_ref = bf16[608,3840]{1,0:T(8,128)(2,1)} concatenate(bf16[608,1216]{1,0:T(8,128)(2,1)} %slice.33, bf16[608,64]{1,0:T(8,128)(2,1)S(1)} %broadcast_in_dim.4, bf16[608,2432]{1,0:T(8,128)(2,1)S(1)} %slice.34, bf16[608,128]{1,0:T(8,128)(2,1)S(1)} %broadcast_in_dim.10), dimensions={1} | concatenate | bytes 9338880 | tf_op jit(solution)/shard_map/concatenate | solution.py:503
  17.7 193.9 %shard_map.130 = (bf16[2432,3840]{1,0:T(8,128)(2,1)}, bf16[4,1216,608]{2,1,0:T(8,128)(2,1)}, bf16[3,2,256,2432]{3,2,1,0:T(8,128)(2,1)}) custom-call(bf16[608,3840]{1,0:T(8,128)(2,1)} %concatenate.17.w_ref, bf16[1216,608]{1,0:T(8,128)(2,1)} %bitcast.18, bf16[2,256,2432]{2,1,0:T(8,128)(2,1)} %bitcast.17), custom_call_target="tpu_custom_call" | custom-call | bytes 37355520 | tf_op jit(solution)/shard_map/pallas_call | solution.py:451
  211.6 16.8 %shard_map.132.refs_0_.refs_1_.refs_2_.refs_3_ = bf16[256,3840]{1,0:T(8,128)(2,1)} custom-call(bf16[2,256,2432]{2,1,0:T(8,128)(2,1)} %x_ref.7, f32[1,2,3,2432]{3,2,1,0:T(4,128)} %copy.14.mod_ref, f32[1,256]{1,0:T(1,128)} %broadcast_in_dim_tile.2.gain_ref, bf16[2432,3840]{1,0:T(8,128)(2,1)} %get-tuple-element.6.w_ref), custom_call_target="tpu_custom_call" | custom-call | flops 4781506560 | bytes 21889024 | tf_op jit(solution)/shard_map/pallas_call | solution.py:78
  228.4 14.7 %shard_map.136.attn_ref = bf16[256,1280]{1,0:T(8,128)(2,1)} custom-call(bf16[256,3840]{1,0:T(8,128)(2,1)} %shard_map.132.refs_0_.refs_1_.refs_2_.refs_3_, bf16[256,3840]{1,0:T(8,128)(2,1)} %shard_map.132.refs_0_.refs_1_.refs_2_.refs_3_, bf16[256,3840]{1,0:T(8,128)(2,1)} %shard_map.132.refs_0_.refs_1_.refs_2_.refs_3_, ...), custom_call_target="tpu_custom_call" | custom-call | flops 5867307008 | bytes 5729792 | tf_op jit(solution)/shard_map/pallas_call | solution.py:151
  243.2 7.3 %shard_map.137 = bf16[256,2432]{1,0:T(8,128)(2,1)} custom-call(bf16[2,256,2432]{2,1,0:T(8,128)(2,1)} %x_ref.7, bf16[256,1280]{1,0:T(8,128)(2,1)} %shard_map.136.attn_ref, f32[1,2,3,2432]{3,2,1,0:T(4,128)} %copy.14.mod_ref, bf16[4,1216,608]{2,1,0:T(8,128)(2,1)} %get-tuple-element.8.w_ref), custom_call_target="tpu_custom_call" | custom-call | flops 1514143744 | bytes 9650176 | tf_op jit(solution)/shard_map/pallas_call | solution.py:204
  250.4 3.6 collective-permute-start.1
  254.1 16.8 %shard_map.131.refs_0_.refs_1_.refs_2_.refs_3_ = bf16[256,3840]{1,0:T(8,128)(2,1)} custom-call(bf16[2,256,2432]{2,1,0:T(8,128)(2,1)} %x_ref.7, f32[1,2,3,2432]{3,2,1,0:T(4,128)} %copy.14.mod_ref, f32[1,256]{1,0:T(1,128)} %broadcast_in_dim_tile.2.gain_ref, bf16[2432,3840]{1,0:T(8,128)(2,1)} %get-tuple-element.6.w_ref), custom_call_target="tpu_custom_call" | custom-call | flops 4781506560 | bytes 21889024 | tf_op jit(solution)/shard_map/pallas_call | solution.py:78
  270.9 14.7 %shard_map.133.attn_ref = bf16[256,1280]{1,0:T(8,128)(2,1)} custom-call(bf16[256,3840]{1,0:T(8,128)(2,1)} %shard_map.131.refs_0_.refs_1_.refs_2_.refs_3_, bf16[256,3840]{1,0:T(8,128)(2,1)} %shard_map.131.refs_0_.refs_1_.refs_2_.refs_3_, bf16[256,3840]{1,0:T(8,128)(2,1)} %shard_map.131.refs_0_.refs_1_.refs_2_.refs_3_, ...), custom_call_target="tpu_custom_call" | custom-call | flops 5867307008 | bytes 5729792 | tf_op jit(solution)/shard_map/pallas_call | solution.py:151
  285.6 0.0 copy-start.6
  285.7 0.0 copy-start.9
  285.7 0.0 copy-start
  285.7 7.4 %shard_map.134 = bf16[256,2432]{1,0:T(8,128)(2,1)} custom-call(bf16[2,256,2432]{2,1,0:T(8,128)(2,1)} %x_ref.7, bf16[256,1280]{1,0:T(8,128)(2,1)} %shard_map.133.attn_ref, f32[1,2,3,2432]{3,2,1,0:T(4,128)} %copy.14.mod_ref, bf16[4,1216,608]{2,1,0:T(8,128)(2,1)} %get-tuple-element.8.w_ref), custom_call_target="tpu_custom_call" | custom-call | flops 1514143744 | bytes 9650176 | tf_op jit(solution)/shard_map/pallas_call | solution.py:204
  293.1 2.3 collective-permute-start
  295.4 0.0 copy-done.6
  295.4 0.1 copy.36
  295.5 2.1 copy.30.rest_1_
  297.6 0.0 copy-done.9
  297.6 0.0 copy-done
  297.6 1.5 slice_bitcast_fusion.2
  299.1 0.0 collective-permute-done.1.x_ref
  299.1 0.0 copy-start.3
  299.1 1.0 copy-done.3
  300.1 16.8 %shard_map.138.refs_0_.refs_1_.refs_2_.refs_3_ = bf16[256,3840]{1,0:T(8,128)(2,1)} custom-call(bf16[256,2432]{1,0:T(8,128)(2,1)} %copy-done.3, f32[1,2,3,2432]{3,2,1,0:T(4,128)} %copy.14.mod_ref, f32[1,256]{1,0:T(1,128)} %broadcast_in_dim_tile.2.gain_ref, bf16[2432,3840]{1,0:T(8,128)(2,1)} %get-tuple-element.6.w_ref), custom_call_target="tpu_custom_call" | custom-call | flops 4781506560 | bytes 21889024 | tf_op jit(solution)/shard_map/pallas_call | solution.py:78
  317.0 14.8 %shard_map.141.attn_ref = bf16[256,1280]{1,0:T(8,128)(2,1)} custom-call(bf16[256,3840]{1,0:T(8,128)(2,1)} %shard_map.138.refs_0_.refs_1_.refs_2_.refs_3_, bf16[256,3840]{1,0:T(8,128)(2,1)} %shard_map.138.refs_0_.refs_1_.refs_2_.refs_3_, bf16[256,3840]{1,0:T(8,128)(2,1)} %shard_map.138.refs_0_.refs_1_.refs_2_.refs_3_, ...), custom_call_target="tpu_custom_call" | custom-call | flops 5867307008 | bytes 5729792 | tf_op jit(solution)/shard_map/pallas_call | solution.py:151
  331.8 0.0 copy-done.2
  331.8 0.1 slice_bitcast_fusion
  331.9 0.0 collective-permute-done.x_ref
  331.9 16.8 %shard_map.135.refs_0_.refs_1_.refs_2_.refs_3_ = bf16[256,3840]{1,0:T(8,128)(2,1)} custom-call(bf16[256,2432]{1,0:T(8,128)(2,1)} %collective-permute-done.x_ref, f32[1,2,3,2432]{3,2,1,0:T(4,128)} %copy.14.mod_ref, f32[1,256]{1,0:T(1,128)} %broadcast_in_dim_tile.2.gain_ref, bf16[2432,3840]{1,0:T(8,128)(2,1)} %get-tuple-element.6.w_ref), custom_call_target="tpu_custom_call" | custom-call | flops 4781506560 | bytes 21889024 | tf_op jit(solution)/shard_map/pallas_call | solution.py:78
  348.7 14.8 %shard_map.139.attn_ref = bf16[256,1280]{1,0:T(8,128)(2,1)} custom-call(bf16[256,3840]{1,0:T(8,128)(2,1)} %shard_map.135.refs_0_.refs_1_.refs_2_.refs_3_, bf16[256,3840]{1,0:T(8,128)(2,1)} %shard_map.135.refs_0_.refs_1_.refs_2_.refs_3_, bf16[256,3840]{1,0:T(8,128)(2,1)} %shard_map.135.refs_0_.refs_1_.refs_2_.refs_3_, ...), custom_call_target="tpu_custom_call" | custom-call | flops 5867307008 | bytes 5729792 | tf_op jit(solution)/shard_map/pallas_call | solution.py:151
  363.5 0.0 copy-done.1
  363.5 0.1 slice_bitcast_fusion.1
  363.6 8.0 %shard_map.142 = f32[256,64]{1,0:T(8,128)} custom-call(bf16[256,2432]{1,0:T(8,128)(2,1)} %copy-done.3, bf16[256,1280]{1,0:T(8,128)(2,1)} %shard_map.141.attn_ref, f32[1,2,3,2432]{3,2,1,0:T(4,128)} %copy.14.mod_ref, bf16[4,1216,608]{2,1,0:T(8,128)(2,1)} %get-tuple-element.8.w_ref, f32[2,2,2432]{2,1,0:T(2,128)} %rest_0_.3, bf16[2432,64]{1,0:T(8,128)(2,1)} %copy.30.rest_1_), custom_call_target="tpu_custom_call" | custom-call | flops 1514143744 | bytes 9650176 | tf_op jit(solution)/shard_map/pallas_call | solution.py:204
  371.7 8.1 %shard_map.140 = f32[256,64]{1,0:T(8,128)} custom-call(bf16[256,2432]{1,0:T(8,128)(2,1)} %collective-permute-done.x_ref, bf16[256,1280]{1,0:T(8,128)(2,1)} %shard_map.139.attn_ref, f32[1,2,3,2432]{3,2,1,0:T(4,128)} %copy.14.mod_ref, bf16[4,1216,608]{2,1,0:T(8,128)(2,1)} %get-tuple-element.8.w_ref, f32[2,2,2432]{2,1,0:T(2,128)} %rest_0_.3, ...), custom_call_target="tpu_custom_call" | custom-call | flops 1514143744 | bytes 9650176 | tf_op jit(solution)/shard_map/pallas_call | solution.py:204
  379.8 0.0 copy-done.4
  379.8 0.9 fusion.1
  380.6 1.3 collective-permute-start.2
  381.9 1.9 maximum_select_fusion
  383.8 3.0 collective-permute-done.2
  386.8 0.1 multiply_subtract_fusion
  386.9 0.7 copy.39
  387.6 0.7 copy.38
  (12 shorter events, 0.1 us)
Async XLA Ops:
  3.3 3.2 copy-start.8
  3.3 3.9 copy-start.7
  250.4 48.6 %collective-permute-start.1 = (bf16[256,2432]{1,0:T(8,128)(2,1)}, bf16[256,2432]{1,0:T(8,128)(2,1)S(1)}, u32[]{:S(2)}, u32[]{:S(2)}) collective-permute-start(bf16[256,2432]{1,0:T(8,128)(2,1)} %shard_map.137), channel_id=1, source_target_pairs={{0,16},{1,17},{2,18},{3,19},{4,20},{5,21},{6,22},{7,23},{8,24},{9,... | collective-permute-start | bytes 3735560 | tf_op jit(solution)/shard_map/ppermute | solution.py:542
  285.6 9.8 %copy-start.6 = (f32[2,128,64]{1,2,0:T(8,128)S(1)}, f32[2,128,64]{1,2,0:T(8,128)}, u32[]{:S(2)}) copy-start(f32[2,128,64]{1,2,0:T(8,128)} %param.20) | copy-start | bytes 196612
  285.7 11.9 %copy-start.9 = (s32[2]{0:T(128)S(1)}, s32[2]{0:T(128)}, u32[]{:S(2)}) copy-start(s32[2]{0:T(128)} %param.21) | copy-start | bytes 28
  285.7 11.9 %copy-start = (bf16[256,3840]{1,0:T(8,128)(2,1)S(1)}, bf16[256,3840]{1,0:T(8,128)(2,1)}, u32[]{:S(2)}) copy-start(bf16[256,3840]{1,0:T(8,128)(2,1)} %shard_map.132.refs_0_.refs_1_.refs_2_.refs_3_) | copy-start | bytes 5898244
  293.1 38.8 %collective-permute-start = (bf16[256,2432]{1,0:T(8,128)(2,1)}, bf16[256,2432]{1,0:T(8,128)(2,1)}, u32[]{:S(2)}, u32[]{:S(2)}) collective-permute-start(bf16[256,2432]{1,0:T(8,128)(2,1)} %shard_map.134), channel_id=1, source_target_pairs={{0,16},{1,17},{2,18},{3,19},{4,20},{5,21},{6,22},{7,23},{8,24},{9,... | collective-permute-start | bytes 3735560 | tf_op jit(solution)/shard_map/ppermute | solution.py:542
  299.1 1.0 copy-start.3
  317.0 14.8 %copy-start.2 = (bf16[256,3840]{1,0:T(8,128)(2,1)S(1)}, bf16[256,3840]{1,0:T(8,128)(2,1)}, u32[]{:S(2)}) copy-start(bf16[256,3840]{1,0:T(8,128)(2,1)} %shard_map.138.refs_0_.refs_1_.refs_2_.refs_3_) | copy-start | bytes 5898244
  348.7 14.8 %copy-start.1 = (bf16[256,3840]{1,0:T(8,128)(2,1)S(1)}, bf16[256,3840]{1,0:T(8,128)(2,1)}, u32[]{:S(2)}) copy-start(bf16[256,3840]{1,0:T(8,128)(2,1)} %shard_map.135.refs_0_.refs_1_.refs_2_.refs_3_) | copy-start | bytes 5898244
  371.7 8.1 %copy-start.4 = (f32[256,64]{1,0:T(8,128)S(1)}, f32[256,64]{1,0:T(8,128)}, u32[]{:S(2)}) copy-start(f32[256,64]{1,0:T(8,128)} %shard_map.142) | copy-start | bytes 196612
  380.6 6.2 %collective-permute-start.2 = (bf16[2,128,64]{2,1,0:T(8,128)(2,1)S(1)}, bf16[2,128,64]{2,1,0:T(8,128)(2,1)S(1)}, u32[]{:S(2)}, u32[]{:S(2)}) collective-permute-start(bf16[2,128,64]{2,1,0:T(8,128)(2,1)S(1)} %fusion.1), channel_id=1, source_target_pairs={{16,0},{17,1},{18,2},{19,3},{20,4},{21,5},{22,6},{23,7},{24,8},{25... | collective-permute-start | bytes 98312 | tf_op jit(solution)/shard_map/ppermute | solution.py:551
  381.9 4.9 %copy-start.5 = (f32[256,64]{1,0:T(8,128)S(1)}, f32[256,64]{1,0:T(8,128)}, u32[]{:S(2)}) copy-start(f32[256,64]{1,0:T(8,128)} %shard_map.140) | copy-start | bytes 196612

commit v4 on v2

--- a/solution.py
+++ b/solution.py
@@ -43,8 +43,10 @@
 
 
 def qkv_kernel(n_query, n_key, x_ref, mod_ref, gain_ref, w_ref, out_ref, normed_ref):
-    step = pl.program_id(0)
-
+    qkv_step(pl.program_id(0), n_query, n_key, x_ref, mod_ref, gain_ref, w_ref, out_ref, normed_ref)
+
+
+def qkv_step(step, n_query, n_key, x_ref, mod_ref, gain_ref, w_ref, out_ref, normed_ref):
     @pl.when(step == 0)
     def _():
         xf = x_ref[...].astype(jnp.float32)
@@ -59,6 +61,25 @@
         out_ref[:, low : low + LANES] = jnp.where(col < n_query + n_key, scaled, part).astype(
             jnp.bfloat16
         )
+
+
+def pack_kernel(width, n_query, w_ref, out_ref):
+    out_ref[...] = jnp.zeros_like(out_ref)
+    out_ref[:, :width] = w_ref[:, :width]
+    out_ref[:, n_query : n_query + 2 * width] = w_ref[:, width:]
+
+
+def pack(w, width, n_query, columns):
+    rows = w.shape[0]
+    block = min(rows, 160)
+    return pl.pallas_call(
+        functools.partial(pack_kernel, width, n_query),
+        grid=(pl.cdiv(rows, block),),
+        in_specs=[pl.BlockSpec((block, w.shape[1]), lambda i: (i, 0))],
+        out_specs=pl.BlockSpec((block, columns), lambda i: (i, 0)),
+        out_shape=jax.ShapeDtypeStruct((rows, columns), w.dtype),
+        compiler_params=PARAMS,
+    )(w)
 
 
 def picked(array, lead, shape, index):
@@ -96,27 +117,35 @@
     q_ref, out_ref = refs[0], refs[-1]
     sets = [refs[1 + 3 * s : 4 + 3 * s] for s in range(n_sets)]
     query = q_ref[...]
+    rows = query.shape[0]
     lane = lax.broadcasted_iota(jnp.int32, (1, LANES), 1)
-    halves = []
-    for head in range(2):
-        mine = (lane >= HEAD) == (head == 1)
-        q_one = jnp.where(mine, query, jnp.zeros_like(query))
-        total = None
-        for keys, value_even, value_odd in sets:
-            values = (value_even, value_odd)[head]
-            scores = lax.dot_general(
-                q_one, keys[...], (((1,), (1,)), ((), ())), preferred_element_type=jnp.float32
-            )
-            weights = jnp.exp(scores).astype(jnp.bfloat16)
-            held = jnp.where(mine, jnp.ones((), jnp.bfloat16), values[...])
-            part = jnp.dot(weights, held, preferred_element_type=jnp.float32)
-            total = part if total is None else total + part
-        halves.append(pltpu.roll(total, HEAD, 1) / total)
+    low = lane < HEAD
+    none = jnp.zeros((), jnp.bfloat16)
+    one = jnp.ones((), jnp.bfloat16)
+    both = jnp.concatenate([jnp.where(low, query, none), jnp.where(low, none, query)], 0)
+    def scores_of(keys):
+        return lax.dot_general(
+            both, keys[...], (((1,), (1,)), ((), ())), preferred_element_type=jnp.float32
+        )
+
+    total = None
+    scores = scores_of(sets[0][0])
+    for place, (_, value_even, value_odd) in enumerate(sets):
+        ahead = scores_of(sets[place + 1][0]) if place + 1 < len(sets) else None
+        weights = jnp.exp(scores).astype(jnp.bfloat16)
+        held = jnp.concatenate(
+            [jnp.where(low, one, value_even[...]), jnp.where(low, value_odd[...], one)], 1
+        )
+        part = jnp.dot(weights, held, preferred_element_type=jnp.float32)
+        total = part if total is None else total + part
+        scores = ahead
+    even, odd = total[:rows, :LANES], total[rows:, LANES:]
+    halves = [pltpu.roll(each, HEAD, 1) / each for each in (even, odd)]
     out_ref[...] = jnp.where(lane < HEAD, halves[0], halves[1]).astype(jnp.bfloat16)
 
 
-def attend(qkv_out, n_query, sets, width):
-    rows = qkv_out.shape[0]
+def attend(qkv_out, held_lead, n_query, sets, width):
+    rows = qkv_out.shape[-2]
     pairs = n_query // LANES
     own = n_query // LANES
     last = 2 * width // LANES - 1
@@ -135,9 +164,9 @@
             ),
         ]
 
-    in_specs = [pl.BlockSpec((rows, LANES), lambda i: (0, i))]
+    in_specs = [picked(qkv_out, held_lead, (rows, LANES), lambda i: (0, i))]
     operands = [qkv_out]
-    for array, lead, offset in [(qkv_out, (), own)] + [pair + (0,) for pair in sets]:
+    for array, lead, offset in [(qkv_out, held_lead, own)] + [pair + (0,) for pair in sets]:
         in_specs += specs(array, lead, offset)
         operands += [array] * 3
     count = rows + sum(array.shape[-2] for array, _ in sets)
@@ -217,6 +246,83 @@
     return ((0, first), (first, rows - first))
 
 
+def greet(n, me, patch):
+    has_left, has_right = me > 0, me < n - 1
+    barrier = pltpu.get_barrier_semaphore()
+    for other in (1, 2):
+        pl.semaphore_signal(
+            barrier, inc=1, device_id={"patch": patch ^ other}, device_id_type=MESH
+        )
+
+    @pl.when(has_left)
+    def _():
+        pl.semaphore_signal(barrier, inc=1, device_id={"shard": me - 1}, device_id_type=MESH)
+
+    @pl.when(has_right)
+    def _():
+        pl.semaphore_signal(barrier, inc=1, device_id={"shard": me + 1}, device_id_type=MESH)
+
+    pl.semaphore_wait(
+        barrier, 2 + jnp.where(has_left, 1, 0) + jnp.where(has_right, 1, 0)
+    )
+
+
+def shard_block(me, way, t):
+    return me - t if way == 0 else me + t
+
+
+def out_copies(wo_ref, wo_all, os_, or_):
+    me = lax.axis_index("shard")
+    patch = lax.axis_index("patch")
+    o_rows = wo_all.shape[1] // 2
+
+    def o_copy(way, t, sending):
+        b = shard_block(me, way, t if sending else t + 1)
+        half = pl.ds(pl.multiple_of((patch % 2) * o_rows, 16), o_rows)
+        dst = wo_all.at[b, half]
+        src = wo_ref.at[half] if sending and t == 0 else dst
+        return pltpu.make_async_remote_copy(
+            src_ref=src,
+            dst_ref=dst,
+            send_sem=os_.at[0, way, t],
+            recv_sem=or_.at[0, way, t],
+            device_id={"shard": me + 1 if way == 0 else me - 1},
+            device_id_type=MESH,
+        )
+
+    def o_hop(way, t, sending):
+        parity = patch % 2 if sending else 1 - patch % 2
+        place = wo_all.at[
+            shard_block(me, way, t + 1), pl.ds(pl.multiple_of(parity * o_rows, 16), o_rows)
+        ]
+        return pltpu.make_async_remote_copy(
+            src_ref=place,
+            dst_ref=place,
+            send_sem=os_.at[1, way, t],
+            recv_sem=or_.at[1, way, t],
+            device_id={"patch": patch ^ 1},
+            device_id_type=MESH,
+        )
+
+    return o_copy, o_hop
+
+
+def stale_copies(stale_ref, stale_all, ss, sr, first=0):
+    patch = lax.axis_index("patch")
+
+    def s_copy(kind, r):
+        return pltpu.make_async_remote_copy(
+            src_ref=stale_all.at[0, r] if kind == 2 else stale_ref.at[r + first],
+            dst_ref=stale_all.at[kind, r],
+            send_sem=ss.at[kind, r],
+            recv_sem=sr.at[kind, r],
+            device_id={"patch": patch ^ (2 if kind == 0 else 1)},
+            device_id_type=MESH,
+        )
+
+    return s_copy
+
+
 def gather_kernel(
     n, w_ref, wo_ref, stale_ref, w_all, wo_all, stale_all, own, zs, zr, hs, hr, os_, or_, ss, sr
 ):
@@ -224,28 +330,10 @@
     patch = lax.axis_index("patch")
     rows, columns = w_ref.shape
     half_rows, half_columns = rows // 2, columns // 2
-    o_rows = wo_ref.shape[0] // 2
     chunks = row_chunks(half_rows)
-    requests = stale_ref.shape[0]
     has_left, has_right = me > 0, me < n - 1
 
-    barrier = pltpu.get_barrier_semaphore()
-    for other in (1, 2):
-        pl.semaphore_signal(
-            barrier, inc=1, device_id={"patch": patch ^ other}, device_id_type=MESH
-        )
-
-    @pl.when(has_left)
-    def _():
-        pl.semaphore_signal(barrier, inc=1, device_id={"shard": me - 1}, device_id_type=MESH)
-
-    @pl.when(has_right)
-    def _():
-        pl.semaphore_signal(barrier, inc=1, device_id={"shard": me + 1}, device_id_type=MESH)
-
-    pl.semaphore_wait(
-        barrier, 2 + jnp.where(has_left, 1, 0) + jnp.where(has_right, 1, 0)
-    )
+    greet(n, me, patch)
 
     def spot(ref, base, quarter, k):
         start, size = chunks[k]
@@ -289,43 +377,9 @@
             device_id_type=MESH,
         )
 
-    def o_copy(way, t, sending):
-        b = block(way, t if sending else t + 1)
-        half = pl.ds(pl.multiple_of((patch % 2) * o_rows, 16), o_rows)
-        dst = wo_all.at[b, half]
-        src = wo_ref.at[half] if sending and t == 0 else dst
-        return pltpu.make_async_remote_copy(
-            src_ref=src,
-            dst_ref=dst,
-            send_sem=os_.at[0, way, t],
-            recv_sem=or_.at[0, way, t],
-            device_id={"shard": me + 1 if way == 0 else me - 1},
-            device_id_type=MESH,
-        )
-
-    def o_hop(way, t, sending):
-        parity = patch % 2 if sending else 1 - patch % 2
-        place = wo_all.at[
-            block(way, t + 1), pl.ds(pl.multiple_of(parity * o_rows, 16), o_rows)
-        ]
-        return pltpu.make_async_remote_copy(
-            src_ref=place,
-            dst_ref=place,
-            send_sem=os_.at[1, way, t],
-            recv_sem=or_.at[1, way, t],
-            device_id={"patch": patch ^ 1},
-            device_id_type=MESH,
-        )
-
-    def s_copy(kind, r):
-        return pltpu.make_async_remote_copy(
-            src_ref=stale_all.at[0, r] if kind == 2 else stale_ref.at[r],
-            dst_ref=stale_all.at[kind, r],
-            send_sem=ss.at[kind, r],
-            recv_sem=sr.at[kind, r],
-            device_id={"patch": patch ^ (2 if kind == 0 else 1)},
-            device_id_type=MESH,
-        )
+    o_copy, o_hop = out_copies(wo_ref, wo_all, os_, or_)
+
+    s_copy = stale_copies(stale_ref, stale_all, ss, sr)
 
     for way in range(2):
 
@@ -335,8 +389,7 @@
                 z_copy(way, 0, k, True).start()
 
     s_copy(0, 0).start()
-    for r in range(requests):
-        s_copy(1, r).start()
+    s_copy(1, 0).start()
     own_w = pltpu.make_async_copy(
         w_ref, w_all.at[pl.ds(pl.multiple_of(me * rows, 16), rows)], own.at[0]
     )
@@ -376,19 +429,16 @@
             def _(way=way):
                 o_copy(way, 0, True).start()
 
-    for r in range(1, requests):
-        s_copy(0, r).start()
     s_copy(0, 0).wait_recv()
     s_copy(2, 0).start()
-    for place in range(max(len(items) - 2 * LAG, 0), len(items)):
-        pass_on(*items[place])
-    for t in range(n - 1):
+    left = items[max(len(items) - 2 * LAG, 0) :]
+    for t in range(n - 2):
         for way in range(2):
 
             @pl.when(incoming(way, t))
             def _(way=way, t=t):
                 o_copy(way, t, False).wait_recv()
-                if t + 1 < n - 1:
+                if t + 1 < n - 2:
 
                     @pl.when(ahead(way))
                     def _():
@@ -396,9 +446,10 @@
 
                 o_hop(way, t, True).start()
 
-    for r in range(1, requests):
-        s_copy(0, r).wait_recv()
-        s_copy(2, r).start()
+        share = pl.cdiv(len(left), n - 2)
+        for item in left[t * share : (t + 1) * share]:
+            pass_on(*item)
+
     for way, t, k in items:
 
         @pl.when(incoming(way, t))
@@ -414,7 +465,7 @@
         def _(way=way, t=t, k=k):
             z_copy(way, t, k, True).wait_send()
 
-        if k == 0:
+        if k == 0 and t < n - 2:
 
             @pl.when(incoming(way, t))
             def _(way=way, t=t):
@@ -425,11 +476,10 @@
             def _(way=way, t=t):
                 o_copy(way, t, True).wait_send()
 
-    for r in range(requests):
-        for kind in range(3):
-            s_copy(kind, r).wait_send()
-        for kind in (1, 2):
-            s_copy(kind, r).wait_recv()
+    for kind in range(3):
+        s_copy(kind, 0).wait_send()
+    for kind in (1, 2):
+        s_copy(kind, 0).wait_recv()
     own_w.wait()
     own_o.wait()
 
@@ -438,7 +488,6 @@
     rows, columns = w.shape
     anywhere = pl.BlockSpec(memory_space=pl.ANY)
     dma = pltpu.SemaphoreType.DMA
-    requests = stale.shape[0]
     return pl.pallas_call(
         functools.partial(gather_kernel, n),
         in_specs=[anywhere] * 3,
@@ -446,7 +495,7 @@
         out_shape=[
             jax.ShapeDtypeStruct((n * rows, columns), w.dtype),
             jax.ShapeDtypeStruct((n,) + w_out.shape, w_out.dtype),
-            jax.ShapeDtypeStruct((3,) + stale.shape, stale.dtype),
+            jax.ShapeDtypeStruct((3, 1) + stale.shape[1:], stale.dtype),
         ],
         scratch_shapes=[
             dma((2,)),
@@ -454,10 +503,10 @@
             dma((2, n - 1, 2)),
             dma((3, 2, n - 1, 2)),
             dma((3, 2, n - 1, 2)),
-            dma((2, 2, n - 1)),
-            dma((2, 2, n - 1)),
-            dma((3, requests)),
-            dma((3, requests)),
+            dma((2, 2, n - 2)),
+            dma((2, 2, n - 2)),
+            dma((3, 1)),
+            dma((3, 1)),
         ],
         compiler_params=pltpu.CompilerParams(
             collective_id=0, has_side_effects=True, vmem_limit_bytes=56 * 1024 * 1024
@@ -466,6 +515,115 @@
             flops=0, bytes_accessed=4 * n * rows * columns, transcendentals=0
         ),
     )(w, w_out, stale)
+
+
+def first_kernel(
+    n, n_query, n_key, x_ref, mod_ref, gain_ref, w_ref, stale_ref, wo_in, out_ref, wo_all,
+    stale_all, normed_ref, os_, or_, ss, sr,
+):
+    step = pl.program_id(1)
+    at = pl.program_id(0) * pl.num_programs(1) + step
+    last = pl.num_programs(0) * pl.num_programs(1) - 1
+    me = lax.axis_index("shard")
+    o_copy, o_hop = out_copies(None, wo_all, os_, or_)
+    s_copy = stale_copies(stale_ref, stale_all, ss, sr, 1)
+    others = stale_all.shape[1]
+    ends = (me == n - 1, me == 0)
+    before = (me == n - 2, me == 1)
+
+    @pl.when(at == 0)
+    def _():
+        greet(n, me, lax.axis_index("patch"))
+        for way in range(2):
+
+            @pl.when(before[way])
+            def _(way=way):
+                o_copy(way, n - 2, True).start()
+
+        for r in range(others):
+            s_copy(0, r).start()
+            s_copy(1, r).start()
+
+    qkv_step(step, n_query, n_key, x_ref, mod_ref, gain_ref, w_ref, out_ref, normed_ref)
+
+    @pl.when(at == last - 1)
+    def _():
+        for way in range(2):
+
+            @pl.when(ends[way])
+            def _(way=way):
+                o_copy(way, n - 2, False).wait_recv()
+                o_hop(way, n - 2, True).start()
+
+        for r in range(others):
+            s_copy(0, r).wait_recv()
+            s_copy(2, r).start()
+
+    @pl.when(at == last)
+    def _():
+        for way in range(2):
+
+            @pl.when(before[way])
+            def _(way=way):
+                o_copy(way, n - 2, True).wait_send()
+
+            @pl.when(ends[way])
+            def _(way=way):
+                o_hop(way, n - 2, True).wait_send()
+                o_hop(way, n - 2, False).wait_recv()
+
+        for r in range(others):
+            for kind in range(3):
+                s_copy(kind, r).wait_send()
+            for kind in (1, 2):
+                s_copy(kind, r).wait_recv()
+
+
+def first_qkv(x, modulation, gain, w, stale, wo_all, n, n_query, n_key):
+    requests, rows, depth = x.shape
+    columns = w.shape[1]
+    gain_row = jnp.tile(gain / math.sqrt(HEAD), LANES // HEAD)[None]
+    anywhere = pl.BlockSpec(memory_space=pl.ANY)
+    dma = pltpu.SemaphoreType.DMA
+    others = requests - 1
+    return pl.pallas_call(
+        functools.partial(first_kernel, n, n_query, n_key),
+        grid=(requests, pl.cdiv(columns, BLOCK)),
+        in_specs=[
+            pl.BlockSpec((None, rows, depth), lambda r, i: (r, 0, 0)),
+            pl.BlockSpec((None, None, 3, depth), lambda r, i: (0, r, 0, 0)),
+            pl.BlockSpec((1, LANES), lambda r, i: (0, 0)),
+            pl.BlockSpec((depth, BLOCK), lambda r, i: (0, i)),
+            anywhere,
+            anywhere,
+        ],
+        out_specs=[
+            pl.BlockSpec((None, rows, BLOCK), lambda r, i: (r, 0, i)),
+            anywhere,
+            anywhere,
+        ],
+        out_shape=[
+            jax.ShapeDtypeStruct((requests, rows, columns), jnp.bfloat16),
+            jax.ShapeDtypeStruct(wo_all.shape, wo_all.dtype),
+            jax.ShapeDtypeStruct((3, others) + stale.shape[1:], stale.dtype),
+        ],
+        scratch_shapes=[
+            pltpu.VMEM((rows, depth), jnp.bfloat16),
+            dma((2, 2, n - 1)),
+            dma((2, 2, n - 1)),
+            dma((3, others)),
+            dma((3, others)),
+        ],
+        input_output_aliases={5: 1},
+        compiler_params=pltpu.CompilerParams(
+            collective_id=1, has_side_effects=True, vmem_limit_bytes=56 * 1024 * 1024
+        ),
+        cost_estimate=pl.CostEstimate(
+            flops=2 * requests * rows * depth * columns,
+            bytes_accessed=2 * depth * columns * requests,
+            transcendentals=0,
+        ),
+    )(x, modulation, gain_row, w, stale, wo_all)
 
 
 def on_device(
@@ -491,18 +649,17 @@
 
     columns = pl.cdiv(n_query + 2 * width, 2 * LANES) * 2 * LANES
     w = qkv_weight[0]
-    packed = jnp.concatenate(
-        [
-            w[:, :width],
-            jnp.zeros((w.shape[0], n_query - width), w.dtype),
-            w[:, width:],
-            jnp.zeros((w.shape[0], columns - n_query - 2 * width), w.dtype),
-        ],
-        1,
-    )
-    if patches == 4 and w.shape[0] % 32 == 0 and width % 32 == 0:
-        w_qkv, w_out, stale = gather(packed, out_weight[0], stale_kv[0], shards)
-        stale = [(stale, (i,)) for i in range(3)]
+    packed = pack(w, width, n_query, columns)
+    if patches == 4 and shards > 2 and requests > 1 and w.shape[0] % 32 == 0 and width % 32 == 0:
+        w_qkv, w_out, stale_first = gather(packed, out_weight[0], stale_kv[0], shards)
+        held, w_out, stale_rest = first_qkv(
+            hidden, modulation, score_gain[0], w_qkv, stale_kv[0], w_out, shards, n_query, width
+        )
+        helds = [(held, (r,)) for r in range(requests)]
+        stale = [
+            [(stale_rest, (i, r - 1)) if r else (stale_first, (i, 0)) for i in range(3)]
+            for r in range(requests)
+        ]
     else:
         share = w.shape[0] // patches
         mine = lax.dynamic_slice_in_dim(packed, patch * share, share, 0)
@@ -517,26 +674,33 @@
             pairs = [(p, p ^ step) for p in range(patches)]
             stale = stale + [lax.ppermute(array, "patch", pairs) for array in stale]
             step //= 2
-        stale = [(array, ()) for array in stale[1:]]
-
-    def layer(r, x, x_lead, final=None):
-        held = qkv(x, x_lead, modulation, r, score_gain[0], w_qkv, n_query, width)
-        sets = [(array, lead + (r,)) for array, lead in stale] + [(text_kv, (0, r))]
-        attn = attend(held, n_query, sets, width)
-        fresh = held[:, n_query : n_query + 2 * width]
-        return project_out(x, x_lead, attn, modulation, r, w_out, final), fresh
+        stale = [[(array, (r,)) for array in stale[1:]] for r in range(requests)]
+        helds = [
+            (qkv(hidden, (r,), modulation, r, score_gain[0], w_qkv, n_query, width), ())
+            for r in range(requests)
+        ]
+
+    def after(r, x, x_lead, held, held_lead, final=None):
+        attn = attend(held, held_lead, n_query, stale[r] + [(text_kv, (0, r))], width)
+        return project_out(x, x_lead, attn, modulation, r, w_out, final)
 
     hop = [(s, s + 1) for s in range(lax.axis_size("section") - 1)]
-    arrived, fresh_first, fresh_last, velocity = [], [], [], []
+    arrived, velocity, lasts = [], [], []
     for r in range(requests):
-        x_next, fresh = layer(r, hidden, (r,))
+        x_next = after(r, hidden, (r,), *helds[r])
         arrived.append(lax.ppermute(x_next, "section", hop))
-        fresh_first.append(fresh)
     for r in range(requests):
-        vel, fresh = layer(r, arrived[r], (), (final_mod, final_weight))
-        velocity.append(vel)
-        fresh_last.append(fresh)
-    fresh = jnp.where(section == 0, jnp.stack(fresh_first), jnp.stack(fresh_last))
+        held = qkv(arrived[r], (), modulation, r, score_gain[0], w_qkv, n_query, width)
+        lasts.append((held, ()))
+        velocity.append(after(r, arrived[r], (), held, (), (final_mod, final_weight)))
+    fresh = jnp.stack(
+        [
+            jnp.where(section == 0, early[lead], late[late_lead])[
+                :, n_query : n_query + 2 * width
+            ]
+            for (early, lead), (late, late_lead) in zip(helds, lasts)
+        ]
+    )
     velocity = jnp.stack(velocity)
     half = latent.shape[1]
     back = lax.ppermute(velocity[:, :half].astype(jnp.bfloat16), "section", [(1, 0)])

time: 380 us -> 375 us (0.987)
  local copies, waits for them, and re-layouts: 23.3 us -> 9.48 us
  Pallas kernels: 341 us -> 351 us
    pallas_call x0 -> x2, Pallas kernels: none -> 42.3 us  [the longest x1 36.7 us: first_qkv(): pl.pallas_call(functools.partial(first_kernel, n, n_query, n_key), grid=(...]
    pallas_call x4 -> x2, Pallas kernels: 54 us -> 27 us  [qkv(): pl.pallas_call(functools.partial(qkv_kernel, n_query, n_key), grid=(pl.cd...]
    concatenate x1 -> x0, local copies, waits for them, and re-layouts: 7.14 us -> none  [on_device(): jnp.concatenate([w[:, :width], jnp.zeros((w.shape[0], n_query - width), w...]
    pallas_call x4, Pallas kernels: 65 us -> 58.8 us  [attend(): pl.pallas_call(functools.partial(attend_kernel, 1 + len(sets)), grid=(pai...]
    slice x2 -> x0, local copies, waits for them, and re-layouts: 5.84 us -> none  [the longest x1 3.2 us: on_device(): w[:, width:]]
    unnamed x26 -> x28, local copies, waits for them, and re-layouts: 8 us -> 7.3 us
  transfers between devices with their start and end apart: 3 -> 3, of which waited for: 1 -> 2; matrix products, arithmetic and copies ran while one was open for 1% -> 1% of each run, Pallas kernels for 18% -> 13%
where the time goes in v4:
time: 375 us; the launch traced here: 374 us
  Pallas kernels  351 us (94%)
  local copies, waits for them, and re-layouts  9.48 us (3%)
  starting transfers between devices  7.22 us (2%)
    pallas_call x1, Pallas kernels, gather(): pl.pallas_call(functools.partial(gather_kernel, n), in_specs=[anywhere] *...  194 us
    pallas_call x4, Pallas kernels, attend(): pl.pallas_call(functools.partial(attend_kernel, 1 + len(sets)), grid=(pai...  58.8 us
    pallas_call x1, Pallas kernels, first_qkv(): pl.pallas_call(functools.partial(first_kernel, n, n_query, n_key), grid=(...  36.7 us
    pallas_call x4, Pallas kernels, project_out(): pl.pallas_call(functools.partial(out_kernel, width), grid=(1,), in_specs=...  28.7 us
    pallas_call x2, Pallas kernels, qkv(): pl.pallas_call(functools.partial(qkv_kernel, n_query, n_key), grid=(pl.cd...  27 us
  transfers between devices with their start and end apart: 3, of which 2 were waited for; matrix products, arithmetic and copies ran while one was open for 1% of the time, Pallas kernels for 13%

profile of v4, /device:TPU:0, one launch (start us, length us, event | category | flops | bytes accessed | tf_op | source)
XLA Modules:
  0.0 374.2 jit_solution(6927705404799126191)
XLA Ops:
  0.6 1.5 copy.15.mod_ref
  2.1 0.0 copy-start.9
  2.1 0.0 copy-start.5
  2.1 5.6 %shard_map.130.w_ref = bf16[608,3840]{1,0:T(8,128)(2,1)} custom-call(bf16[608,3648]{1,0:T(8,128)(2,1)} %bitcast.17), custom_call_target="tpu_custom_call" | custom-call | tf_op jit(solution)/shard_map/pallas_call | solution.py:75
  7.7 0.0 copy-done.9
  7.7 0.6 broadcast_in_dim_tile.2.gain_ref
  8.3 0.0 copy-done.5
  8.3 1.3 copy.16.refs_13_.refs_14_.refs_15_
  9.6 193.8 %shard_map.131 = (bf16[2432,3840]{1,0:T(8,128)(2,1)}, bf16[4,1216,608]{2,1,0:T(8,128)(2,1)}, bf16[3,1,256,2432]{3,2,1,0:T(8,128)(2,1)}) custom-call(bf16[608,3840]{1,0:T(8,128)(2,1)} %shard_map.130.w_ref, bf16[1216,608]{1,0:T(8,128)(2,1)} %bitcast.20, bf16[2,256,2432]{2,1,0:T(8,128)(2,1)} %bitcast.18), custom_call_target="tpu_custom_call" | custom-call | bytes 37355520 | tf_op jit(solution)/shard_map/pallas_call | solution.py:491
  203.4 36.7 %shard_map.132 = (bf16[2,256,3840]{2,1,0:T(8,128)(2,1)}, bf16[4,1216,608]{2,1,0:T(8,128)(2,1)}, bf16[3,1,256,2432]{3,2,1,0:T(8,128)(2,1)}) custom-call(bf16[2,256,2432]{2,1,0:T(8,128)(2,1)} %x_ref.5, f32[1,2,3,2432]{3,2,1,0:T(4,128)} %copy.15.mod_ref, f32[1,128]{1,0:T(1,128)} %broadcast_in_dim_tile.2.gain_ref, ...), custom_call_target="tpu_custom_call", output_to_operand_aliasing={{1}: (5, {})} | custom-call | flops 9563013120 | bytes 37355520 | tf_op jit(solution)/shard_map/pallas_call | solution.py:589
  240.1 14.7 %shard_map.133.attn_ref = bf16[256,1280]{1,0:T(8,128)(2,1)} custom-call(bf16[2,256,3840]{2,1,0:T(8,128)(2,1)} %get-tuple-element.11.refs_0_.refs_1_.refs_2_.refs_3_, bf16[2,256,3840]{2,1,0:T(8,128)(2,1)} %get-tuple-element.11.refs_0_.refs_1_.refs_2_.refs_3_, bf16[2,256,3840]{2,1,0:T(8,128)(2,1)} %get-tuple-element.11.refs_0_.refs_1_.refs_2_.refs_3_, ...), custom_call_target="tpu_custom_call" | custom-call | flops 5867307008 | bytes 5729792 | tf_op jit(solution)/shard_map/pallas_call | solution.py:173
  254.8 6.7 %shard_map.134 = bf16[256,2432]{1,0:T(8,128)(2,1)} custom-call(bf16[2,256,2432]{2,1,0:T(8,128)(2,1)} %x_ref.5, bf16[256,1280]{1,0:T(8,128)(2,1)} %shard_map.133.attn_ref, f32[1,2,3,2432]{3,2,1,0:T(4,128)} %copy.15.mod_ref, bf16[4,1216,608]{2,1,0:T(8,128)(2,1)} %get-tuple-element.13.w_ref), custom_call_target="tpu_custom_call" | custom-call | flops 1514143744 | bytes 9650176 | tf_op jit(solution)/shard_map/pallas_call | solution.py:225
  261.6 3.5 collective-permute-start
  265.1 14.7 %shard_map.136.attn_ref = bf16[256,1280]{1,0:T(8,128)(2,1)} custom-call(bf16[2,256,3840]{2,1,0:T(8,128)(2,1)} %get-tuple-element.11.refs_0_.refs_1_.refs_2_.refs_3_, bf16[2,256,3840]{2,1,0:T(8,128)(2,1)} %get-tuple-element.11.refs_0_.refs_1_.refs_2_.refs_3_, bf16[2,256,3840]{2,1,0:T(8,128)(2,1)} %get-tuple-element.11.refs_0_.refs_1_.refs_2_.refs_3_, ...), custom_call_target="tpu_custom_call" | custom-call | flops 5867307008 | bytes 5729792 | tf_op jit(solution)/shard_map/pallas_call | solution.py:173
  279.8 0.0 copy-start
  279.8 6.8 %shard_map.137 = bf16[256,2432]{1,0:T(8,128)(2,1)} custom-call(bf16[2,256,2432]{2,1,0:T(8,128)(2,1)} %x_ref.5, bf16[256,1280]{1,0:T(8,128)(2,1)} %shard_map.136.attn_ref, f32[1,2,3,2432]{3,2,1,0:T(4,128)} %copy.15.mod_ref, bf16[4,1216,608]{2,1,0:T(8,128)(2,1)} %get-tuple-element.13.w_ref), custom_call_target="tpu_custom_call" | custom-call | flops 1514143744 | bytes 9650176 | tf_op jit(solution)/shard_map/pallas_call | solution.py:225
  286.6 0.0 copy-start.8
  286.6 2.5 collective-permute-start.1
  289.1 0.0 copy-done
  289.1 1.6 slice_bitcast_fusion.1
  290.7 0.0 copy-done.8
  290.7 1.1 copy.30.rest_1_
  291.8 0.9 copy.36
  292.7 0.0 copy-done.10
  292.7 0.3 collective-permute-done.x_ref
  293.0 1.0 copy-done.4
  294.0 13.5 %shard_map.135.refs_0_.refs_1_.refs_2_.refs_3_ = bf16[256,3840]{1,0:T(8,128)(2,1)} custom-call(bf16[256,2432]{1,0:T(8,128)(2,1)} %copy-done.4, f32[1,2,3,2432]{3,2,1,0:T(4,128)} %copy.15.mod_ref, f32[1,128]{1,0:T(1,128)} %broadcast_in_dim_tile.2.gain_ref, bf16[2432,3840]{1,0:T(8,128)(2,1)} %get-tuple-element.9.w_ref), custom_call_target="tpu_custom_call" | custom-call | flops 4781506560 | bytes 21889024 | tf_op jit(solution)/shard_map/pallas_call | solution.py:95
  307.5 14.7 %shard_map.139.attn_ref = bf16[256,1280]{1,0:T(8,128)(2,1)} custom-call(bf16[256,3840]{1,0:T(8,128)(2,1)} %shard_map.135.refs_0_.refs_1_.refs_2_.refs_3_, bf16[256,3840]{1,0:T(8,128)(2,1)} %shard_map.135.refs_0_.refs_1_.refs_2_.refs_3_, bf16[256,3840]{1,0:T(8,128)(2,1)} %shard_map.135.refs_0_.refs_1_.refs_2_.refs_3_, ...), custom_call_target="tpu_custom_call" | custom-call | flops 5867307008 | bytes 5729792 | tf_op jit(solution)/shard_map/pallas_call | solution.py:173
  322.2 0.0 collective-permute-done.1.x_ref
  322.3 13.5 %shard_map.138.refs_0_.refs_1_.refs_2_.refs_3_ = bf16[256,3840]{1,0:T(8,128)(2,1)} custom-call(bf16[256,2432]{1,0:T(8,128)(2,1)} %collective-permute-done.1.x_ref, f32[1,2,3,2432]{3,2,1,0:T(4,128)} %copy.15.mod_ref, f32[1,128]{1,0:T(1,128)} %broadcast_in_dim_tile.2.gain_ref, bf16[2432,3840]{1,0:T(8,128)(2,1)} %get-tuple-element.9.w_ref), custom_call_target="tpu_custom_call" | custom-call | flops 4781506560 | bytes 21889024 | tf_op jit(solution)/shard_map/pallas_call | solution.py:95
  335.8 14.7 %shard_map.141.attn_ref = bf16[256,1280]{1,0:T(8,128)(2,1)} custom-call(bf16[256,3840]{1,0:T(8,128)(2,1)} %shard_map.138.refs_0_.refs_1_.refs_2_.refs_3_, bf16[256,3840]{1,0:T(8,128)(2,1)} %shard_map.138.refs_0_.refs_1_.refs_2_.refs_3_, bf16[256,3840]{1,0:T(8,128)(2,1)} %shard_map.138.refs_0_.refs_1_.refs_2_.refs_3_, ...), custom_call_target="tpu_custom_call" | custom-call | flops 5867307008 | bytes 5729792 | tf_op jit(solution)/shard_map/pallas_call | solution.py:173
  350.5 7.5 %shard_map.140 = f32[256,64]{1,0:T(8,128)} custom-call(bf16[256,2432]{1,0:T(8,128)(2,1)} %copy-done.4, bf16[256,1280]{1,0:T(8,128)(2,1)} %shard_map.139.attn_ref, f32[1,2,3,2432]{3,2,1,0:T(4,128)} %copy.15.mod_ref, bf16[4,1216,608]{2,1,0:T(8,128)(2,1)} %get-tuple-element.13.w_ref, f32[2,2,2432]{2,1,0:T(2,128)} %rest_0_.3, bf16[2432,64]{1,0:T(8,128)(2,1)} %copy.30.rest_1_), custom_call_target="tpu_custom_call" | custom-call | flops 1514143744 | bytes 9650176 | tf_op jit(solution)/shard_map/pallas_call | solution.py:225
  357.9 7.6 %shard_map.142 = f32[256,64]{1,0:T(8,128)} custom-call(bf16[256,2432]{1,0:T(8,128)(2,1)} %collective-permute-done.1.x_ref, bf16[256,1280]{1,0:T(8,128)(2,1)} %shard_map.141.attn_ref, f32[1,2,3,2432]{3,2,1,0:T(4,128)} %copy.15.mod_ref, bf16[4,1216,608]{2,1,0:T(8,128)(2,1)} %get-tuple-element.13.w_ref, f32[2,2,2432]{2,1,0:T(2,128)} %rest_0_.3, ...), custom_call_target="tpu_custom_call" | custom-call | flops 1514143744 | bytes 9650176 | tf_op jit(solution)/shard_map/pallas_call | solution.py:225
  365.6 0.0 copy-done.6
  365.6 1.0 fusion.3
  366.6 1.3 collective-permute-start.2
  367.9 0.0 copy-done.1
  367.9 0.0 copy-done.3
  367.9 0.1 fusion.1
  368.0 0.0 copy-done.2
  368.0 0.2 fusion
  368.2 0.0 copy-start.7
  368.2 1.7 maximum_bitcast_fusion
  369.9 2.8 collective-permute-done.2
  372.7 0.0 copy-done.7
  372.7 0.1 multiply_subtract_fusion
  372.8 0.7 copy.38
  373.5 0.7 copy.39
  (9 shorter events, 0.0 us)
Async XLA Ops:
  2.1 5.6 %copy-start.9 = (f32[1,64]{1,0:T(1,128)S(1)}, f32[1,64]{1,0:T(1,128)}, u32[]{:S(2)}) copy-start(f32[1,64]{1,0:T(1,128)} %param.15) | copy-start | bytes 772
  2.1 6.2 %copy-start.5 = (bf16[1,2,154,2432]{3,1,2,0:T(2,128)(2,1)S(1)}, bf16[1,2,154,2432]{3,1,2,0:T(2,128)(2,1)}, u32[]{:S(2)}) copy-start(bf16[1,2,154,2432]{3,1,2,0:T(2,128)(2,1)} %param.12) | copy-start | bytes 4494340
  261.6 31.4 %collective-permute-start = (bf16[256,2432]{1,0:T(8,128)(2,1)}, bf16[256,2432]{1,0:T(8,128)(2,1)S(1)}, u32[]{:S(2)}, u32[]{:S(2)}) collective-permute-start(bf16[256,2432]{1,0:T(8,128)(2,1)} %shard_map.134), channel_id=1, source_target_pairs={{0,16},{1,17},{2,18},{3,19},{4,20},{5,21},{6,22},{7,23},{8,24},{9,... | collective-permute-start | bytes 3735560 | tf_op jit(solution)/shard_map/ppermute | solution.py:691
  279.8 9.3 %copy-start = (bf16[2,256,3840]{2,1,0:T(8,128)(2,1)S(1)}, bf16[2,256,3840]{2,1,0:T(8,128)(2,1)}, u32[]{:S(2)}) copy-start(bf16[2,256,3840]{2,1,0:T(8,128)(2,1)} %get-tuple-element.11.refs_0_.refs_1_.refs_2_.refs_3_) | copy-start | bytes 11796484
  286.6 4.1 %copy-start.8 = (bf16[2432,64]{0,1:T(8,128)(2,1)S(1)}, bf16[2432,64]{0,1:T(8,128)(2,1)}, u32[]{:S(2)}) copy-start(bf16[2432,64]{0,1:T(8,128)(2,1)} %param.19) | copy-start | bytes 933892
  286.6 6.1 %copy-start.10 = (s32[2]{0:T(128)S(1)}, s32[2]{0:T(128)}, u32[]{:S(2)}) copy-start(s32[2]{0:T(128)} %param.21) | copy-start | bytes 28
  286.6 35.6 %collective-permute-start.1 = (bf16[256,2432]{1,0:T(8,128)(2,1)}, bf16[256,2432]{1,0:T(8,128)(2,1)}, u32[]{:S(2)}, u32[]{:S(2)}) collective-permute-start(bf16[256,2432]{1,0:T(8,128)(2,1)} %shard_map.137), channel_id=1, source_target_pairs={{0,16},{1,17},{2,18},{3,19},{4,20},{5,21},{6,22},{7,23},{8,24},{9,... | collective-permute-start | bytes 3735560 | tf_op jit(solution)/shard_map/ppermute | solution.py:691
  293.0 1.0 copy-start.4
  357.9 7.6 %copy-start.6 = (f32[256,64]{1,0:T(8,128)S(1)}, f32[256,64]{1,0:T(8,128)}, u32[]{:S(2)}) copy-start(f32[256,64]{1,0:T(8,128)} %shard_map.140) | copy-start | bytes 196612
  357.9 9.9 %copy-start.1 = (bf16[256,3840]{1,0:T(8,128)(2,1)S(1)}, bf16[256,3840]{1,0:T(8,128)(2,1)}, u32[]{:S(2)}) copy-start(bf16[256,3840]{1,0:T(8,128)(2,1)} %shard_map.135.refs_0_.refs_1_.refs_2_.refs_3_) | copy-start | bytes 5898244
  357.9 9.9 %copy-start.3 = (bf16[256,3840]{1,0:T(8,128)(2,1)S(1)}, bf16[256,3840]{1,0:T(8,128)(2,1)}, u32[]{:S(2)}) copy-start(bf16[256,3840]{1,0:T(8,128)(2,1)} %get-tuple-element.20) | copy-start | bytes 5898244
  365.6 2.5 copy-start.2
  366.6 6.2 %collective-permute-start.2 = (bf16[2,128,64]{2,1,0:T(8,128)(2,1)S(1)}, bf16[2,128,64]{2,1,0:T(8,128)(2,1)S(1)}, u32[]{:S(2)}, u32[]{:S(2)}) collective-permute-start(bf16[2,128,64]{2,1,0:T(8,128)(2,1)S(1)} %fusion.3), channel_id=1, source_target_pairs={{16,0},{17,1},{18,2},{19,3},{20,4},{21,5},{22,6},{23,7},{24,8},{25... | collective-permute-start | bytes 98312 | tf_op jit(solution)/shard_map/ppermute | solution.py:706
  368.2 4.5 %copy-start.7 = (f32[256,64]{1,0:T(8,128)S(1)}, f32[256,64]{1,0:T(8,128)}, u32[]{:S(2)}) copy-start(f32[256,64]{1,0:T(8,128)} %shard_map.142) | copy-start | bytes 196612

commit v5 on v4

--- a/solution.py
+++ b/solution.py
@@ -241,9 +241,16 @@
 LAG = 3
 
 
-def row_chunks(rows):
-    first = pl.cdiv(rows // 16, 2) * 16
-    return ((0, first), (first, rows - first))
+def row_pieces(rows, shared):
+    if not shared:
+        return ((0, rows // 2, rows // 2, True),)
+    own = rows * 27 // 64 // 32 * 32
+    half = own // 2
+    return (
+        (0, rows - own, half, True),
+        (half, rows - half, half, True),
+        (own, own, rows - 2 * own, False),
+    )
 
 
 def greet(n, me, patch):
@@ -271,90 +278,14 @@
     return me - t if way == 0 else me + t
 
 
-def out_copies(wo_ref, wo_all, os_, or_):
+def relay(w_ref, spot, zs, zr, hs, hr):
     me = lax.axis_index("shard")
     patch = lax.axis_index("patch")
-    o_rows = wo_all.shape[1] // 2
-
-    def o_copy(way, t, sending):
+
+    def z_copy(way, t, k, sending):
         b = shard_block(me, way, t if sending else t + 1)
-        half = pl.ds(pl.multiple_of((patch % 2) * o_rows, 16), o_rows)
-        dst = wo_all.at[b, half]
-        src = wo_ref.at[half] if sending and t == 0 else dst
-        return pltpu.make_async_remote_copy(
-            src_ref=src,
-            dst_ref=dst,
-            send_sem=os_.at[0, way, t],
-            recv_sem=or_.at[0, way, t],
-            device_id={"shard": me + 1 if way == 0 else me - 1},
-            device_id_type=MESH,
-        )
-
-    def o_hop(way, t, sending):
-        parity = patch % 2 if sending else 1 - patch % 2
-        place = wo_all.at[
-            shard_block(me, way, t + 1), pl.ds(pl.multiple_of(parity * o_rows, 16), o_rows)
-        ]
-        return pltpu.make_async_remote_copy(
-            src_ref=place,
-            dst_ref=place,
-            send_sem=os_.at[1, way, t],
-            recv_sem=or_.at[1, way, t],
-            device_id={"patch": patch ^ 1},
-            device_id_type=MESH,
-        )
-
-    return o_copy, o_hop
-
-
-def stale_copies(stale_ref, stale_all, ss, sr, first=0):
-    patch = lax.axis_index("patch")
-
-    def s_copy(kind, r):
-        return pltpu.make_async_remote_copy(
-            src_ref=stale_all.at[0, r] if kind == 2 else stale_ref.at[r + first],
-            dst_ref=stale_all.at[kind, r],
-            send_sem=ss.at[kind, r],
-            recv_sem=sr.at[kind, r],
-            device_id={"patch": patch ^ (2 if kind == 0 else 1)},
-            device_id_type=MESH,
-        )
-
-    return s_copy
-
-
-def gather_kernel(
-    n, w_ref, wo_ref, stale_ref, w_all, wo_all, stale_all, own, zs, zr, hs, hr, os_, or_, ss, sr
-):
-    me = lax.axis_index("shard")
-    patch = lax.axis_index("patch")
-    rows, columns = w_ref.shape
-    half_rows, half_columns = rows // 2, columns // 2
-    chunks = row_chunks(half_rows)
-    has_left, has_right = me > 0, me < n - 1
-
-    greet(n, me, patch)
-
-    def spot(ref, base, quarter, k):
-        start, size = chunks[k]
-        return ref.at[
-            pl.ds(pl.multiple_of(base + (quarter // 2) * half_rows + start, 16), size),
-            pl.ds(pl.multiple_of((quarter % 2) * half_columns, LANES), half_columns),
-        ]
-
-    def block(way, t):
-        return me - t if way == 0 else me + t
-
-    def incoming(way, t):
-        return (me - 1 - t >= 0) if way == 0 else (me + 1 + t < n)
-
-    def ahead(way):
-        return has_right if way == 0 else has_left
-
-    def z_copy(way, t, k, sending):
-        b = block(way, t if sending else t + 1)
-        dst = spot(w_all, b * rows, patch, k)
-        src = spot(w_ref, 0, patch, k) if sending and t == 0 else dst
+        dst = spot(None, b, patch, k)
+        src = spot(w_ref, None, patch, k) if sending and t == 0 else dst
         return pltpu.make_async_remote_copy(
             src_ref=src,
             dst_ref=dst,
@@ -367,7 +298,7 @@
     def hop(kind, way, t, k, sending):
         to = 2 if kind == 0 else 1
         held = patch ^ 2 if kind == 2 else patch
-        place = spot(w_all, block(way, t + 1) * rows, held if sending else held ^ to, k)
+        place = spot(None, shard_block(me, way, t + 1), held if sending else held ^ to, k)
         return pltpu.make_async_remote_copy(
             src_ref=place,
             dst_ref=place,
@@ -377,136 +308,147 @@
             device_id_type=MESH,
         )
 
-    o_copy, o_hop = out_copies(wo_ref, wo_all, os_, or_)
-
-    s_copy = stale_copies(stale_ref, stale_all, ss, sr)
-
-    for way in range(2):
-
-        @pl.when(ahead(way))
-        def _(way=way):
-            for k in range(len(chunks)):
-                z_copy(way, 0, k, True).start()
-
-    s_copy(0, 0).start()
-    s_copy(1, 0).start()
+    return z_copy, hop
+
+
+class Gather:
+    def __init__(self, n, pieces, z_copy, hop):
+        self.n, self.pieces, self.z_copy, self.hop = n, pieces, z_copy, hop
+        self.me = lax.axis_index("shard")
+        self.items = [
+            (way, t, k) for t in range(n - 1) for k in range(len(pieces)) for way in range(2)
+        ]
+
+    def incoming(self, way, t):
+        return (self.me - 1 - t >= 0) if way == 0 else (self.me + 1 + t < self.n)
+
+    def ahead(self, way):
+        return self.me < self.n - 1 if way == 0 else self.me > 0
+
+    def begin(self):
+        for way in range(2):
+
+            @pl.when(self.ahead(way))
+            def _(way=way):
+                for k in range(len(self.pieces)):
+                    self.z_copy(way, 0, k, True).start()
+
+    def arrive(self, way, t, k):
+        @pl.when(self.incoming(way, t))
+        def _():
+            self.z_copy(way, t, k, False).wait_recv()
+            if t + 1 < self.n - 1:
+
+                @pl.when(self.ahead(way))
+                def _():
+                    self.z_copy(way, t + 1, k, True).start()
+
+            if self.pieces[k][3]:
+                self.hop(0, way, t, k, True).start()
+            self.hop(1, way, t, k, True).start()
+
+    def pass_on(self, way, t, k):
+        if self.pieces[k][3]:
+
+            @pl.when(self.incoming(way, t))
+            def _():
+                self.hop(0, way, t, k, False).wait_recv()
+                self.hop(2, way, t, k, True).start()
+
+    def finish(self):
+        for way, t, k in self.items:
+            kinds = (0, 1, 2) if self.pieces[k][3] else (1,)
+
+            @pl.when(self.incoming(way, t))
+            def _(way=way, t=t, k=k, kinds=kinds):
+                for kind in kinds:
+                    self.hop(kind, way, t, k, True).wait_send()
+                for kind in kinds:
+                    if kind:
+                        self.hop(kind, way, t, k, False).wait_recv()
+
+            sends = self.incoming(way, t - 1) if t > 0 else True
+
+            @pl.when(jnp.logical_and(self.ahead(way), sends))
+            def _(way=way, t=t, k=k):
+                self.z_copy(way, t, k, True).wait_send()
+
+
+def gather_kernel(n, w_ref, stale_ref, w_all, stale_all, beside, own, zs, zr, hs, hr, ss, sr):
+    me = lax.axis_index("shard")
+    patch = lax.axis_index("patch")
+    rows, columns = w_ref.shape
+    half_columns = columns // 2
+    pieces = row_pieces(rows, True)
+    greet(n, me, patch)
+
+    def spot(ref, shard, quarter, k):
+        early, late, size, _ = pieces[k]
+        base = 0 if shard is None else shard * rows
+        start = base + jnp.where(quarter // 2 == 0, early, late)
+        return (w_all if ref is None else ref).at[
+            pl.ds(pl.multiple_of(start, 16), size),
+            pl.ds(pl.multiple_of((quarter % 2) * half_columns, LANES), half_columns),
+        ]
+
+    def s_copy(kind):
+        src = (stale_ref.at[0], stale_ref.at[0], stale_all.at[0], stale_ref.at[pl.ds(1, others)])
+        return pltpu.make_async_remote_copy(
+            src_ref=src[kind],
+            dst_ref=beside if kind == 3 else stale_all.at[kind],
+            send_sem=ss.at[kind],
+            recv_sem=sr.at[kind],
+            device_id={"patch": patch ^ (2 if kind == 0 else 1)},
+            device_id_type=MESH,
+        )
+
+    others = beside.shape[0]
+    steps = Gather(n, pieces, *relay(w_ref, spot, zs, zr, hs, hr))
+    steps.begin()
+    for kind in (0, 1, 3):
+        s_copy(kind).start()
     own_w = pltpu.make_async_copy(
-        w_ref, w_all.at[pl.ds(pl.multiple_of(me * rows, 16), rows)], own.at[0]
-    )
-    own_o = pltpu.make_async_copy(wo_ref, wo_all.at[me], own.at[1])
+        w_ref, w_all.at[pl.ds(pl.multiple_of(me * rows, 16), rows)], own
+    )
     own_w.start()
-    own_o.start()
-
-    items = [
-        (way, t, k) for t in range(n - 1) for k in range(len(chunks)) for way in range(2)
-    ]
-
-    def pass_on(way, t, k):
-        @pl.when(incoming(way, t))
-        def _():
-            hop(0, way, t, k, False).wait_recv()
-            hop(2, way, t, k, True).start()
-
-    for place, (way, t, k) in enumerate(items):
-
-        @pl.when(incoming(way, t))
-        def _(way=way, t=t, k=k):
-            z_copy(way, t, k, False).wait_recv()
-            if t + 1 < n - 1:
-
-                @pl.when(ahead(way))
-                def _():
-                    z_copy(way, t + 1, k, True).start()
-
-            hop(0, way, t, k, True).start()
-            hop(1, way, t, k, True).start()
-
-        if place >= 2 * LAG:
-            pass_on(*items[place - 2 * LAG])
-        if t == max(n - 3, 0) and k == len(chunks) - 1:
-
-            @pl.when(ahead(way))
-            def _(way=way):
-                o_copy(way, 0, True).start()
-
-    s_copy(0, 0).wait_recv()
-    s_copy(2, 0).start()
-    left = items[max(len(items) - 2 * LAG, 0) :]
-    for t in range(n - 2):
-        for way in range(2):
-
-            @pl.when(incoming(way, t))
-            def _(way=way, t=t):
-                o_copy(way, t, False).wait_recv()
-                if t + 1 < n - 2:
-
-                    @pl.when(ahead(way))
-                    def _():
-                        o_copy(way, t + 1, True).start()
-
-                o_hop(way, t, True).start()
-
-        share = pl.cdiv(len(left), n - 2)
-        for item in left[t * share : (t + 1) * share]:
-            pass_on(*item)
-
-    for way, t, k in items:
-
-        @pl.when(incoming(way, t))
-        def _(way=way, t=t, k=k):
-            for kind in range(3):
-                hop(kind, way, t, k, True).wait_send()
-            for kind in (1, 2):
-                hop(kind, way, t, k, False).wait_recv()
-
-        sends = incoming(way, t - 1) if t > 0 else True
-
-        @pl.when(jnp.logical_and(ahead(way), sends))
-        def _(way=way, t=t, k=k):
-            z_copy(way, t, k, True).wait_send()
-
-        if k == 0 and t < n - 2:
-
-            @pl.when(incoming(way, t))
-            def _(way=way, t=t):
-                o_hop(way, t, True).wait_send()
-                o_hop(way, t, False).wait_recv()
-
-            @pl.when(jnp.logical_and(ahead(way), sends))
-            def _(way=way, t=t):
-                o_copy(way, t, True).wait_send()
-
-    for kind in range(3):
-        s_copy(kind, 0).wait_send()
-    for kind in (1, 2):
-        s_copy(kind, 0).wait_recv()
+    lag = 2 * LAG
+    for place, item in enumerate(steps.items):
+        steps.arrive(*item)
+        if place >= lag:
+            steps.pass_on(*steps.items[place - lag])
+    s_copy(0).wait_recv()
+    s_copy(2).start()
+    for item in steps.items[max(len(steps.items) - lag, 0) :]:
+        steps.pass_on(*item)
+    steps.finish()
+    for kind in range(4):
+        s_copy(kind).wait_send()
+    for kind in (1, 2, 3):
+        s_copy(kind).wait_recv()
     own_w.wait()
-    own_o.wait()
-
-
-def gather(w, w_out, stale, n):
+
+
+def gather(w, stale, n):
     rows, columns = w.shape
     anywhere = pl.BlockSpec(memory_space=pl.ANY)
     dma = pltpu.SemaphoreType.DMA
     return pl.pallas_call(
         functools.partial(gather_kernel, n),
-        in_specs=[anywhere] * 3,
+        in_specs=[anywhere] * 2,
         out_specs=[anywhere] * 3,
         out_shape=[
             jax.ShapeDtypeStruct((n * rows, columns), w.dtype),
-            jax.ShapeDtypeStruct((n,) + w_out.shape, w_out.dtype),
-            jax.ShapeDtypeStruct((3, 1) + stale.shape[1:], stale.dtype),
+            jax.ShapeDtypeStruct((3,) + stale.shape[1:], stale.dtype),
+            jax.ShapeDtypeStruct((stale.shape[0] - 1,) + stale.shape[1:], stale.dtype),
         ],
         scratch_shapes=[
-            dma((2,)),
-            dma((2, n - 1, 2)),
-            dma((2, n - 1, 2)),
-            dma((3, 2, n - 1, 2)),
-            dma((3, 2, n - 1, 2)),
-            dma((2, 2, n - 2)),
-            dma((2, 2, n - 2)),
-            dma((3, 1)),
-            dma((3, 1)),
+            dma,
+            dma((2, n - 1, 3)),
+            dma((2, n - 1, 3)),
+            dma((3, 2, n - 1, 3)),
+            dma((3, 2, n - 1, 3)),
+            dma((4,)),
+            dma((4,)),
         ],
         compiler_params=pltpu.CompilerParams(
             collective_id=0, has_side_effects=True, vmem_limit_bytes=56 * 1024 * 1024
@@ -514,107 +456,82 @@
         cost_estimate=pl.CostEstimate(
             flops=0, bytes_accessed=4 * n * rows * columns, transcendentals=0
         ),
-    )(w, w_out, stale)
+    )(w, stale)
 
 
 def first_kernel(
-    n, n_query, n_key, x_ref, mod_ref, gain_ref, w_ref, stale_ref, wo_in, out_ref, wo_all,
-    stale_all, normed_ref, os_, or_, ss, sr,
+    n, total, n_query, n_key, x_ref, mod_ref, gain_ref, w_ref, wo_ref, out_ref, wo_all,
+    normed_ref, own, zs, zr, hs, hr,
 ):
     step = pl.program_id(1)
     at = pl.program_id(0) * pl.num_programs(1) + step
-    last = pl.num_programs(0) * pl.num_programs(1) - 1
     me = lax.axis_index("shard")
-    o_copy, o_hop = out_copies(None, wo_all, os_, or_)
-    s_copy = stale_copies(stale_ref, stale_all, ss, sr, 1)
-    others = stale_all.shape[1]
-    ends = (me == n - 1, me == 0)
-    before = (me == n - 2, me == 1)
+    pieces = row_pieces(wo_ref.shape[0], False)
+
+    def spot(ref, shard, quarter, k):
+        place = wo_all.at[shard] if ref is None else ref
+        size = pieces[k][2] // 2
+        return place.at[pl.ds(pl.multiple_of(quarter * size, 16), size)]
+
+    steps = Gather(n, pieces, *relay(wo_ref, spot, zs, zr, hs, hr))
+    own_o = pltpu.make_async_copy(wo_ref, wo_all.at[me], own)
 
     @pl.when(at == 0)
     def _():
         greet(n, me, lax.axis_index("patch"))
-        for way in range(2):
-
-            @pl.when(before[way])
-            def _(way=way):
-                o_copy(way, n - 2, True).start()
-
-        for r in range(others):
-            s_copy(0, r).start()
-            s_copy(1, r).start()
+        steps.begin()
+        own_o.start()
 
     qkv_step(step, n_query, n_key, x_ref, mod_ref, gain_ref, w_ref, out_ref, normed_ref)
 
-    @pl.when(at == last - 1)
+    hooks = [min(total * (t + 1) // (n - 1), total - 2) for t in range(n - 1)]
+    for t in range(n - 1):
+
+        @pl.when(at == hooks[t])
+        def _(t=t):
+            for way in range(2):
+                steps.arrive(way, t, 0)
+                if t > 0:
+                    steps.pass_on(way, t - 1, 0)
+
+    @pl.when(at == total - 1)
     def _():
         for way in range(2):
-
-            @pl.when(ends[way])
-            def _(way=way):
-                o_copy(way, n - 2, False).wait_recv()
-                o_hop(way, n - 2, True).start()
-
-        for r in range(others):
-            s_copy(0, r).wait_recv()
-            s_copy(2, r).start()
-
-    @pl.when(at == last)
-    def _():
-        for way in range(2):
-
-            @pl.when(before[way])
-            def _(way=way):
-                o_copy(way, n - 2, True).wait_send()
-
-            @pl.when(ends[way])
-            def _(way=way):
-                o_hop(way, n - 2, True).wait_send()
-                o_hop(way, n - 2, False).wait_recv()
-
-        for r in range(others):
-            for kind in range(3):
-                s_copy(kind, r).wait_send()
-            for kind in (1, 2):
-                s_copy(kind, r).wait_recv()
-
-
-def first_qkv(x, modulation, gain, w, stale, wo_all, n, n_query, n_key):
+            steps.pass_on(way, n - 2, 0)
+        steps.finish()
+        own_o.wait()
+
+
+def first_qkv(x, modulation, gain, w, w_out, n, n_query, n_key):
     requests, rows, depth = x.shape
     columns = w.shape[1]
     gain_row = jnp.tile(gain / math.sqrt(HEAD), LANES // HEAD)[None]
     anywhere = pl.BlockSpec(memory_space=pl.ANY)
     dma = pltpu.SemaphoreType.DMA
-    others = requests - 1
+    blocks = pl.cdiv(columns, BLOCK)
     return pl.pallas_call(
-        functools.partial(first_kernel, n, n_query, n_key),
-        grid=(requests, pl.cdiv(columns, BLOCK)),
+        functools.partial(first_kernel, n, requests * blocks, n_query, n_key),
+        grid=(requests, blocks),
         in_specs=[
             pl.BlockSpec((None, rows, depth), lambda r, i: (r, 0, 0)),
             pl.BlockSpec((None, None, 3, depth), lambda r, i: (0, r, 0, 0)),
             pl.BlockSpec((1, LANES), lambda r, i: (0, 0)),
             pl.BlockSpec((depth, BLOCK), lambda r, i: (0, i)),
             anywhere,
-            anywhere,
         ],
-        out_specs=[
-            pl.BlockSpec((None, rows, BLOCK), lambda r, i: (r, 0, i)),
-            anywhere,
-            anywhere,
-        ],
+        out_specs=[pl.BlockSpec((None, rows, BLOCK), lambda r, i: (r, 0, i)), anywhere],
         out_shape=[
             jax.ShapeDtypeStruct((requests, rows, columns), jnp.bfloat16),
-            jax.ShapeDtypeStruct(wo_all.shape, wo_all.dtype),
-            jax.ShapeDtypeStruct((3, others) + stale.shape[1:], stale.dtype),
+            jax.ShapeDtypeStruct((n,) + w_out.shape, w_out.dtype),
         ],
         scratch_shapes=[
             pltpu.VMEM((rows, depth), jnp.bfloat16),
-            dma((2, 2, n - 1)),
-            dma((2, 2, n - 1)),
-            dma((3, others)),
-            dma((3, others)),
+            dma,
+            dma((2, n - 1, 1)),
+            dma((2, n - 1, 1)),
+            dma((3, 2, n - 1, 1)),
+            dma((3, 2, n - 1, 1)),
         ],
-        input_output_aliases={5: 1},
         compiler_params=pltpu.CompilerParams(
             collective_id=1, has_side_effects=True, vmem_limit_bytes=56 * 1024 * 1024
         ),
@@ -623,7 +540,7 @@
             bytes_accessed=2 * depth * columns * requests,
             transcendentals=0,
         ),
-    )(x, modulation, gain_row, w, stale, wo_all)
+    )(x, modulation, gain_row, w, w_out)
 
 
 def on_device(
@@ -650,16 +567,16 @@
     columns = pl.cdiv(n_query + 2 * width, 2 * LANES) * 2 * LANES
     w = qkv_weight[0]
     packed = pack(w, width, n_query, columns)
-    if patches == 4 and shards > 2 and requests > 1 and w.shape[0] % 32 == 0 and width % 32 == 0:
-        w_qkv, w_out, stale_first = gather(packed, out_weight[0], stale_kv[0], shards)
-        held, w_out, stale_rest = first_qkv(
-            hidden, modulation, score_gain[0], w_qkv, stale_kv[0], w_out, shards, n_query, width
+    if patches == 4 and shards > 2 and requests > 1 and w.shape[0] % 32 == 0 and width % 64 == 0:
+        w_qkv, stale_first, beside = gather(packed, stale_kv[0], shards)
+        w_qkv, later = lax.optimization_barrier((w_qkv, stale_kv[0, 1:]))
+        across = lax.ppermute(later, "patch", [(p, p ^ 2) for p in range(patches)])
+        held, w_out = first_qkv(
+            hidden, modulation, score_gain[0], w_qkv, out_weight[0], shards, n_query, width
         )
         helds = [(held, (r,)) for r in range(requests)]
-        stale = [
-            [(stale_rest, (i, r - 1)) if r else (stale_first, (i, 0)) for i in range(3)]
-            for r in range(requests)
-        ]
+        pending = (across, beside)
+        stale = [[(stale_first, (i,)) for i in range(3)]]
     else:
         share = w.shape[0] // patches
         mine = lax.dynamic_slice_in_dim(packed, patch * share, share, 0)
@@ -675,6 +592,7 @@
             stale = stale + [lax.ppermute(array, "patch", pairs) for array in stale]
             step //= 2
         stale = [[(array, (r,)) for array in stale[1:]] for r in range(requests)]
+        pending = None
         helds = [
             (qkv(hidden, (r,), modulation, r, score_gain[0], w_qkv, n_query, width), ())
             for r in range(requests)
@@ -682,6 +600,13 @@
 
     def after(r, x, x_lead, held, held_lead, final=None):
         attn = attend(held, held_lead, n_query, stale[r] + [(text_kv, (0, r))], width)
+        if len(stale) < requests:
+            attn, across = lax.optimization_barrier((attn, pending[0]))
+            both = lax.ppermute(across, "patch", [(p, p ^ 1) for p in range(patches)])
+            stale.extend(
+                [(array, (i,)) for array in (across, pending[1], both)]
+                for i in range(requests - 1)
+            )
         return project_out(x, x_lead, attn, modulation, r, w_out, final)
 
     hop = [(s, s + 1) for s in range(lax.axis_size("section") - 1)]
@@ -689,6 +614,7 @@
     for r in range(requests):
         x_next = after(r, hidden, (r,), *helds[r])
         arrived.append(lax.ppermute(x_next, "section", hop))
+    arrived = [lax.optimization_barrier((x, x_next))[0] for x in arrived[:-1]] + arrived[-1:]
     for r in range(requests):
         held = qkv(arrived[r], (), modulation, r, score_gain[0], w_qkv, n_query, width)
         lasts.append((held, ()))

time: 375 us -> 349 us (0.931)
  Pallas kernels: 351 us -> 321 us
    pallas_call x1, Pallas kernels: 194 us -> 147 us  [gather(): pl.pallas_call(functools.partial(gather_kernel, n), in_specs=[anywhere] *...]
    pallas_call x1, Pallas kernels: 36.7 us -> 53.6 us  [first_qkv(): pl.pallas_call(functools.partial(first_kernel, n, requests * blocks, n_qu...]
  transfers between devices with their start and end apart: 3 -> 5, of which waited for: 2 -> 1; matrix products, arithmetic and copies ran while one was open for 1% -> 2% of each run, Pallas kernels for 13% -> 38%
where the time goes in v5:
time: 349 us; the launch traced here: 348 us
  Pallas kernels  321 us (92%)
  local copies, waits for them, and re-layouts  10.7 us (3%)
  starting transfers between devices  9.43 us (3%)
    pallas_call x1, Pallas kernels, gather(): pl.pallas_call(functools.partial(gather_kernel, n), in_specs=[anywhere] *...  147 us
    pallas_call x4, Pallas kernels, attend(): pl.pallas_call(functools.partial(attend_kernel, 1 + len(sets)), grid=(pai...  58.8 us
    pallas_call x1, Pallas kernels, first_qkv(): pl.pallas_call(functools.partial(first_kernel, n, requests * blocks, n_qu...  53.6 us
    pallas_call x4, Pallas kernels, project_out(): pl.pallas_call(functools.partial(out_kernel, width), grid=(1,), in_specs=...  28.8 us
    pallas_call x2, Pallas kernels, qkv(): pl.pallas_call(functools.partial(qkv_kernel, n_query, n_key), grid=(pl.cd...  27 us
  transfers between devices with their start and end apart: 5, of which 1 were waited for; matrix products, arithmetic and copies ran while one was open for 2% of the time, Pallas kernels for 38%

profile of v5, /device:TPU:0, one launch (start us, length us, event | category | flops | bytes accessed | tf_op | source)
XLA Modules:
  0.0 347.9 jit_solution(18270456882317506643)
XLA Ops:
  0.6 0.0 copy-start.5
  0.6 5.7 %shard_map.130.w_ref = bf16[608,3840]{1,0:T(8,128)(2,1)} custom-call(bf16[608,3648]{1,0:T(8,128)(2,1)} %bitcast.20), custom_call_target="tpu_custom_call" | custom-call | tf_op jit(solution)/shard_map/pallas_call | solution.py:75
  6.3 0.0 copy-done.5
  6.3 1.1 slice_bitcast_fusion.2
  7.4 146.9 %shard_map.131 = (bf16[2432,3840]{1,0:T(8,128)(2,1)}, bf16[3,256,2432]{2,1,0:T(8,128)(2,1)}, bf16[1,256,2432]{2,1,0:T(8,128)(2,1)}) custom-call(bf16[608,3840]{1,0:T(8,128)(2,1)} %shard_map.130.w_ref, bf16[2,256,2432]{2,1,0:T(8,128)(2,1)} %bitcast.19), custom_call_target="tpu_custom_call" | custom-call | bytes 37355520 | tf_op jit(solution)/shard_map/pallas_call | solution.py:435
  154.4 1.6 collective-permute-start
  156.0 0.0 copy-done.14
  156.0 0.7 copy.14.mod_ref
  156.6 0.6 broadcast_in_dim_tile.2.gain_ref
  157.2 1.3 copy.15.refs_13_.refs_14_.refs_15_
  158.5 53.6 %shard_map.132 = (bf16[2,256,3840]{2,1,0:T(8,128)(2,1)}, bf16[4,1216,608]{2,1,0:T(8,128)(2,1)}) custom-call(bf16[2,256,2432]{2,1,0:T(8,128)(2,1)} %x_ref.5, f32[1,2,3,2432]{3,2,1,0:T(4,128)} %copy.14.mod_ref, f32[1,128]{1,0:T(1,128)} %broadcast_in_dim_tile.2.gain_ref, bf16[2432,3840]{1,0:T(8,128)(2,1)} %get-tuple-element.14.w_ref, bf16[1216,608]{1,0:T(8,128)(2,1)} %bitcast.25), custom_call_target="tpu_custom_call" | custom-call | flops 9563013120 | bytes 37355520 | tf_op jit(solution)/shard_map/pallas_call | solution.py:512
  212.1 14.7 %shard_map.133.attn_ref = bf16[256,1280]{1,0:T(8,128)(2,1)} custom-call(bf16[2,256,3840]{2,1,0:T(8,128)(2,1)} %get-tuple-element.15.refs_0_.refs_1_.refs_2_.refs_3_, bf16[2,256,3840]{2,1,0:T(8,128)(2,1)} %get-tuple-element.15.refs_0_.refs_1_.refs_2_.refs_3_, bf16[2,256,3840]{2,1,0:T(8,128)(2,1)} %get-tuple-element.15.refs_0_.refs_1_.refs_2_.refs_3_, ...), custom_call_target="tpu_custom_call" | custom-call | flops 5867307008 | bytes 5729792 | tf_op jit(solution)/shard_map/pallas_call | solution.py:173
  226.9 0.0 collective-permute-done.refs_4_.refs_5_.refs_6_
  226.9 0.4 collective-permute-start.2
  227.3 6.9 %shard_map.134 = bf16[256,2432]{1,0:T(8,128)(2,1)} custom-call(bf16[2,256,2432]{2,1,0:T(8,128)(2,1)} %x_ref.5, bf16[256,1280]{1,0:T(8,128)(2,1)} %shard_map.133.attn_ref, f32[1,2,3,2432]{3,2,1,0:T(4,128)} %copy.14.mod_ref, bf16[4,1216,608]{2,1,0:T(8,128)(2,1)} %get-tuple-element.19.w_ref), custom_call_target="tpu_custom_call" | custom-call | flops 1514143744 | bytes 9650176 | tf_op jit(solution)/shard_map/pallas_call | solution.py:225
  234.2 0.0 copy-start.16
  234.2 4.6 %collective-permute-start.1 = (bf16[256,2432]{1,0:T(8,128)(2,1)}, bf16[256,2432]{1,0:T(8,128)(2,1)}, u32[]{:S(2)}, u32[]{:S(2)}) collective-permute-start(bf16[256,2432]{1,0:T(8,128)(2,1)} %shard_map.134), channel_id=1, source_target_pairs={{0,16},{1,17},{2,18},{3,19},{4,20},{5,21},{6,22},{7,23},{8,24},{9,... | collective-permute-start | bytes 3735560 | tf_op jit(solution)/shard_map/ppermute | solution.py:616
  238.8 2.2 slice_bitcast_fusion.1
  241.0 1.1 copy.29.rest_1_
  242.1 0.1 copy.35
  242.2 0.0 collective-permute-done.2.refs_10_.refs_11_.refs_12_
  242.3 0.0 copy-start.4
  242.3 1.0 copy-done.4
  243.3 14.7 %shard_map.135.attn_ref = bf16[256,1280]{1,0:T(8,128)(2,1)} custom-call(bf16[2,256,3840]{2,1,0:T(8,128)(2,1)} %get-tuple-element.15.refs_0_.refs_1_.refs_2_.refs_3_, bf16[2,256,3840]{2,1,0:T(8,128)(2,1)} %get-tuple-element.15.refs_0_.refs_1_.refs_2_.refs_3_, bf16[2,256,3840]{2,1,0:T(8,128)(2,1)} %get-tuple-element.15.refs_0_.refs_1_.refs_2_.refs_3_, ...), custom_call_target="tpu_custom_call" | custom-call | flops 5867307008 | bytes 5729792 | tf_op jit(solution)/shard_map/pallas_call | solution.py:173
  258.0 6.7 %shard_map.136 = bf16[256,2432]{1,0:T(8,128)(2,1)} custom-call(bf16[2,256,2432]{2,1,0:T(8,128)(2,1)} %x_ref.5, bf16[256,1280]{1,0:T(8,128)(2,1)} %shard_map.135.attn_ref, f32[1,2,3,2432]{3,2,1,0:T(4,128)} %copy.14.mod_ref, bf16[4,1216,608]{2,1,0:T(8,128)(2,1)} %get-tuple-element.19.w_ref), custom_call_target="tpu_custom_call" | custom-call | flops 1514143744 | bytes 9650176 | tf_op jit(solution)/shard_map/pallas_call | solution.py:225
  264.7 1.5 collective-permute-start.3
  266.3 0.0 collective-permute-done.1.x_ref
  266.3 13.6 %shard_map.137.refs_0_.refs_1_.refs_2_.refs_3_ = bf16[256,3840]{1,0:T(8,128)(2,1)} custom-call(bf16[256,2432]{1,0:T(8,128)(2,1)} %collective-permute-done.1.x_ref, f32[1,2,3,2432]{3,2,1,0:T(4,128)} %copy.14.mod_ref, f32[1,128]{1,0:T(1,128)} %broadcast_in_dim_tile.2.gain_ref, bf16[2432,3840]{1,0:T(8,128)(2,1)} %get-tuple-element.14.w_ref), custom_call_target="tpu_custom_call" | custom-call | flops 4781506560 | bytes 21889024 | tf_op jit(solution)/shard_map/pallas_call | solution.py:95
  279.8 14.7 %shard_map.139.attn_ref = bf16[256,1280]{1,0:T(8,128)(2,1)} custom-call(bf16[256,3840]{1,0:T(8,128)(2,1)} %shard_map.137.refs_0_.refs_1_.refs_2_.refs_3_, bf16[256,3840]{1,0:T(8,128)(2,1)} %shard_map.137.refs_0_.refs_1_.refs_2_.refs_3_, bf16[256,3840]{1,0:T(8,128)(2,1)} %shard_map.137.refs_0_.refs_1_.refs_2_.refs_3_, ...), custom_call_target="tpu_custom_call" | custom-call | flops 5867307008 | bytes 5729792 | tf_op jit(solution)/shard_map/pallas_call | solution.py:173
  294.6 0.0 copy-start.7
  294.6 7.6 %shard_map.140 = f32[256,64]{1,0:T(8,128)} custom-call(bf16[256,2432]{1,0:T(8,128)(2,1)} %collective-permute-done.1.x_ref, bf16[256,1280]{1,0:T(8,128)(2,1)} %shard_map.139.attn_ref, f32[1,2,3,2432]{3,2,1,0:T(4,128)} %copy.14.mod_ref, bf16[4,1216,608]{2,1,0:T(8,128)(2,1)} %get-tuple-element.19.w_ref, f32[2,2,2432]{2,1,0:T(2,128)} %rest_0_.3, ...), custom_call_target="tpu_custom_call" | custom-call | flops 1514143744 | bytes 9650176 | tf_op jit(solution)/shard_map/pallas_call | solution.py:225
  302.2 0.1 fusion.1
  302.3 0.0 collective-permute-done.3.x_ref
  302.3 1.1 copy-done.8
  303.5 13.5 %shard_map.138.refs_0_.refs_1_.refs_2_.refs_3_ = bf16[256,3840]{1,0:T(8,128)(2,1)} custom-call(bf16[256,2432]{1,0:T(8,128)(2,1)} %copy-done.8, f32[1,2,3,2432]{3,2,1,0:T(4,128)} %copy.14.mod_ref, f32[1,128]{1,0:T(1,128)} %broadcast_in_dim_tile.2.gain_ref, bf16[2432,3840]{1,0:T(8,128)(2,1)} %get-tuple-element.14.w_ref), custom_call_target="tpu_custom_call" | custom-call | flops 4781506560 | bytes 21889024 | tf_op jit(solution)/shard_map/pallas_call | solution.py:95
  316.9 14.7 %shard_map.141.attn_ref = bf16[256,1280]{1,0:T(8,128)(2,1)} custom-call(bf16[256,3840]{1,0:T(8,128)(2,1)} %shard_map.138.refs_0_.refs_1_.refs_2_.refs_3_, bf16[256,3840]{1,0:T(8,128)(2,1)} %shard_map.138.refs_0_.refs_1_.refs_2_.refs_3_, bf16[256,3840]{1,0:T(8,128)(2,1)} %shard_map.138.refs_0_.refs_1_.refs_2_.refs_3_, ...), custom_call_target="tpu_custom_call" | custom-call | flops 5867307008 | bytes 5729792 | tf_op jit(solution)/shard_map/pallas_call | solution.py:173
  331.6 0.0 copy-start.10
  331.7 0.0 copy-start.1
  331.7 7.6 %shard_map.142 = f32[256,64]{1,0:T(8,128)} custom-call(bf16[256,2432]{1,0:T(8,128)(2,1)} %copy-done.8, bf16[256,1280]{1,0:T(8,128)(2,1)} %shard_map.141.attn_ref, f32[1,2,3,2432]{3,2,1,0:T(4,128)} %copy.14.mod_ref, bf16[4,1216,608]{2,1,0:T(8,128)(2,1)} %get-tuple-element.19.w_ref, f32[2,2,2432]{2,1,0:T(2,128)} %rest_0_.3, bf16[2432,64]{1,0:T(8,128)(2,1)} %copy.29.rest_1_), custom_call_target="tpu_custom_call" | custom-call | flops 1514143744 | bytes 9650176 | tf_op jit(solution)/shard_map/pallas_call | solution.py:225
  339.3 0.9 fusion.3
  340.2 1.3 collective-permute-start.4
  341.5 0.1 fusion
  341.6 0.0 copy-start.11
  341.6 1.7 maximum_bitcast_fusion
  343.3 3.0 collective-permute-done.4
  346.3 0.1 multiply_subtract_fusion
  346.4 0.7 copy.37
  347.1 0.7 copy.38
  (26 shorter events, 0.1 us)
Async XLA Ops:
  0.6 5.7 %copy-start.5 = (bf16[1,2,256,2432]{3,2,1,0:T(8,128)(2,1)S(1)}, bf16[1,2,256,2432]{3,2,1,0:T(8,128)(2,1)}, u32[]{:S(2)}) copy-start(bf16[1,2,256,2432]{3,2,1,0:T(8,128)(2,1)} %param.13) | copy-start | bytes 7471108
  7.4 148.5 %copy-start.14 = (f32[1,2,3,2432]{3,1,2,0:T(2,128)S(1)}, f32[1,2,3,2432]{3,1,2,0:T(2,128)}, u32[]{:S(2)}) copy-start(f32[1,2,3,2432]{3,1,2,0:T(2,128)} %param.14) | copy-start | bytes 175108
  7.4 149.2 %copy-start.15 = (f32[1,64]{1,0:T(1,128)S(1)}, f32[1,64]{1,0:T(1,128)}, u32[]{:S(2)}) copy-start(f32[1,64]{1,0:T(1,128)} %param.15) | copy-start | bytes 772
  7.4 149.8 %copy-start.9 = (bf16[1,2,154,2432]{3,1,2,0:T(2,128)(2,1)S(1)}, bf16[1,2,154,2432]{3,1,2,0:T(2,128)(2,1)}, u32[]{:S(2)}) copy-start(bf16[1,2,154,2432]{3,1,2,0:T(2,128)(2,1)} %param.12) | copy-start | bytes 4494340
  154.4 72.5 %collective-permute-start = (bf16[1,256,2432]{2,1,0:T(8,128)(2,1)}, bf16[1,256,2432]{2,1,0:T(8,128)(2,1)S(1)}, u32[]{:S(2)}, u32[]{:S(2)}) collective-permute-start(bf16[1,256,2432]{2,1,0:T(8,128)(2,1)} %slice_bitcast_fusion.2), channel_id=1, source_target_pairs={{0,8},{4,12},{8,0},{12,4},{1,9},{5,13},{9,1},{13,5},{2,10},{6,14},... | collective-permute-start | bytes 3735560 | tf_op jit(solution)/shard_map/ppermute | solution.py:573
  226.9 7.3 %copy-start.3 = (bf16[1,256,2432]{2,1,0:T(8,128)(2,1)}, bf16[1,256,2432]{2,1,0:T(8,128)(2,1)S(1)}, u32[]{:S(2)}) copy-start(bf16[1,256,2432]{2,1,0:T(8,128)(2,1)S(1)} %collective-permute-done.refs_4_.refs_5_.refs_6_) | copy-start | bytes 3735556
  226.9 15.4 %collective-permute-start.2 = (bf16[1,256,2432]{2,1,0:T(8,128)(2,1)S(1)}, bf16[1,256,2432]{2,1,0:T(8,128)(2,1)S(1)}, u32[]{:S(2)}, u32[]{:S(2)}) collective-permute-start(bf16[1,256,2432]{2,1,0:T(8,128)(2,1)S(1)} %collective-permute-done.refs_4_.refs_5_.refs_6_), channel_id=1, source_target_pairs={{0,4},{4,0},{8,12},{12,8},{1,5},{5,1},{9,13},{13,9},{2,6},{6,2},{1... | collective-permute-start | bytes 3735560 | tf_op jit(solution)/shard_map/ppermute | solution.py:605
  227.3 11.5 %copy-start = (bf16[2,256,3840]{2,1,0:T(8,128)(2,1)S(1)}, bf16[2,256,3840]{2,1,0:T(8,128)(2,1)}, u32[]{:S(2)}) copy-start(bf16[2,256,3840]{2,1,0:T(8,128)(2,1)} %get-tuple-element.15.refs_0_.refs_1_.refs_2_.refs_3_) | copy-start | bytes 11796484
  234.2 6.8 %copy-start.12 = (bf16[2432,64]{0,1:T(8,128)(2,1)S(1)}, bf16[2432,64]{0,1:T(8,128)(2,1)}, u32[]{:S(2)}) copy-start(bf16[2432,64]{0,1:T(8,128)(2,1)} %param.19) | copy-start | bytes 933892
  234.2 7.9 %copy-start.13 = (f32[2,128,64]{1,2,0:T(8,128)S(1)}, f32[2,128,64]{1,2,0:T(8,128)}, u32[]{:S(2)}) copy-start(f32[2,128,64]{1,2,0:T(8,128)} %param.20) | copy-start | bytes 196612
  234.2 8.0 %copy-start.16 = (s32[2]{0:T(128)S(1)}, s32[2]{0:T(128)}, u32[]{:S(2)}) copy-start(s32[2]{0:T(128)} %param.21) | copy-start | bytes 28
  234.2 32.0 %collective-permute-start.1 = (bf16[256,2432]{1,0:T(8,128)(2,1)}, bf16[256,2432]{1,0:T(8,128)(2,1)}, u32[]{:S(2)}, u32[]{:S(2)}) collective-permute-start(bf16[256,2432]{1,0:T(8,128)(2,1)} %shard_map.134), channel_id=1, source_target_pairs={{0,16},{1,17},{2,18},{3,19},{4,20},{5,21},{6,22},{7,23},{8,24},{9,... | collective-permute-start | bytes 3735560 | tf_op jit(solution)/shard_map/ppermute | solution.py:616
  242.3 1.0 copy-start.4
  264.7 37.6 %collective-permute-start.3 = (bf16[256,2432]{1,0:T(8,128)(2,1)}, bf16[256,2432]{1,0:T(8,128)(2,1)S(1)}, u32[]{:S(2)}, u32[]{:S(2)}) collective-permute-start(bf16[256,2432]{1,0:T(8,128)(2,1)} %shard_map.136), channel_id=1, source_target_pairs={{0,16},{1,17},{2,18},{3,19},{4,20},{5,21},{6,22},{7,23},{8,24},{9,... | collective-permute-start | bytes 3735560 | tf_op jit(solution)/shard_map/ppermute | solution.py:616
  294.5 7.6 %copy-start.2 = (bf16[256,3840]{1,0:T(8,128)(2,1)S(1)}, bf16[256,3840]{1,0:T(8,128)(2,1)}, u32[]{:S(2)}) copy-start(bf16[256,3840]{1,0:T(8,128)(2,1)} %shard_map.137.refs_0_.refs_1_.refs_2_.refs_3_) | copy-start | bytes 5898244
  294.6 7.6 %copy-start.7 = (bf16[256,3840]{1,0:T(8,128)(2,1)S(1)}, bf16[256,3840]{1,0:T(8,128)(2,1)}, u32[]{:S(2)}) copy-start(bf16[256,3840]{1,0:T(8,128)(2,1)} %get-tuple-element.28) | copy-start | bytes 5898244
  302.3 1.1 copy-start.8
  331.6 7.7 %copy-start.10 = (f32[256,64]{1,0:T(8,128)S(1)}, f32[256,64]{1,0:T(8,128)}, u32[]{:S(2)}) copy-start(f32[256,64]{1,0:T(8,128)} %shard_map.140) | copy-start | bytes 196612
  331.7 9.8 %copy-start.1 = (bf16[256,3840]{1,0:T(8,128)(2,1)S(1)}, bf16[256,3840]{1,0:T(8,128)(2,1)}, u32[]{:S(2)}) copy-start(bf16[256,3840]{1,0:T(8,128)(2,1)} %shard_map.138.refs_0_.refs_1_.refs_2_.refs_3_) | copy-start | bytes 5898244
  331.7 9.8 %copy-start.6 = (bf16[256,3840]{1,0:T(8,128)(2,1)S(1)}, bf16[256,3840]{1,0:T(8,128)(2,1)}, u32[]{:S(2)}) copy-start(bf16[256,3840]{1,0:T(8,128)(2,1)} %get-tuple-element.29) | copy-start | bytes 5898244
  340.2 6.2 %collective-permute-start.4 = (bf16[2,128,64]{2,1,0:T(8,128)(2,1)S(1)}, bf16[2,128,64]{2,1,0:T(8,128)(2,1)S(1)}, u32[]{:S(2)}, u32[]{:S(2)}) collective-permute-start(bf16[2,128,64]{2,1,0:T(8,128)(2,1)S(1)} %fusion.3), channel_id=1, source_target_pairs={{16,0},{17,1},{18,2},{19,3},{20,4},{21,5},{22,6},{23,7},{24,8},{25... | collective-permute-start | bytes 98312 | tf_op jit(solution)/shard_map/ppermute | solution.py:632
  341.6 4.7 %copy-start.11 = (f32[256,64]{1,0:T(8,128)S(1)}, f32[256,64]{1,0:T(8,128)}, u32[]{:S(2)}) copy-start(f32[256,64]{1,0:T(8,128)} %shard_map.142) | copy-start | bytes 196612

commit v6 on v5

--- a/solution.py
+++ b/solution.py
@@ -61,25 +61,6 @@
         out_ref[:, low : low + LANES] = jnp.where(col < n_query + n_key, scaled, part).astype(
             jnp.bfloat16
         )
-
-
-def pack_kernel(width, n_query, w_ref, out_ref):
-    out_ref[...] = jnp.zeros_like(out_ref)
-    out_ref[:, :width] = w_ref[:, :width]
-    out_ref[:, n_query : n_query + 2 * width] = w_ref[:, width:]
-
-
-def pack(w, width, n_query, columns):
-    rows = w.shape[0]
-    block = min(rows, 160)
-    return pl.pallas_call(
-        functools.partial(pack_kernel, width, n_query),
-        grid=(pl.cdiv(rows, block),),
-        in_specs=[pl.BlockSpec((block, w.shape[1]), lambda i: (i, 0))],
-        out_specs=pl.BlockSpec((block, columns), lambda i: (i, 0)),
-        out_shape=jax.ShapeDtypeStruct((rows, columns), w.dtype),
-        compiler_params=PARAMS,
-    )(w)
 
 
 def picked(array, lead, shape, index):
@@ -238,19 +219,6 @@
 
 
 MESH = pl.DeviceIdType.MESH
-LAG = 3
-
-
-def row_pieces(rows, shared):
-    if not shared:
-        return ((0, rows // 2, rows // 2, True),)
-    own = rows * 27 // 64 // 32 * 32
-    half = own // 2
-    return (
-        (0, rows - own, half, True),
-        (half, rows - half, half, True),
-        (own, own, rows - 2 * own, False),
-    )
 
 
 def greet(n, me, patch):
@@ -374,173 +342,82 @@
                 self.z_copy(way, t, k, True).wait_send()
 
 
-def gather_kernel(n, w_ref, stale_ref, w_all, stale_all, beside, own, zs, zr, hs, hr, ss, sr):
+def gather_kernel(n, wo_ref, stale_ref, wo_all, stale_all, own, zs, zr, hs, hr, ss, sr):
     me = lax.axis_index("shard")
     patch = lax.axis_index("patch")
-    rows, columns = w_ref.shape
-    half_columns = columns // 2
-    pieces = row_pieces(rows, True)
+    requests = stale_ref.shape[0]
+    size = wo_ref.shape[0] // 4
     greet(n, me, patch)
 
     def spot(ref, shard, quarter, k):
-        early, late, size, _ = pieces[k]
-        base = 0 if shard is None else shard * rows
-        start = base + jnp.where(quarter // 2 == 0, early, late)
-        return (w_all if ref is None else ref).at[
-            pl.ds(pl.multiple_of(start, 16), size),
-            pl.ds(pl.multiple_of((quarter % 2) * half_columns, LANES), half_columns),
-        ]
-
-    def s_copy(kind):
-        src = (stale_ref.at[0], stale_ref.at[0], stale_all.at[0], stale_ref.at[pl.ds(1, others)])
+        place = wo_all.at[shard] if ref is None else ref
+        return place.at[pl.ds(pl.multiple_of(quarter * size, 16), size)]
+
+    def s_copy(kind, r):
         return pltpu.make_async_remote_copy(
-            src_ref=src[kind],
-            dst_ref=beside if kind == 3 else stale_all.at[kind],
-            send_sem=ss.at[kind],
-            recv_sem=sr.at[kind],
+            src_ref=stale_all.at[0, r] if kind == 2 else stale_ref.at[r],
+            dst_ref=stale_all.at[kind, r],
+            send_sem=ss.at[kind, r],
+            recv_sem=sr.at[kind, r],
             device_id={"patch": patch ^ (2 if kind == 0 else 1)},
             device_id_type=MESH,
         )
 
-    others = beside.shape[0]
-    steps = Gather(n, pieces, *relay(w_ref, spot, zs, zr, hs, hr))
+    steps = Gather(n, ((0, 0, size, True),), *relay(wo_ref, spot, zs, zr, hs, hr))
     steps.begin()
-    for kind in (0, 1, 3):
-        s_copy(kind).start()
-    own_w = pltpu.make_async_copy(
-        w_ref, w_all.at[pl.ds(pl.multiple_of(me * rows, 16), rows)], own
-    )
-    own_w.start()
-    lag = 2 * LAG
-    for place, item in enumerate(steps.items):
+    s_copy(0, 0).start()
+    for r in range(requests):
+        s_copy(1, r).start()
+    own_o = pltpu.make_async_copy(wo_ref, wo_all.at[me], own)
+    own_o.start()
+    for item in steps.items:
         steps.arrive(*item)
-        if place >= lag:
-            steps.pass_on(*steps.items[place - lag])
-    s_copy(0).wait_recv()
-    s_copy(2).start()
-    for item in steps.items[max(len(steps.items) - lag, 0) :]:
+    for r in range(1, requests):
+        s_copy(0, r).start()
+    s_copy(0, 0).wait_recv()
+    s_copy(2, 0).start()
+    for item in steps.items:
         steps.pass_on(*item)
+    for r in range(1, requests):
+        s_copy(0, r).wait_recv()
+        s_copy(2, r).start()
     steps.finish()
-    for kind in range(4):
-        s_copy(kind).wait_send()
-    for kind in (1, 2, 3):
-        s_copy(kind).wait_recv()
-    own_w.wait()
-
-
-def gather(w, stale, n):
-    rows, columns = w.shape
+    for r in range(requests):
+        for kind in range(3):
+            s_copy(kind, r).wait_send()
+        for kind in (1, 2):
+            s_copy(kind, r).wait_recv()
+    own_o.wait()
+
+
+def gather(w_out, stale, n):
     anywhere = pl.BlockSpec(memory_space=pl.ANY)
     dma = pltpu.SemaphoreType.DMA
+    requests = stale.shape[0]
     return pl.pallas_call(
         functools.partial(gather_kernel, n),
         in_specs=[anywhere] * 2,
-        out_specs=[anywhere] * 3,
+        out_specs=[anywhere] * 2,
         out_shape=[
-            jax.ShapeDtypeStruct((n * rows, columns), w.dtype),
-            jax.ShapeDtypeStruct((3,) + stale.shape[1:], stale.dtype),
-            jax.ShapeDtypeStruct((stale.shape[0] - 1,) + stale.shape[1:], stale.dtype),
+            jax.ShapeDtypeStruct((n,) + w_out.shape, w_out.dtype),
+            jax.ShapeDtypeStruct((3,) + stale.shape, stale.dtype),
         ],
         scratch_shapes=[
             dma,
-            dma((2, n - 1, 3)),
-            dma((2, n - 1, 3)),
-            dma((3, 2, n - 1, 3)),
-            dma((3, 2, n - 1, 3)),
-            dma((4,)),
-            dma((4,)),
+            dma((2, n - 1, 1)),
+            dma((2, n - 1, 1)),
+            dma((3, 2, n - 1, 1)),
+            dma((3, 2, n - 1, 1)),
+            dma((3, requests)),
+            dma((3, requests)),
         ],
         compiler_params=pltpu.CompilerParams(
             collective_id=0, has_side_effects=True, vmem_limit_bytes=56 * 1024 * 1024
         ),
         cost_estimate=pl.CostEstimate(
-            flops=0, bytes_accessed=4 * n * rows * columns, transcendentals=0
+            flops=0, bytes_accessed=200 * 1024 * 1024, transcendentals=0
         ),
-    )(w, stale)
-
-
-def first_kernel(
-    n, total, n_query, n_key, x_ref, mod_ref, gain_ref, w_ref, wo_ref, out_ref, wo_all,
-    normed_ref, own, zs, zr, hs, hr,
-):
-    step = pl.program_id(1)
-    at = pl.program_id(0) * pl.num_programs(1) + step
-    me = lax.axis_index("shard")
-    pieces = row_pieces(wo_ref.shape[0], False)
-
-    def spot(ref, shard, quarter, k):
-        place = wo_all.at[shard] if ref is None else ref
-        size = pieces[k][2] // 2
-        return place.at[pl.ds(pl.multiple_of(quarter * size, 16), size)]
-
-    steps = Gather(n, pieces, *relay(wo_ref, spot, zs, zr, hs, hr))
-    own_o = pltpu.make_async_copy(wo_ref, wo_all.at[me], own)
-
-    @pl.when(at == 0)
-    def _():
-        greet(n, me, lax.axis_index("patch"))
-        steps.begin()
-        own_o.start()
-
-    qkv_step(step, n_query, n_key, x_ref, mod_ref, gain_ref, w_ref, out_ref, normed_ref)
-
-    hooks = [min(total * (t + 1) // (n - 1), total - 2) for t in range(n - 1)]
-    for t in range(n - 1):
-
-        @pl.when(at == hooks[t])
-        def _(t=t):
-            for way in range(2):
-                steps.arrive(way, t, 0)
-                if t > 0:
-                    steps.pass_on(way, t - 1, 0)
-
-    @pl.when(at == total - 1)
-    def _():
-        for way in range(2):
-            steps.pass_on(way, n - 2, 0)
-        steps.finish()
-        own_o.wait()
-
-
-def first_qkv(x, modulation, gain, w, w_out, n, n_query, n_key):
-    requests, rows, depth = x.shape
-    columns = w.shape[1]
-    gain_row = jnp.tile(gain / math.sqrt(HEAD), LANES // HEAD)[None]
-    anywhere = pl.BlockSpec(memory_space=pl.ANY)
-    dma = pltpu.SemaphoreType.DMA
-    blocks = pl.cdiv(columns, BLOCK)
-    return pl.pallas_call(
-        functools.partial(first_kernel, n, requests * blocks, n_query, n_key),
-        grid=(requests, blocks),
-        in_specs=[
-            pl.BlockSpec((None, rows, depth), lambda r, i: (r, 0, 0)),
-            pl.BlockSpec((None, None, 3, depth), lambda r, i: (0, r, 0, 0)),
-            pl.BlockSpec((1, LANES), lambda r, i: (0, 0)),
-            pl.BlockSpec((depth, BLOCK), lambda r, i: (0, i)),
-            anywhere,
-        ],
-        out_specs=[pl.BlockSpec((None, rows, BLOCK), lambda r, i: (r, 0, i)), anywhere],
-        out_shape=[
-            jax.ShapeDtypeStruct((requests, rows, columns), jnp.bfloat16),
-            jax.ShapeDtypeStruct((n,) + w_out.shape, w_out.dtype),
-        ],
-        scratch_shapes=[
-            pltpu.VMEM((rows, depth), jnp.bfloat16),
-            dma,
-            dma((2, n - 1, 1)),
-            dma((2, n - 1, 1)),
-            dma((3, 2, n - 1, 1)),
-            dma((3, 2, n - 1, 1)),
-        ],
-        compiler_params=pltpu.CompilerParams(
-            collective_id=1, has_side_effects=True, vmem_limit_bytes=56 * 1024 * 1024
-        ),
-        cost_estimate=pl.CostEstimate(
-            flops=2 * requests * rows * depth * columns,
-            bytes_accessed=2 * depth * columns * requests,
-            transcendentals=0,
-        ),
-    )(x, modulation, gain_row, w, w_out)
+    )(w_out, stale)
 
 
 def on_device(
@@ -564,67 +441,44 @@
     width = out_weight.shape[1]
     n_query = pl.cdiv(width, LANES) * LANES
 
-    columns = pl.cdiv(n_query + 2 * width, 2 * LANES) * 2 * LANES
     w = qkv_weight[0]
-    packed = pack(w, width, n_query, columns)
-    if patches == 4 and shards > 2 and requests > 1 and w.shape[0] % 32 == 0 and width % 64 == 0:
-        w_qkv, stale_first, beside = gather(packed, stale_kv[0], shards)
-        w_qkv, later = lax.optimization_barrier((w_qkv, stale_kv[0, 1:]))
-        across = lax.ppermute(later, "patch", [(p, p ^ 2) for p in range(patches)])
-        held, w_out = first_qkv(
-            hidden, modulation, score_gain[0], w_qkv, out_weight[0], shards, n_query, width
-        )
-        helds = [(held, (r,)) for r in range(requests)]
-        pending = (across, beside)
-        stale = [[(stale_first, (i,)) for i in range(3)]]
-    else:
-        share = w.shape[0] // patches
-        mine = lax.dynamic_slice_in_dim(packed, patch * share, share, 0)
-        w_qkv = lax.all_gather(mine, ("shard", "patch"), axis=0, tiled=True)
-        share = width // patches
-        mine = lax.dynamic_slice_in_dim(out_weight[0], patch * share, share, 0)
-        w_out = lax.all_gather(mine, ("shard", "patch"), axis=0, tiled=True)
-        w_out = w_out.reshape(shards, width, out_weight.shape[2])
-        stale = [stale_kv[0]]
-        step = patches // 2
-        while step >= 1:
-            pairs = [(p, p ^ step) for p in range(patches)]
-            stale = stale + [lax.ppermute(array, "patch", pairs) for array in stale]
-            step //= 2
-        stale = [[(array, (r,)) for array in stale[1:]] for r in range(requests)]
-        pending = None
-        helds = [
-            (qkv(hidden, (r,), modulation, r, score_gain[0], w_qkv, n_query, width), ())
-            for r in range(requests)
-        ]
-
-    def after(r, x, x_lead, held, held_lead, final=None):
-        attn = attend(held, held_lead, n_query, stale[r] + [(text_kv, (0, r))], width)
-        if len(stale) < requests:
-            attn, across = lax.optimization_barrier((attn, pending[0]))
-            both = lax.ppermute(across, "patch", [(p, p ^ 1) for p in range(patches)])
-            stale.extend(
-                [(array, (i,)) for array in (across, pending[1], both)]
-                for i in range(requests - 1)
-            )
-        return project_out(x, x_lead, attn, modulation, r, w_out, final)
+    share = w.shape[0] // patches
+    mine = lax.dynamic_slice_in_dim(w, patch * share, share, 0)
+    packed = jnp.concatenate(
+        [
+            mine[:, :width],
+            jnp.zeros((share, n_query - width), w.dtype),
+            mine[:, width:],
+        ],
+        1,
+    )
+    w_qkv = lax.all_gather(packed, ("shard", "patch"), axis=0, tiled=True)
+    w_out, stale = gather(out_weight[0], stale_kv[0], shards)
+
+    def layer(r, x, x_lead, final=None):
+        held = qkv(x, x_lead, modulation, r, score_gain[0], w_qkv, n_query, width)
+        sets = [(stale, (i, r)) for i in range(3)] + [(text_kv, (0, r))]
+        attn = attend(held, (), n_query, sets, width)
+        return project_out(x, x_lead, attn, modulation, r, w_out, final), held
 
     hop = [(s, s + 1) for s in range(lax.axis_size("section") - 1)]
-    arrived, velocity, lasts = [], [], []
+    arrived, velocity, firsts, lasts = [], [], [], []
     for r in range(requests):
-        x_next = after(r, hidden, (r,), *helds[r])
+        x_next, held = layer(r, hidden, (r,))
+        firsts.append(held)
         arrived.append(lax.ppermute(x_next, "section", hop))
     arrived = [lax.optimization_barrier((x, x_next))[0] for x in arrived[:-1]] + arrived[-1:]
     for r in range(requests):
-        held = qkv(arrived[r], (), modulation, r, score_gain[0], w_qkv, n_query, width)
-        lasts.append((held, ()))
-        velocity.append(after(r, arrived[r], (), held, (), (final_mod, final_weight)))
+        x = arrived[r]
+        if velocity:
+            x = lax.optimization_barrier((x, velocity[-1]))[0]
+        vel, held = layer(r, x, (), (final_mod, final_weight))
+        lasts.append(held)
+        velocity.append(vel)
     fresh = jnp.stack(
         [
-            jnp.where(section == 0, early[lead], late[late_lead])[
-                :, n_query : n_query + 2 * width
-            ]
-            for (early, lead), (late, late_lead) in zip(helds, lasts)
+            jnp.where(section == 0, early, late)[:, n_query : n_query + 2 * width]
+            for early, late in zip(firsts, lasts)
         ]
     )
     velocity = jnp.stack(velocity)

time: 349 us -> 351 us (level)
  Pallas kernels: 321 us -> 305 us
  between operations: 0.88 us -> 14.2 us
  waiting for transfers between devices: 3 us -> 8.96 us
    pallas_call x2 -> x0, Pallas kernels: 59.3 us -> none  [the longest x1 53.6 us: first_qkv(): pl.pallas_call(functools.partial(first_kernel, n, requests * blocks, n_qu...]
    pallas_call x2 -> x4, Pallas kernels: 27 us -> 53.3 us  [qkv(): pl.pallas_call(functools.partial(qkv_kernel, n_query, n_key), grid=(pl.cd...]
    pallas_call x1, Pallas kernels: 147 us -> 164 us  [gather(): pl.pallas_call(functools.partial(gather_kernel, n), in_specs=[anywhere] *...]
    all_gather x0 -> x1, waiting for transfers between devices: none -> 5.77 us  [on_device(): w_qkv = lax.all_gather(packed, ('shard', 'patch'), axis=0, tiled=True)]
    unnamed x40 -> x38, local copies, waits for them, and re-layouts: 6.77 us -> 8.1 us
  transfers between devices with their start and end apart: 5 -> 4, of which waited for: 1 -> 2; matrix products, arithmetic and copies ran while one was open for 2% -> 2% of each run, Pallas kernels for 38% -> 67%
where the time goes in v6:
time: 351 us; the launch traced here: 350 us
  Pallas kernels  305 us (87%)
  between operations  14.2 us (4%)
  local copies, waits for them, and re-layouts  12.2 us (3%)
  waiting for transfers between devices  8.96 us (3%)
  starting transfers between devices  6.68 us (2%)
  other arithmetic  3.53 us (1%)
    pallas_call x1, Pallas kernels, gather(): pl.pallas_call(functools.partial(gather_kernel, n), in_specs=[anywhere] *...  164 us
    pallas_call x4, Pallas kernels, attend(): pl.pallas_call(functools.partial(attend_kernel, 1 + len(sets)), grid=(pai...  59 us
    pallas_call x4, Pallas kernels, qkv(): pl.pallas_call(functools.partial(qkv_kernel, n_query, n_key), grid=(pl.cd...  53.3 us
    pallas_call x4, Pallas kernels, project_out(): pl.pallas_call(functools.partial(out_kernel, width), grid=(1,), in_specs=...  28.4 us
    unnamed x38, local copies, waits for them, and re-layouts  8.1 us
  transfers between devices with their start and end apart: 4, of which 2 were waited for; matrix products, arithmetic and copies ran while one was open for 2% of the time, Pallas kernels for 67%

profile of v6, /device:TPU:0, one launch (start us, length us, event | category | flops | bytes accessed | tf_op | source)
XLA Modules:
  0.0 350.5 jit_solution(17039295906979545591)
XLA Ops:
  7.2 0.0 all-gather.2.cloned.1.call-start
  7.2 1.3 dynamic-slice_bitcast_fusion
  8.6 0.3 slice.26
  8.9 0.0 copy-start.11
  8.9 0.0 copy-start.14
  8.9 0.0 copy-start.6
  8.9 1.9 concatenate.3
  10.8 0.0 all-gather.2.cloned.1.call-update
  10.8 0.7 copy.14.mod_ref
  11.5 0.6 broadcast_in_dim_tile.2.gain_ref
  12.1 1.3 copy.15.refs_13_.refs_14_.refs_15_
  13.4 1.1 copy.29.rest_1_
  14.5 0.1 copy.36
  14.6 164.2 %shard_map.131 = (bf16[4,1216,608]{2,1,0:T(8,128)(2,1)}, bf16[3,2,256,2432]{3,2,1,0:T(8,128)(2,1)}) custom-call(bf16[1216,608]{1,0:T(8,128)(2,1)} %bitcast.15, bf16[2,256,2432]{2,1,0:T(8,128)(2,1)} %bitcast.14), custom_call_target="tpu_custom_call" | custom-call | bytes 209715200 | tf_op jit(solution)/shard_map/pallas_call | solution.py:397
  178.8 5.8 %all-gather.2.cloned.1.call-done.w_ref = bf16[2432,3712]{1,0:T(8,128)(2,1)} async-done(((bf16[152,3712]{1,0:T(8,128)(2,1)}), bf16[2432,3712]{1,0:T(8,128)(2,1)}) %all-gather.2.cloned.1.call-update) | async-done | bytes 18055184 | tf_op jit(solution)/shard_map/all_gather | solution.py:455
  184.5 13.3 %shard_map.130.refs_0_.refs_1_.refs_2_.refs_3_ = bf16[256,3712]{1,0:T(8,128)(2,1)} custom-call(bf16[2,256,2432]{2,1,0:T(8,128)(2,1)} %x_ref.7, f32[1,2,3,2432]{3,2,1,0:T(4,128)} %copy.14.mod_ref, f32[1,128]{1,0:T(1,128)} %broadcast_in_dim_tile.2.gain_ref, bf16[2432,3712]{1,0:T(8,128)(2,1)} %all-gather.2.cloned.1.call-done.w_ref), custom_call_target="tpu_custom_call" | custom-call | flops 4622123008 | bytes 21200896 | tf_op jit(solution)/shard_map/pallas_call | solution.py:76
  197.9 14.7 %shard_map.132.attn_ref = bf16[256,1280]{1,0:T(8,128)(2,1)} custom-call(bf16[256,3712]{1,0:T(8,128)(2,1)} %shard_map.130.refs_0_.refs_1_.refs_2_.refs_3_, bf16[256,3712]{1,0:T(8,128)(2,1)} %shard_map.130.refs_0_.refs_1_.refs_2_.refs_3_, bf16[256,3712]{1,0:T(8,128)(2,1)} %shard_map.130.refs_0_.refs_1_.refs_2_.refs_3_, ...), custom_call_target="tpu_custom_call" | custom-call | flops 5867307008 | bytes 5729792 | tf_op jit(solution)/shard_map/pallas_call | solution.py:154
  212.6 6.7 %shard_map.133 = bf16[256,2432]{1,0:T(8,128)(2,1)} custom-call(bf16[2,256,2432]{2,1,0:T(8,128)(2,1)} %x_ref.7, bf16[256,1280]{1,0:T(8,128)(2,1)} %shard_map.132.attn_ref, f32[1,2,3,2432]{3,2,1,0:T(4,128)} %copy.14.mod_ref, bf16[4,1216,608]{2,1,0:T(8,128)(2,1)} %get-tuple-element.8.w_ref), custom_call_target="tpu_custom_call" | custom-call | flops 1514143744 | bytes 9650176 | tf_op jit(solution)/shard_map/pallas_call | solution.py:206
  219.3 3.6 %collective-permute-start = (bf16[256,2432]{1,0:T(8,128)(2,1)}, bf16[256,2432]{1,0:T(8,128)(2,1)S(1)}, u32[]{:S(2)}, u32[]{:S(2)}) collective-permute-start(bf16[256,2432]{1,0:T(8,128)(2,1)} %shard_map.133), channel_id=1, source_target_pairs={{0,16},{1,17},{2,18},{3,19},{4,20},{5,21},{6,22},{7,23},{8,24},{9,... | collective-permute-start | bytes 3735560 | tf_op jit(solution)/shard_map/ppermute | solution.py:469
  222.9 13.3 %shard_map.134.refs_0_.refs_1_.refs_2_.refs_3_ = bf16[256,3712]{1,0:T(8,128)(2,1)} custom-call(bf16[2,256,2432]{2,1,0:T(8,128)(2,1)} %x_ref.7, f32[1,2,3,2432]{3,2,1,0:T(4,128)} %copy.14.mod_ref, f32[1,128]{1,0:T(1,128)} %broadcast_in_dim_tile.2.gain_ref, bf16[2432,3712]{1,0:T(8,128)(2,1)} %all-gather.2.cloned.1.call-done.w_ref), custom_call_target="tpu_custom_call" | custom-call | flops 4622123008 | bytes 21200896 | tf_op jit(solution)/shard_map/pallas_call | solution.py:76
  236.2 14.7 %shard_map.135.attn_ref = bf16[256,1280]{1,0:T(8,128)(2,1)} custom-call(bf16[256,3712]{1,0:T(8,128)(2,1)} %shard_map.134.refs_0_.refs_1_.refs_2_.refs_3_, bf16[256,3712]{1,0:T(8,128)(2,1)} %shard_map.134.refs_0_.refs_1_.refs_2_.refs_3_, bf16[256,3712]{1,0:T(8,128)(2,1)} %shard_map.134.refs_0_.refs_1_.refs_2_.refs_3_, ...), custom_call_target="tpu_custom_call" | custom-call | flops 5867307008 | bytes 5729792 | tf_op jit(solution)/shard_map/pallas_call | solution.py:154
  250.9 0.0 copy-start.15
  250.9 6.7 %shard_map.136 = bf16[256,2432]{1,0:T(8,128)(2,1)} custom-call(bf16[2,256,2432]{2,1,0:T(8,128)(2,1)} %x_ref.7, bf16[256,1280]{1,0:T(8,128)(2,1)} %shard_map.135.attn_ref, f32[1,2,3,2432]{3,2,1,0:T(4,128)} %copy.14.mod_ref, bf16[4,1216,608]{2,1,0:T(8,128)(2,1)} %get-tuple-element.8.w_ref), custom_call_target="tpu_custom_call" | custom-call | flops 1514143744 | bytes 9650176 | tf_op jit(solution)/shard_map/pallas_call | solution.py:206
  257.7 1.6 collective-permute-start.1
  259.3 0.5 divide_subtract_fusion
  259.8 0.0 collective-permute-done.x_ref
  259.8 1.1 copy-done.5
  260.9 13.3 %shard_map.137.refs_0_.refs_1_.refs_2_.refs_3_ = bf16[256,3712]{1,0:T(8,128)(2,1)} custom-call(bf16[256,2432]{1,0:T(8,128)(2,1)} %copy-done.5, f32[1,2,3,2432]{3,2,1,0:T(4,128)} %copy.14.mod_ref, f32[1,128]{1,0:T(1,128)} %broadcast_in_dim_tile.2.gain_ref, bf16[2432,3712]{1,0:T(8,128)(2,1)} %all-gather.2.cloned.1.call-done.w_ref), custom_call_target="tpu_custom_call" | custom-call | flops 4622123008 | bytes 21200896 | tf_op jit(solution)/shard_map/pallas_call | solution.py:76
  274.2 14.7 %shard_map.138.attn_ref = bf16[256,1280]{1,0:T(8,128)(2,1)} custom-call(bf16[256,3712]{1,0:T(8,128)(2,1)} %shard_map.137.refs_0_.refs_1_.refs_2_.refs_3_, bf16[256,3712]{1,0:T(8,128)(2,1)} %shard_map.137.refs_0_.refs_1_.refs_2_.refs_3_, bf16[256,3712]{1,0:T(8,128)(2,1)} %shard_map.137.refs_0_.refs_1_.refs_2_.refs_3_, ...), custom_call_target="tpu_custom_call" | custom-call | flops 5867307008 | bytes 5729792 | tf_op jit(solution)/shard_map/pallas_call | solution.py:154
  288.9 7.5 %shard_map.139 = f32[256,64]{1,0:T(8,128)} custom-call(bf16[256,2432]{1,0:T(8,128)(2,1)} %copy-done.5, bf16[256,1280]{1,0:T(8,128)(2,1)} %shard_map.138.attn_ref, f32[1,2,3,2432]{3,2,1,0:T(4,128)} %copy.14.mod_ref, bf16[4,1216,608]{2,1,0:T(8,128)(2,1)} %get-tuple-element.8.w_ref, f32[2,2,2432]{2,1,0:T(2,128)} %rest_0_.3, bf16[2432,64]{1,0:T(8,128)(2,1)} %copy.29.rest_1_), custom_call_target="tpu_custom_call" | custom-call | flops 1514143744 | bytes 9650176 | tf_op jit(solution)/shard_map/pallas_call | solution.py:206
  296.4 0.0 collective-permute-done.1.x_ref
  296.4 1.1 copy-done.4
  297.4 13.3 %shard_map.140.refs_0_.refs_1_.refs_2_.refs_3_ = bf16[256,3712]{1,0:T(8,128)(2,1)} custom-call(bf16[256,2432]{1,0:T(8,128)(2,1)} %copy-done.4, f32[1,2,3,2432]{3,2,1,0:T(4,128)} %copy.14.mod_ref, f32[1,128]{1,0:T(1,128)} %broadcast_in_dim_tile.2.gain_ref, bf16[2432,3712]{1,0:T(8,128)(2,1)} %all-gather.2.cloned.1.call-done.w_ref), custom_call_target="tpu_custom_call" | custom-call | flops 4622123008 | bytes 21200896 | tf_op jit(solution)/shard_map/pallas_call | solution.py:76
  310.8 14.9 %shard_map.141.attn_ref = bf16[256,1280]{1,0:T(8,128)(2,1)} custom-call(bf16[256,3712]{1,0:T(8,128)(2,1)} %shard_map.140.refs_0_.refs_1_.refs_2_.refs_3_, bf16[256,3712]{1,0:T(8,128)(2,1)} %shard_map.140.refs_0_.refs_1_.refs_2_.refs_3_, bf16[256,3712]{1,0:T(8,128)(2,1)} %shard_map.140.refs_0_.refs_1_.refs_2_.refs_3_, ...), custom_call_target="tpu_custom_call" | custom-call | flops 5867307008 | bytes 5729792 | tf_op jit(solution)/shard_map/pallas_call | solution.py:154
  325.7 0.0 copy-start.1
  325.7 0.1 fusion.1
  325.8 0.0 copy-done.3
  325.8 1.4 copy-done.1
  327.2 0.2 fusion
  327.4 7.5 %shard_map.142 = f32[256,64]{1,0:T(8,128)} custom-call(bf16[256,2432]{1,0:T(8,128)(2,1)} %copy-done.4, bf16[256,1280]{1,0:T(8,128)(2,1)} %shard_map.141.attn_ref, f32[1,2,3,2432]{3,2,1,0:T(4,128)} %copy.14.mod_ref, bf16[4,1216,608]{2,1,0:T(8,128)(2,1)} %get-tuple-element.8.w_ref, f32[2,2,2432]{2,1,0:T(2,128)} %rest_0_.3, bf16[2432,64]{1,0:T(8,128)(2,1)} %copy.29.rest_1_), custom_call_target="tpu_custom_call" | custom-call | flops 1514143744 | bytes 9650176 | tf_op jit(solution)/shard_map/pallas_call | solution.py:206
  334.9 0.9 fusion.3
  335.8 0.0 copy-start.12
  335.8 1.4 collective-permute-start.2
  337.3 1.7 maximum_bitcast_fusion
  338.9 3.2 collective-permute-done.2
  342.1 0.1 multiply_subtract_fusion
  342.2 0.7 copy.38
  342.9 0.7 copy.39
  (26 shorter events, 0.1 us)
Async XLA Ops:
  7.2 177.4 %all-gather.2.cloned.1.call-start = ((), (), s32[]{:S(2)}) async-start(), calls=%async_computation | async-start | bytes 19183616 | tf_op jit(solution)/shard_map/all_gather | solution.py:455
  8.9 1.9 copy-start.11
  8.9 2.6 copy-start.14
  8.9 3.2 copy-start.6
  11.5 1.9 copy-start.9
  12.1 2.4 copy-start.10
  219.3 40.5 %collective-permute-start = (bf16[256,2432]{1,0:T(8,128)(2,1)}, bf16[256,2432]{1,0:T(8,128)(2,1)S(1)}, u32[]{:S(2)}, u32[]{:S(2)}) collective-permute-start(bf16[256,2432]{1,0:T(8,128)(2,1)} %shard_map.133), channel_id=1, source_target_pairs={{0,16},{1,17},{2,18},{3,19},{4,20},{5,21},{6,22},{7,23},{8,24},{9,... | collective-permute-start | bytes 3735560 | tf_op jit(solution)/shard_map/ppermute | solution.py:469
  250.9 8.3 %copy-start.15 = (s32[2]{0:T(128)S(1)}, s32[2]{0:T(128)}, u32[]{:S(2)}) copy-start(s32[2]{0:T(128)} %param.21) | copy-start | bytes 28
  257.7 38.7 %collective-permute-start.1 = (bf16[256,2432]{1,0:T(8,128)(2,1)}, bf16[256,2432]{1,0:T(8,128)(2,1)S(1)}, u32[]{:S(2)}, u32[]{:S(2)}) collective-permute-start(bf16[256,2432]{1,0:T(8,128)(2,1)} %shard_map.136), channel_id=1, source_target_pairs={{0,16},{1,17},{2,18},{3,19},{4,20},{5,21},{6,22},{7,23},{8,24},{9,... | collective-permute-start | bytes 3735560 | tf_op jit(solution)/shard_map/ppermute | solution.py:469
  259.8 1.1 copy-start.5
  296.4 1.1 copy-start.4
  310.8 14.9 %copy-start = (bf16[256,3712]{1,0:T(8,128)(2,1)S(1)}, bf16[256,3712]{1,0:T(8,128)(2,1)}, u32[]{:S(2)}) copy-start(bf16[256,3712]{1,0:T(8,128)(2,1)} %shard_map.130.refs_0_.refs_1_.refs_2_.refs_3_) | copy-start | bytes 5701636
  310.8 14.9 %copy-start.2 = (bf16[256,3712]{1,0:T(8,128)(2,1)S(1)}, bf16[256,3712]{1,0:T(8,128)(2,1)}, u32[]{:S(2)}) copy-start(bf16[256,3712]{1,0:T(8,128)(2,1)} %shard_map.137.refs_0_.refs_1_.refs_2_.refs_3_) | copy-start | bytes 5701636
  310.8 15.1 %copy-start.3 = (bf16[256,3712]{1,0:T(8,128)(2,1)S(1)}, bf16[256,3712]{1,0:T(8,128)(2,1)}, u32[]{:S(2)}) copy-start(bf16[256,3712]{1,0:T(8,128)(2,1)} %shard_map.140.refs_0_.refs_1_.refs_2_.refs_3_) | copy-start | bytes 5701636
  325.7 1.5 copy-start.1
  327.4 7.5 %copy-start.7 = (f32[256,64]{1,0:T(8,128)S(1)}, f32[256,64]{1,0:T(8,128)}, u32[]{:S(2)}) copy-start(f32[256,64]{1,0:T(8,128)} %shard_map.139) | copy-start | bytes 196612
  335.8 6.3 %copy-start.8 = (f32[256,64]{1,0:T(8,128)S(1)}, f32[256,64]{1,0:T(8,128)}, u32[]{:S(2)}) copy-start(f32[256,64]{1,0:T(8,128)} %shard_map.142) | copy-start | bytes 196612
  335.8 6.3 %copy-start.12 = (f32[2]{0:T(128)S(1)}, f32[2]{0:T(128)}, u32[]{:S(2)}) copy-start(f32[2]{0:T(128)} %get-tuple-element.14) | copy-start | bytes 28
  335.8 6.3 %copy-start.13 = (f32[2]{0:T(128)S(1)}, f32[2]{0:T(128)}, u32[]{:S(2)}) copy-start(f32[2]{0:T(128)} %get-tuple-element.15) | copy-start | bytes 28
  335.8 6.3 %collective-permute-start.2 = (bf16[2,128,64]{2,1,0:T(8,128)(2,1)S(1)}, bf16[2,128,64]{2,1,0:T(8,128)(2,1)S(1)}, u32[]{:S(2)}, u32[]{:S(2)}) collective-permute-start(bf16[2,128,64]{2,1,0:T(8,128)(2,1)S(1)} %fusion.3), channel_id=1, source_target_pairs={{16,0},{17,1},{18,2},{19,3},{20,4},{21,5},{22,6},{23,7},{24,8},{25... | collective-permute-start | bytes 98312 | tf_op jit(solution)/shard_map/ppermute | solution.py:486
Sparse Core Ops, SparseCore 0:
  10.9 173.5 all-gather.1
